TPU v7x, 32 devices: a whole 2x2x4 slice. The times are simulated.
32 devices in a mesh: pool: 2 (over y), ctx: 4 (over z), mp: 4 (over x, core).
Axes of the slice: x: 2, y: 2, z: 4, core: 2. Of those that a mesh axis runs over, the one named last changes fastest.
Arguments:
- tokens: bfloat16 [2, 2048, 4096], P('pool', 'ctx', 'mp'), may hold values from -2.5 to 2.5
- norm_gain: float32 [4096], replicated, may hold values from 0.5 to 1.5
- cross_gain: float32 [4096], replicated, may hold values from 0.1 to 1.9
- w_query: bfloat16 [4096, 4096], P(None, 'mp'), may hold values from -8 to 8
- w_key: bfloat16 [4096, 4096], P(None, 'mp'), may hold values from -0.09375 to 0.09375
- w_value: bfloat16 [4096, 4096], P(None, 'mp'), may hold values from -0.09375 to 0.09375
- w_out: bfloat16 [4096, 4096], P('mp'), may hold values from -0.125 to 0.125
- w_cross_query: bfloat16 [4096, 4096], P(None, 'mp'), may hold values from -8 to 8
- w_cross_kv: bfloat16 [2, 896, 4096], P(None, None, 'mp'), may hold values from -0.1875 to 0.1875
- w_cross_out: bfloat16 [4096, 4096], P('mp'), may hold values from -0.125 to 0.125
- encoded: bfloat16 [512, 128, 896], P(('pool', 'ctx'), 'mp'), may hold values from -6 to 6
- owners: int32 [2, 32, 2], replicated, may hold values from 0 to 7, all different within a row; in each aligned block of 8 rows (0 to 7, 8 to 15, ..., all dimensions but the last counted through in order) at most 4 rows name the same one
- slots: int32 [2, 32, 2], replicated, may hold values from 0 to 63
Outputs:
- layer_out: bfloat16 [2, 2048, 4096], P('pool', 'ctx', 'mp')
Inputs may be any that keep to these rules, and one draw needn't show every extreme that they name: The 2 neighbours of a span have different owners; among the spans of one index of pool and ctx (aligned blocks of 8 spans, sequence by sequence) no owner is named more than 4 times.
All inputs are finite; a program needn't handle non-finite values.
Results may differ from a plain program's by a relative error of at most 0.035.
Values may be sent and summed in bfloat16 or wider, within the bound.
A program may use at most 192 MiB of HBM per device.

v0:
```python
import jax
import jax.numpy as jnp
from jax import lax
from jax.sharding import PartitionSpec as P

HEAD = 128
SPAN = 64
NB_TOK = 128
NB_PER = 2


norm_eps = 1e-05
mask_floor = -1e30


def from_behind(block, axis, distance):
    devices = range(lax.axis_size(axis))
    route = [(i - distance, i) for i in devices if i - distance in devices]
    return lax.ppermute(block, axis, route)


def fetch_neighbours(encoded, owners, slots, w_cross_kv):
    group_count = lax.axis_size(("pool", "ctx"))
    my_group = lax.axis_index(("pool", "ctx"))
    per_group = owners.size // group_count
    capacity = max(2, 2 * per_group // group_count)
    owner_table = owners.reshape(group_count, per_group)
    slot_table = slots.reshape(group_count, per_group)
    matched = (owner_table == my_group).astype(jnp.int32)
    order_rank = jnp.cumsum(matched, axis=1) - 1
    slot_index = jnp.arange(capacity, dtype=jnp.int32)
    picked = matched[:, None, :] * (order_rank[:, None, :] == slot_index[None, :, None]).astype(
        jnp.int32
    )
    source_rows = jnp.sum(picked * slot_table[:, None, :], axis=2).reshape(-1)
    filled = jnp.sum(picked, axis=2).reshape(-1)
    outgoing = jnp.where(
        filled[:, None, None] > 0, encoded[source_rows], jnp.zeros((), encoded.dtype)
    )
    outgoing = outgoing.reshape((group_count, capacity) + encoded.shape[1:])
    incoming = lax.all_to_all(outgoing, ("pool", "ctx"), split_axis=0, concat_axis=0, tiled=True)
    wanted = lax.dynamic_index_in_dim(owner_table, my_group, 0, keepdims=False)
    positions = jnp.arange(per_group, dtype=jnp.int32)
    same_owner = (wanted[:, None] == wanted[None, :]).astype(jnp.int32)
    before_this = (positions[None, :] < positions[:, None]).astype(jnp.int32)
    arrival = wanted * capacity + jnp.sum(same_owner * before_this, axis=1)
    arrived = incoming.reshape((group_count * capacity,) + encoded.shape[1:])[arrival]
    return jnp.einsum(
        "nrw,cwd->cnrd",
        lax.all_gather(arrived, "mp", axis=1, tiled=True),
        w_cross_kv,
        preferred_element_type=jnp.float32,
    ).astype(jnp.bfloat16)


def self_attention(queries, key_rows, value_rows, first_row):
    tok_rows, head_count, head_dim = queries.shape
    score_scale = head_dim ** (-0.5)
    query_pos = first_row + jnp.arange(tok_rows, dtype=jnp.int32)
    last_row = first_row + tok_rows - 1
    start_state = (
        jnp.full((head_count, tok_rows), mask_floor, jnp.float32),
        jnp.zeros((head_count, tok_rows), jnp.float32),
        jnp.zeros((head_count, tok_rows, head_dim), jnp.float32),
    )
    pieces = (
        lax.all_gather(key_rows, "ctx", axis=0, tiled=True),
        lax.all_gather(value_rows, "ctx", axis=0, tiled=True),
    )

    def update(state):
        running_max, running_sum, running_out = state
        keys_here, values_here = pieces
        key_pos = jnp.arange(keys_here.shape[0], dtype=jnp.int32)
        allowed = (key_pos[None, :] <= query_pos[:, None])[None]
        scores = (
            jnp.einsum("qhe,khe->hqk", queries, keys_here, preferred_element_type=jnp.float32)
            * score_scale
        )
        scores = jnp.where(allowed, scores, mask_floor)
        new_max = jnp.maximum(running_max, jnp.max(scores, axis=-1))
        weights = jnp.where(allowed, jnp.exp(scores - new_max[..., None]), 0.0)
        running_sum = jnp.sum(weights, axis=-1)
        running_out = jnp.einsum(
            "hqk,khe->hqe",
            weights.astype(jnp.bfloat16),
            values_here,
            preferred_element_type=jnp.float32,
        )
        return (new_max, running_sum, running_out)

    running_max, running_sum, running_out = lax.cond(
        jnp.int32(0) <= last_row, update, lambda state: state, start_state
    )
    attended = (running_out / running_sum[..., None]).astype(jnp.bfloat16)
    return jnp.transpose(attended, (1, 0, 2)).reshape(tok_rows, head_count * head_dim)


def cross_attention(queries, neighbour_kv):
    tok_rows, head_count, head_dim = queries.shape
    score_scale = head_dim ** (-0.5)
    span_count = neighbour_kv.shape[1] // NB_PER
    grouped = neighbour_kv.reshape(2, span_count, NB_PER * NB_TOK, head_count, head_dim)
    earlier = from_behind(grouped[:, -1:], "ctx", 1)
    extended = jnp.concatenate([earlier, grouped], axis=1)
    padded = jnp.concatenate(
        [
            jnp.zeros((1, head_count, head_dim), jnp.bfloat16),
            queries,
            jnp.zeros((SPAN - 1, head_count, head_dim), jnp.bfloat16),
        ],
        axis=0,
    )
    padded = padded.reshape(span_count + 1, SPAN, head_count, head_dim)
    scores = (
        jnp.einsum("cmhe,cnhe->chmn", padded, extended[0], preferred_element_type=jnp.float32)
        * score_scale
    )
    peak = jnp.max(scores, axis=-1, keepdims=True)
    weights = jnp.exp(scores - peak)
    totals = jnp.sum(weights, axis=-1)
    mixed_out = jnp.einsum(
        "chmn,cnhe->cmhe",
        weights.astype(jnp.bfloat16),
        extended[1],
        preferred_element_type=jnp.float32,
    )
    mixed_out = (mixed_out / jnp.transpose(totals, (0, 2, 1))[..., None]).astype(jnp.bfloat16)
    mixed_out = mixed_out.reshape((span_count + 1) * SPAN, head_count * head_dim)
    return mixed_out[1 : tok_rows + 1]


def per_device(
    tokens,
    norm_gain,
    cross_gain,
    w_query,
    w_key,
    w_value,
    w_out,
    w_cross_query,
    w_cross_kv,
    w_cross_out,
    encoded,
    owners,
    slots,
):
    tok_rows = tokens.shape[1]
    head_count = w_query.shape[1] // HEAD
    whole_rows = lax.all_gather(tokens[0], "mp", axis=1, tiled=True)
    whole_float = whole_rows.astype(jnp.float32)
    normed = (
        whole_float
        * lax.rsqrt(jnp.mean(whole_float * whole_float, axis=-1, keepdims=True) + norm_eps)
        * norm_gain
    ).astype(jnp.bfloat16)
    queries = (
        jnp.dot(normed, w_query, preferred_element_type=jnp.float32)
        .astype(jnp.bfloat16)
        .reshape(tok_rows, head_count, HEAD)
    )
    key_rows = (
        jnp.dot(normed, w_key, preferred_element_type=jnp.float32)
        .astype(jnp.bfloat16)
        .reshape(tok_rows, head_count, HEAD)
    )
    value_rows = (
        jnp.dot(normed, w_value, preferred_element_type=jnp.float32)
        .astype(jnp.bfloat16)
        .reshape(tok_rows, head_count, HEAD)
    )
    attended = self_attention(queries, key_rows, value_rows, lax.axis_index("ctx") * tok_rows)
    branch_terms = jnp.dot(attended, w_out, preferred_element_type=jnp.float32)
    share = lax.psum_scatter(
        branch_terms.astype(jnp.bfloat16), "mp", scatter_dimension=1, tiled=True
    ).astype(jnp.float32)
    residual_part = (tokens[0].astype(jnp.float32) + share).astype(jnp.bfloat16)
    mixed_rows = lax.all_gather(residual_part, "mp", axis=1, tiled=True)
    mixed_float = mixed_rows.astype(jnp.float32)
    cross_in = (
        mixed_float
        * lax.rsqrt(jnp.mean(mixed_float * mixed_float, axis=-1, keepdims=True) + norm_eps)
        * cross_gain
    ).astype(jnp.bfloat16)
    cross_queries = (
        jnp.dot(cross_in, w_cross_query, preferred_element_type=jnp.float32)
        .astype(jnp.bfloat16)
        .reshape(tok_rows, head_count, HEAD)
    )
    neighbour_kv = fetch_neighbours(encoded, owners, slots, w_cross_kv)
    crossed = cross_attention(cross_queries, neighbour_kv)
    cross_terms = jnp.dot(crossed, w_cross_out, preferred_element_type=jnp.float32)
    cross_part = lax.psum_scatter(
        cross_terms.astype(jnp.bfloat16), "mp", scatter_dimension=1, tiled=True
    ).astype(jnp.float32)
    return (residual_part.astype(jnp.float32) + cross_part).astype(jnp.bfloat16)[None]


def solution(mesh):
    placed = (
        P("pool", "ctx", "mp"),
        P(),
        P(),
        P(None, "mp"),
        P(None, "mp"),
        P(None, "mp"),
        P("mp", None),
        P(None, "mp"),
        P(None, None, "mp"),
        P("mp", None),
        P(("pool", "ctx"), "mp", None),
        P(),
        P(),
    )
    return jax.shard_map(
        per_device, mesh=mesh, in_specs=placed, out_specs=P("pool", "ctx", "mp"), check_vma=False
    )
```

profile of v0, /device:TPU:12, one launch (start us, length us, event | category | flops | bytes accessed | tf_op | source)
XLA Modules:
  0.0 516.3 jit_solution(17144848033120393766)
XLA Ops:
  6.5 0.7 all-gather.14.cloned.1.call-update
  7.3 0.0 all-gather.8.cloned.1.call-start
  7.3 37.2 %all-gather.14.cloned.1.call-done = bf16[1,512,4096]{2,1,0:T(8,128)(2,1)} async-done(((bf16[1,512,1024]{2,1,0:T(8,128)(2,1)}), bf16[1,512,4096]{2,1,0:T(8,128)(2,1)}) %all-gather.14.cloned.1.call-update) | async-done | bytes 4194320 | tf_op jit(solution)/shard_map/all_gather | solution.py:150
  44.5 3.1 fusion.15
  47.6 9.2 %fusion.36 = bf16[64,8,8,128]{3,2,1,0:T(8,128)(2,1)S(1)} fusion(bf16[4096,1024]{1,0:T(8,128)(2,1)} %param.19, bf16[1,512,4096]{2,1,0:T(8,128)(2,1)} %all-gather.14.cloned.1.call-done, f32[4096]{0:T(1024)S(1)} %copy-done.4, f32[512]{0:T(512)S(1)} %add_rsqrt_fusion.1), kind=kOutput, calls=%fused_computation.57 | convolution fusion | flops 4303880192 | bytes 13649920 | tf_op jit(solution)/shard_map/dot_general | solution.py:163
  56.8 1.2 copy.69
  58.0 0.0 all-gather.8.cloned.1.call-update
  58.0 0.0 all-gather.10.cloned.1.call-start
  58.1 9.2 %fusion.37 = bf16[64,8,8,128]{3,2,1,0:T(8,128)(2,1)S(1)} fusion(bf16[4096,1024]{1,0:T(8,128)(2,1)} %param.20, bf16[1,512,4096]{2,1,0:T(8,128)(2,1)} %all-gather.14.cloned.1.call-done, f32[4096]{0:T(1024)S(1)} %copy-done.4, f32[512]{0:T(512)S(1)} %add_rsqrt_fusion.1), kind=kOutput, calls=%fused_computation.58 | convolution fusion | flops 4303880192 | bytes 13649920 | tf_op jit(solution)/shard_map/dot_general | solution.py:168
  67.3 1.2 copy.68
  68.4 0.0 all-gather.10.cloned.1.call-update
  68.5 0.3 reduce-scatter.3.cloned.1.call-start
  68.7 9.2 %convolution_convert_fusion.4 = bf16[512,1024]{1,0:T(8,128)(2,1)S(1)} fusion(bf16[4096,1024]{1,0:T(8,128)(2,1)} %param.18, bf16[1,512,4096]{2,1,0:T(8,128)(2,1)} %all-gather.14.cloned.1.call-done, f32[4096]{0:T(1024)S(1)} %copy-done.4, f32[512]{0:T(512)S(1)} %add_rsqrt_fusion.1), kind=kOutput, calls=%fused_computation.56 | convolution fusion | flops 4303880192 | bytes 13649920 | tf_op jit(solution)/shard_map/dot_general | solution.py:158
  77.9 58.6 %all-gather.8.cloned.1.call-done = bf16[2048,8,128]{2,0,1:T(8,128)(2,1)} async-done(((bf16[512,8,128]{2,0,1:T(8,128)(2,1)}), bf16[2048,8,128]{2,0,1:T(8,128)(2,1)}) %all-gather.8.cloned.1.call-update) | async-done | bytes 4194320 | tf_op jit(solution)/shard_map/all_gather | solution.py:67
  136.5 80.9 %all-gather.10.cloned.1.call-done = bf16[2048,8,128]{2,0,1:T(8,128)(2,1)} async-done(((bf16[512,8,128]{2,0,1:T(8,128)(2,1)}), bf16[2048,8,128]{2,0,1:T(8,128)(2,1)}) %all-gather.10.cloned.1.call-update) | async-done | bytes 4194320 | tf_op jit(solution)/shard_map/all_gather | solution.py:68
  217.4 49.2 %conditional.1 = (f32[8,512]{1,0:T(8,128)S(1)}, f32[8,512,128]{1,2,0:T(8,128)S(1)}) conditional(s32[]{:T(128)} %convert_element_type.86, () %tuple.13, (s32[]{:T(128)}, s32[512]{0:T(512)S(1)}, bf16[512,1024]{1,0:T(8,128)(2,1)S(1)}, bf16[2048,8,128]{2,0,1:T(8,128)(2,1)}, bf16[2048,8,128]{2,0,1:T(8,128)(2,1)}) %tuple.14), branch_computations={%region_1.0_spmd, %region_2.5_spmd} | conditional | flops 4405064192 | bytes 116496400 | solution.py:92
  217.4 0.7 iota_compare_fusion
  218.1 16.2 %fusion = (f32[8,512]{1,0:T(8,128)S(1)}, f32[8,512,2048]{2,1,0:T(8,128)}) fusion(pred[512,2048]{1,0:T(8,128)(4,1)S(1)} %iota_compare_fusion, bf16[2048,8,128]{2,0,1:T(8,128)(2,1)} %get-tuple-element.21, bf16[512,1024]{1,0:T(8,128)(2,1)S(1)} %get-tuple-element.20), kind=kOutput, calls=%fused_computation.4 | convolution fusion | flops 2172645376 | bytes 39862272 | tf_op jit(solution)/shard_map/cond/branch_1_fun/qhe,khe->hqk/dot_general | solution.py:77
  234.3 16.7 %fusion.3 = f32[8,512,128]{1,2,0:T(8,128)S(1)} fusion(bf16[2048,8,128]{2,0,1:T(8,128)(2,1)} %get-tuple-element.22, f32[8,512,2048]{2,1,0:T(8,128)} %get-tuple-element.31, f32[8,512]{1,0:T(8,128)S(1)} %broadcast_maximum_fusion, pred[512,2048]{1,0:T(8,128)(4,1)S(1)} %iota_compare_fusion), kind=kOutput, calls=%fused_computation.7 | convolution fusion | flops 2189426688 | bytes 40910848 | tf_op jit(solution)/shard_map/cond | solution.py:92
  251.1 15.6 %fusion.2 = f32[8,512]{1,0:T(8,128)S(1)} fusion(f32[8,512,2048]{2,1,0:T(8,128)} %get-tuple-element.31, f32[8,512]{1,0:T(8,128)S(1)} %broadcast_maximum_fusion, pred[512,2048]{1,0:T(8,128)(4,1)S(1)} %iota_compare_fusion), kind=kLoop, calls=%fused_computation.6 | loop fusion | flops 41938944 | bytes 34635776 | tf_op jit(solution)/shard_map/cond/branch_1_fun/reduce_sum | solution.py:83
  266.7 0.3 divide_convert_fusion
  267.0 9.5 %convolution_convert_fusion.1 = bf16[512,4096]{1,0:T(8,128)(2,1)} fusion(bf16[512,1024]{0,1:T(8,128)(2,1)S(1)} %bitcast.110, bf16[1024,4096]{1,0:T(8,128)(2,1)} %param.21), kind=kOutput, calls=%fused_computation.30 | convolution fusion | flops 4297064448 | bytes 13631488 | tf_op jit(solution)/shard_map/dot_general | solution.py:173
  276.5 0.1 copy.34
  276.6 0.1 reshape.166
  276.7 0.2 reduce_window_sum.11
  276.9 0.1 copy.36
  277.0 0.1 mul.96
  277.1 0.2 select_reduce_fusion
  277.3 0.1 copy.35
  277.4 0.1 copy.37
  277.5 0.1 reshape.167
  277.6 2.9 gather_fusion
  280.5 1.5 broadcast_select_fusion
  282.0 6.6 %all-to-all-start = ((bf16[8,4,32,896]{3,2,1,0:T(8,128)(2,1)}), bf16[8,4,32,896]{3,2,1,0:T(8,128)(2,1)S(1)}, u32[]{:S(2)}, u32[]{:S(2)}) async-start(bf16[8,4,32,896]{3,2,1,0:T(8,128)(2,1)} %broadcast_select_fusion), calls=%async_computation.1 | async-start | bytes 3670016 | tf_op jit(solution)/shard_map/all_to_all | solution.py:41
  288.6 0.2 select_reduce_fusion.1
  288.8 39.5 %all-to-all-done = bf16[8,4,32,896]{3,2,1,0:T(8,128)(2,1)S(1)} async-done(((bf16[8,4,32,896]{3,2,1,0:T(8,128)(2,1)}), bf16[8,4,32,896]{3,2,1,0:T(8,128)(2,1)S(1)}, u32[]{:S(2)}, u32[]{:S(2)}) %all-to-all-start) | async-done | bytes 1835040 | tf_op jit(solution)/shard_map/all_to_all | solution.py:41
  328.2 1.6 gather_fusion.1
  329.8 0.0 all-gather.12.cloned.1.call-start
  329.9 0.0 reduce-scatter.3.cloned.1.call-done
  329.9 2.6 fusion.32
  332.5 0.0 reduce-scatter.5.cloned.1.call-start
  332.6 29.8 %all-gather.16.cloned.1.call-done = bf16[16,128,896]{2,1,0:T(8,128)(2,1)} async-done(((bf16[16,32,896]{2,1,0:T(8,128)(2,1)}), bf16[16,128,896]{2,1,0:T(8,128)(2,1)}) %all-gather.16.cloned.1.call-update) | async-done | bytes 3670032 | tf_op jit(solution)/shard_map/all_gather | solution.py:50
  362.3 14.1 %convert_bitcast_fusion = bf16[2,16,128,1024]{3,2,0,1:T(8,128)(2,1)} fusion(bf16[16,128,896]{2,1,0:T(8,128)(2,1)} %all-gather.16.cloned.1.call-done, bf16[2,896,1024]{2,1,0:T(8,128)(2,1)} %param.23), kind=kOutput, calls=%fused_computation.28 | convolution fusion | flops 7520387072 | bytes 15728640 | tf_op jit(solution)/shard_map/nrw,cwd->cnrd/dot_general | solution.py:48
  376.5 8.3 %copy.38 = bf16[2,16,128,1024]{3,2,1,0:T(8,128)(2,1)} copy(bf16[2,16,128,1024]{3,2,0,1:T(8,128)(2,1)} %convert_bitcast_fusion) | data formatting | bytes 16777216 | tf_op jit(solution)/shard_map/convert_element_type | solution.py:53
  384.8 8.9 %copy.50 = bf16[512,8,8,128]{3,2,1,0:T(8,128)(2,1)} copy(bf16[512,8,8,128]{3,1,2,0:T(8,128)(2,1)} %bitcast.99) | data formatting | bytes 16777216
  393.7 1.3 slice.20
  395.0 0.2 copy.62
  395.2 3.6 collective-permute-start
  398.7 0.1 pad.2.clone
  398.8 23.6 %collective-permute-done = bf16[2,1,256,8,128]{4,2,3,1,0:T(8,128)(2,1)S(1)} collective-permute-done((bf16[2,1,256,8,128]{4,2,3,1,0:T(8,128)(2,1)S(1)}, bf16[2,1,256,8,128]{4,2,3,1,0:T(8,128)(2,1)S(1)}, u32[]{:S(2)}, u32[]{:S(2)}) %collective-permute-start) | collective-permute-done | bytes 1048608 | tf_op jit(solution)/shard_map/ppermute | solution.py:19
  422.4 1.2 constant_dynamic-update-slice_fusion.1
  423.6 9.2 %constant_dynamic-update-slice_fusion = bf16[2,9,256,8,128]{4,2,3,1,0:T(8,128)(2,1)} fusion(bf16[2,9,256,8,128]{4,2,3,1,0:T(8,128)(2,1)} %constant_dynamic-update-slice_fusion.1, bf16[2,8,256,8,128]{4,3,2,1,0:T(8,128)(2,1)} %bitcast.98), kind=kLoop, calls=%fused_computation.75 | loop fusion | bytes 16777216 | tf_op jit(solution)/shard_map/concatenate | solution.py:105
  432.8 3.2 fusion.12
  436.0 9.3 %fusion.38 = bf16[64,8,8,128]{3,1,2,0:T(8,128)(2,1)S(1)} fusion(bf16[4096,1024]{1,0:T(8,128)(2,1)} %param.22, bf16[512,4096]{1,0:T(8,128)(2,1)} %all-gather.12.cloned.1.call-done, f32[4096]{0:T(1024)S(1)} %copy-done.5, f32[512]{0:T(512)S(1)} %add_rsqrt_fusion), kind=kOutput, calls=%fused_computation.59 | convolution fusion | flops 4303880192 | bytes 13649920 | tf_op jit(solution)/shard_map/dot_general | solution.py:186
  445.4 0.3 copy.49
  445.6 3.4 maximum_maximum_fusion
  449.1 1.8 multiply_reduce_fusion
  450.9 1.6 fusion.24
  452.5 2.1 fusion.29
  454.6 0.8 copy.42
  455.4 0.3 copy.67
  455.8 6.1 %convolution_convert_fusion = bf16[512,4096]{1,0:T(8,128)(2,1)} fusion(bf16[1024,4096]{1,0:T(8,128)(2,1)S(1)} %bitcast.113, bf16[576,1024]{1,0:T(8,128)(2,1)S(1)} %bitcast.109), kind=kOutput, calls=%fused_computation.29 | convolution fusion | flops 4297064448 | bytes 13631488 | tf_op jit(solution)/shard_map/dot_general | solution.py:192
  461.9 44.7 %reduce-scatter.5.cloned.1.call-done = bf16[512,1024]{1,0:T(8,128)(2,1)} async-done(((bf16[512,4096]{1,0:T(8,128)(2,1)}), bf16[512,1024]{1,0:T(8,128)(2,1)}) %reduce-scatter.5.cloned.1.call-update) | async-done | bytes 1048592 | tf_op jit(solution)/shard_map/reduce_scatter | solution.py:193
  506.6 2.6 fusion.42
  (46 shorter events, 0.2 us)
Async XLA Ops:
  6.5 41.1 %copy-start.4 = (f32[4096]{0:T(1024)S(1)}, f32[4096]{0:T(1024)}, u32[]{:S(2)}) copy-start(f32[4096]{0:T(1024)} %param.16) | copy-start | bytes 49156
  6.5 38.0 %all-gather.14.cloned.1.call-start = ((), (), s32[]{:S(2)}) async-start(), calls=%async_computation.8 | async-start | bytes 5242880 | tf_op jit(solution)/shard_map/all_gather | solution.py:150
  7.3 129.3 %all-gather.8.cloned.1.call-start = ((), (), s32[]{:S(2)}) async-start(), calls=%async_computation.3 | async-start | bytes 5242880 | tf_op jit(solution)/shard_map/all_gather | solution.py:67
  58.0 159.4 %all-gather.10.cloned.1.call-start = ((), (), s32[]{:S(2)}) async-start(), calls=%async_computation.4 | async-start | bytes 5242880 | tf_op jit(solution)/shard_map/all_gather | solution.py:68
  68.5 261.4 %reduce-scatter.3.cloned.1.call-start = ((), (), s32[]{:S(2)}) async-start(), calls=%async_computation.5 | async-start | bytes 5242880 | tf_op jit(solution)/shard_map/reduce_scatter | solution.py:174
  267.0 9.6 %copy-start.2 = (s32[2,32,2]{1,2,0:T(2,128)S(1)}, s32[2,32,2]{1,2,0:T(2,128)}, u32[]{:S(2)}) copy-start(s32[2,32,2]{1,2,0:T(2,128)} %param.26) | copy-start | bytes 1540
  267.0 9.9 %copy-start.3 = (s32[2,32,2]{1,2,0:T(2,128)S(1)}, s32[2,32,2]{1,2,0:T(2,128)}, u32[]{:S(2)}) copy-start(s32[2,32,2]{1,2,0:T(2,128)} %param.27) | copy-start | bytes 1540
  280.5 49.4 %copy-start.1 = (bf16[1,512,1024]{2,1,0:T(8,128)(2,1)S(1)}, bf16[1,512,1024]{2,1,0:T(8,128)(2,1)}, u32[]{:S(2)}) copy-start(bf16[1,512,1024]{2,1,0:T(8,128)(2,1)} %param.15) | copy-start | bytes 3145732
  282.0 46.3 %all-to-all-start = ((bf16[8,4,32,896]{3,2,1,0:T(8,128)(2,1)}), bf16[8,4,32,896]{3,2,1,0:T(8,128)(2,1)S(1)}, u32[]{:S(2)}, u32[]{:S(2)}) async-start(bf16[8,4,32,896]{3,2,1,0:T(8,128)(2,1)} %broadcast_select_fusion), calls=%async_computation.1 | async-start | bytes 3670016 | tf_op jit(solution)/shard_map/all_to_all | solution.py:41
  288.6 73.8 %all-gather.16.cloned.1.call-start = ((), (), s32[]{:S(2)}) async-start(), calls=%async_computation.9 | async-start | bytes 4587520 | tf_op jit(solution)/shard_map/all_gather | solution.py:50
  329.8 102.9 %all-gather.12.cloned.1.call-start = ((), (), s32[]{:S(2)}) async-start(), calls=%async_computation.6 | async-start | bytes 5242880 | tf_op jit(solution)/shard_map/all_gather | solution.py:178
  332.5 174.0 %reduce-scatter.5.cloned.1.call-start = ((), (), s32[]{:S(2)}) async-start(), calls=%async_computation.7 | async-start | bytes 5242880 | tf_op jit(solution)/shard_map/reduce_scatter | solution.py:193
  395.2 27.2 %collective-permute-start = (bf16[2,1,256,8,128]{4,2,3,1,0:T(8,128)(2,1)S(1)}, bf16[2,1,256,8,128]{4,2,3,1,0:T(8,128)(2,1)S(1)}, u32[]{:S(2)}, u32[]{:S(2)}) collective-permute-start(bf16[2,1,256,8,128]{4,2,3,1,0:T(8,128)(2,1)S(1)} %copy.62), channel_id=1, source_target_pairs={{0,4},{4,8},{8,12},{1,5},{5,9},{9,13},{2,6},{6,10},{10,14},{3,7},{... | collective-permute-start | bytes 3145736 | tf_op jit(solution)/shard_map/ppermute | solution.py:19
  423.6 12.4 %copy-start.5 = (f32[4096]{0:T(1024)S(1)}, f32[4096]{0:T(1024)}, u32[]{:S(2)}) copy-start(f32[4096]{0:T(1024)} %param.17) | copy-start | bytes 49156
  432.8 16.2 %slice-start = ((s8[9437184]{0:T(1024)(128)(4,1)}), s8[4194304]{0:T(1024)(128)(4,1)S(1)}, s32[]{:S(2)}) async-start(s8[9437184]{0:T(1024)(128)(4,1)} %bitcast.107), calls=%async_computation.10 | async-start | bytes 8388608
  436.0 13.0 %slice-start.1 = ((s8[9437184]{0:T(1024)(128)(4,1)}), s8[4194304]{0:T(1024)(128)(4,1)S(1)}, s32[]{:S(2)}) async-start(s8[9437184]{0:T(1024)(128)(4,1)} %bitcast.107), calls=%async_computation.11 | async-start | bytes 8388608
  436.0 13.0 %slice-start.2 = ((s8[9437184]{0:T(1024)(128)(4,1)}), s8[1048576]{0:T(1024)(128)(4,1)S(1)}, s32[]{:S(2)}) async-start(s8[9437184]{0:T(1024)(128)(4,1)} %bitcast.107), calls=%async_computation.12 | async-start | bytes 2097152
  449.1 6.7 %slice-start.3 = ((s8[8388608]{0:T(1024)(128)(4,1)}), s8[4194304]{0:T(1024)(128)(4,1)S(1)}, s32[]{:S(2)}) async-start(s8[8388608]{0:T(1024)(128)(4,1)} %bitcast.112), calls=%async_computation.13 | async-start | bytes 8388608
  452.5 3.3 slice-start.4
  461.9 44.7 %copy-start = (bf16[512,1024]{1,0:T(8,128)(2,1)S(1)}, bf16[512,1024]{1,0:T(8,128)(2,1)}, u32[]{:S(2)}) copy-start(bf16[512,1024]{1,0:T(8,128)(2,1)} %fusion.32) | copy-start | bytes 3145732
Sparse Core Ops, SparseCore 0:
  8.9 35.5 all-gather.13
  58.2 78.3 all-gather.7
  138.1 79.2 all-gather.9
  276.6 45.4 reduce-scatter.2
  330.0 32.3 all-gather.15
  363.8 34.4 all-gather.11
  462.0 44.5 reduce-scatter.4
where the time goes:
time: 525 us; the launch traced here: 516 us
  waiting for transfers between devices  315 us (60%)
  matrix products  104 us (20%)
  local copies, waits for them, and re-layouts  38 us (7%)
  other arithmetic  35.1 us (7%)
  between operations  14 us (3%)
  starting transfers between devices  10.6 us (2%)
    all_gather x1, waiting for transfers between devices, self_attention(): lax.all_gather(value_rows, 'ctx', axis=0, tiled=True)  80.9 us
    all_gather x1, waiting for transfers between devices, self_attention(): lax.all_gather(key_rows, 'ctx', axis=0, tiled=True)  58.6 us
    reduce_scatter x1, waiting for transfers between devices, per_device(): lax.psum_scatter(cross_terms.astype(jnp.bfloat16), 'mp', scatter_dimensio...  44.7 us
    all_to_all x1, waiting for transfers between devices, fetch_neighbours(): lax.all_to_all(outgoing, ('pool', 'ctx'), split_axis=0, concat_axis=0, ti...  39.5 us
    all_gather x1, waiting for transfers between devices, per_device(): whole_rows = lax.all_gather(tokens[0], 'mp', axis=1, tiled=True)  37.2 us
    all_gather x1, waiting for transfers between devices, fetch_neighbours(): lax.all_gather(arrived, 'mp', axis=1, tiled=True)  29.8 us
    ppermute x1, waiting for transfers between devices, from_behind(): return lax.ppermute(block, axis, route)  23.6 us
    cond x1, matrix products, self_attention(): lax.cond(jnp.int32(0) <= last_row, update, lambda state: state, start_state)  16.7 us
  transfers between devices with their start and end apart: 9, of which 7 were waited for; matrix products, arithmetic and copies ran while one was open for 14% of the time, Pallas kernels for 0%

commit v1 on v0

v1 whole, which is shorter than its diff:
```python
import functools

import jax
import jax.numpy as jnp
from jax import lax
from jax.experimental import pallas as pl
from jax.experimental.pallas import tpu as pltpu
from jax.sharding import PartitionSpec as P

HEAD = 128
SPAN = 64
NB_TOK = 128
NB_PER = 2
MIB = 1 << 20
LOG2E = 1.4426950408889634

norm_eps = 1e-05


def params(mib, steps=1):
    return pltpu.CompilerParams(
        vmem_limit_bytes=mib * MIB, dimension_semantics=("arbitrary",) * steps
    )


def cost(flops, moved, exps=0):
    return pl.CostEstimate(flops=int(flops), bytes_accessed=int(moved), transcendentals=int(exps))


def from_behind(block, axis, distance):
    devices = range(lax.axis_size(axis))
    route = [(i - distance, i) for i in devices if i - distance in devices]
    return lax.ppermute(block, axis, route)


def swap(block, bit):
    return lax.ppermute(block, "mp", [(i, i ^ bit) for i in range(lax.axis_size("mp"))])


def gather_blocks(block):
    count = lax.axis_size("mp")
    blocks = {0: block}
    bit = count // 2
    while bit:
        blocks.update({o ^ bit: swap(b, bit) for o, b in list(blocks.items())})
        bit //= 2
    return [blocks[o] for o in range(count)]


def scatter_sum(partials):
    count = lax.axis_size("mp")
    held = dict(enumerate(partials))
    bit = 1
    while bit < count:
        summed = {}
        for o in sorted((o for o in held if not o & bit), reverse=True):
            total = held[o].astype(jnp.float32) + swap(held[o | bit], bit).astype(jnp.float32)
            summed[o] = total if 2 * bit == count else total.astype(jnp.bfloat16)
        held = summed
        bit *= 2
    return held[0]


def norm_kernel(place_ref, gain_ref, *refs):
    *blocks, out_ref = refs
    width = blocks[0].shape[1]
    features = width * len(blocks)
    squares = 0.0
    for b in blocks:
        x = b[...].astype(jnp.float32)
        squares += jnp.sum(x * x, axis=1, keepdims=True)
    scale = lax.rsqrt(squares / features + norm_eps)
    for o, b in enumerate(blocks):
        columns = pl.ds(pl.multiple_of(place_ref[o] * width, width), width)
        out_ref[:, columns] = (b[...].astype(jnp.float32) * scale * gain_ref[:, columns]).astype(
            jnp.bfloat16
        )


def normalised(blocks, gain):
    rows, width = blocks[0].shape
    features = width * len(blocks)
    tile = min(rows, 128)
    places = lax.axis_index("mp") ^ jnp.arange(len(blocks), dtype=jnp.int32)
    return pl.pallas_call(
        norm_kernel,
        grid_spec=pltpu.PrefetchScalarGridSpec(
            num_scalar_prefetch=1,
            grid=(rows // tile,),
            in_specs=[pl.BlockSpec((1, features), lambda i, p: (0, 0))]
            + [pl.BlockSpec((tile, width), lambda i, p: (i, 0))] * len(blocks),
            out_specs=pl.BlockSpec((tile, features), lambda i, p: (i, 0)),
        ),
        out_shape=jax.ShapeDtypeStruct((rows, features), jnp.bfloat16),
        compiler_params=params(24),
        cost_estimate=cost(6 * rows * features, 4 * rows * features),
        name="norm",
    )(places, gain.reshape(1, features), *blocks)


def project_kernel(flip, x_ref, w_ref, out_ref):
    product = jnp.dot(x_ref[...], w_ref[...], preferred_element_type=jnp.float32)
    if flip:
        product = jnp.transpose(product)
    out_ref[...] = product.astype(jnp.bfloat16)


def project(x, w, first, width, flip=False):
    rows, depth = x.shape
    tile = min(width, 256)
    base = first // tile
    if flip:
        out_spec, out_dims = pl.BlockSpec((tile, rows), lambda j: (j, 0)), (width, rows)
    else:
        out_spec, out_dims = pl.BlockSpec((rows, tile), lambda j: (0, j)), (rows, width)
    return pl.pallas_call(
        functools.partial(project_kernel, flip),
        grid=(width // tile,),
        in_specs=[
            pl.BlockSpec((rows, depth), lambda j: (0, 0)),
            pl.BlockSpec((depth, tile), lambda j: (0, base + j)),
        ],
        out_specs=out_spec,
        out_shape=jax.ShapeDtypeStruct(out_dims, jnp.bfloat16),
        compiler_params=params(24),
        cost_estimate=cost(2 * rows * depth * width, 2 * depth * (rows + width)),
        name="project",
    )(x, w)


def block_kernel(place_ref, x_ref, w_ref, out_ref):
    out_ref[...] = jnp.dot(
        x_ref[...], w_ref[...], preferred_element_type=jnp.float32
    ).astype(jnp.bfloat16)


def project_block(x, w, place, width):
    rows, depth = x.shape
    tile = min(width, 512)
    steps = width // tile
    return pl.pallas_call(
        block_kernel,
        grid_spec=pltpu.PrefetchScalarGridSpec(
            num_scalar_prefetch=1,
            grid=(steps,),
            in_specs=[
                pl.BlockSpec((rows, depth), lambda j, p: (0, 0)),
                pl.BlockSpec((depth, tile), lambda j, p: (0, p[0] * steps + j)),
            ],
            out_specs=pl.BlockSpec((rows, tile), lambda j, p: (0, j)),
        ),
        out_shape=jax.ShapeDtypeStruct((rows, width), jnp.bfloat16),
        compiler_params=params(16),
        cost_estimate=cost(2 * rows * depth * width, 2 * depth * (rows + width)),
        name="project_block",
    )(place.reshape(1), x, w)


def project_scattered(x, w):
    count = lax.axis_size("mp")
    width = w.shape[1] // count
    me = lax.axis_index("mp")
    partials = {}
    for o in sorted(range(count), key=lambda o: (1 - o % 2, -o)):
        partials[o] = project_block(x, w, me ^ o, width)
    return scatter_sum([partials[o] for o in range(count)])


def scores_of(keys, queries):
    return lax.dot_general(
        keys, queries, (((1,), (1,)), ((), ())), preferred_element_type=jnp.float32
    ) * (HEAD**-0.5 * LOG2E)


def attend(parts):
    peak = functools.reduce(jnp.maximum, [jnp.max(s, axis=0, keepdims=True) for s, _ in parts])
    total, out = 0.0, 0.0
    for s, values in parts:
        weights = jnp.exp2(s - peak)
        total += jnp.sum(weights, axis=0, keepdims=True)
        out += jnp.dot(values, weights.astype(jnp.bfloat16), preferred_element_type=jnp.float32)
    return out / total, peak + jnp.log2(total)


def far_kernel(flag_ref, qa, qb, k0, v0, k1, v1, oa, la, ob, lb):
    rows = qa.shape[0]
    tile = min(rows, 256)

    @pl.when(flag_ref[0] == 1)
    def _():
        for q, o, l in ((qa, oa, la), (qb, ob, lb)):
            for at in range(0, rows, tile):
                queries = q[at : at + tile, :]
                out, log = attend(
                    [(scores_of(k0[...], queries), v0[...]), (scores_of(k1[...], queries), v1[...])]
                )
                o[:, at : at + tile] = out.astype(jnp.bfloat16)
                l[0, :, at : at + tile] = log


def near_kernel(flag_ref, q, k0, v0, k1, v1, o, l):
    rows = q.shape[0]
    tile = min(rows, 256)

    def run(with_earlier):
        for at in range(0, rows, tile):
            queries = q[at : at + tile, :]
            end = at + tile
            own = scores_of(k1[:end, :], queries)
            key_pos = lax.broadcasted_iota(jnp.int32, own.shape, 0)
            query_pos = at + lax.broadcasted_iota(jnp.int32, own.shape, 1)
            own = jnp.where(key_pos <= query_pos, own, -1e30)
            parts = [(own, v1[:, :end])]
            if with_earlier:
                parts.append((scores_of(k0[...], queries), v0[...]))
            out, log = attend(parts)
            o[:, at:end] = out.astype(jnp.bfloat16)
            l[0, :, at:end] = log

    @pl.when(flag_ref[0] % 2 == 1)
    def _():
        run(True)

    @pl.when(flag_ref[0] % 2 == 0)
    def _():
        run(False)


def merge_kernel(flag_ref, o, l, far_o, far_l, out):
    @pl.when(flag_ref[0] >= 2)
    def _():
        peak = jnp.maximum(l[0], far_l[0])
        here, there = jnp.exp2(l[0] - peak), jnp.exp2(far_l[0] - peak)
        mixed = (o[...].astype(jnp.float32) * here + far_o[...].astype(jnp.float32) * there) / (
            here + there
        )
        out[...] = jnp.transpose(mixed).astype(jnp.bfloat16)

    @pl.when(flag_ref[0] < 2)
    def _():
        out[...] = jnp.transpose(o[...].astype(jnp.float32)).astype(jnp.bfloat16)


def head_call(kernel, name, flag, rows, heads, ins, outs, work):
    specs = {
        "rows": (pl.BlockSpec((rows, HEAD), lambda h, f: (0, h)), (rows, heads * HEAD), jnp.bfloat16),
        "flat": (pl.BlockSpec((HEAD, rows), lambda h, f: (h, 0)), (heads * HEAD, rows), jnp.bfloat16),
        "log": (pl.BlockSpec((1, 1, rows), lambda h, f: (h, 0, 0)), (heads, 1, rows), jnp.float32),
    }
    return pl.pallas_call(
        kernel,
        grid_spec=pltpu.PrefetchScalarGridSpec(
            num_scalar_prefetch=1,
            grid=(heads,),
            in_specs=[specs[kind][0] for kind, _ in ins],
            out_specs=[specs[kind][0] for kind in outs],
        ),
        out_shape=[jax.ShapeDtypeStruct(specs[kind][1], specs[kind][2]) for kind in outs],
        compiler_params=params(24),
        cost_estimate=cost(
            4 * HEAD * work * heads, 2 * rows * HEAD * heads * len(ins), work * heads
        ),
        name=name,
    )(flag, *[x for _, x in ins])


def self_attention(normed, w_query, w_key, w_value):
    rows = normed.shape[0]
    assert lax.axis_size("ctx") == 4
    ctx = lax.axis_index("ctx")
    width = w_query.shape[1] // 2
    heads = width // HEAD
    flag = ctx.reshape(1)
    merged = []
    for first in (0, width):
        q = project(normed, w_query, first, width)
        qa = lax.ppermute(q, "ctx", [(2, 1)])
        qb = lax.ppermute(q, "ctx", [(3, 1)])
        k = project(normed, w_key, first, width)
        k0 = lax.ppermute(k, "ctx", [(0, 1), (2, 3)])
        v = project(normed, w_value, first, width, flip=True)
        v0 = lax.ppermute(v, "ctx", [(0, 1), (2, 3)])
        keys = [("rows", k0), ("flat", v0), ("rows", k), ("flat", v)]
        oa, la, ob, lb = head_call(
            far_kernel, "far_attention", flag, rows, heads,
            [("rows", qa), ("rows", qb)] + keys, ["flat", "log"] * 2, 4 * rows * rows,
        )
        far_a = [lax.ppermute(x, "ctx", [(1, 2)]) for x in (oa, la)]
        far_b = [lax.ppermute(x, "ctx", [(1, 3)]) for x in (ob, lb)]
        o, l = head_call(
            near_kernel, "near_attention", flag, rows, heads,
            [("rows", q)] + keys, ["flat", "log"], 2 * rows * rows,
        )
        far_o, far_l = [jnp.where(ctx == 3, b, a) for a, b in zip(far_a, far_b)]
        (out,) = head_call(
            merge_kernel, "merge", flag, rows, heads,
            [("flat", o), ("log", l), ("flat", far_o), ("log", far_l)], ["rows"], rows,
        )
        merged.append(out)
    return jnp.concatenate(merged, axis=1)


def fetch_neighbours(encoded, owners, slots):
    group_count = lax.axis_size(("pool", "ctx"))
    my_group = lax.axis_index(("pool", "ctx"))
    per_group = owners.size // group_count
    capacity = max(2, 2 * per_group // group_count)
    owner_table = owners.reshape(group_count, per_group)
    slot_table = slots.reshape(group_count, per_group)
    matched = (owner_table == my_group).astype(jnp.int32)
    order_rank = jnp.cumsum(matched, axis=1) - 1
    slot_index = jnp.arange(capacity, dtype=jnp.int32)
    picked = matched[:, None, :] * (order_rank[:, None, :] == slot_index[None, :, None]).astype(
        jnp.int32
    )
    source_rows = jnp.sum(picked * slot_table[:, None, :], axis=2).reshape(-1)
    outgoing = encoded[source_rows].reshape((group_count, capacity) + encoded.shape[1:])
    incoming = lax.all_to_all(outgoing, ("pool", "ctx"), split_axis=0, concat_axis=0, tiled=True)
    wanted = lax.dynamic_index_in_dim(owner_table, my_group, 0, keepdims=False)
    positions = jnp.arange(per_group, dtype=jnp.int32)
    same_owner = (wanted[:, None] == wanted[None, :]).astype(jnp.int32)
    before_this = (positions[None, :] < positions[:, None]).astype(jnp.int32)
    arrival = wanted * capacity + jnp.sum(same_owner * before_this, axis=1)
    arrived = incoming.reshape((group_count * capacity,) + encoded.shape[1:])[arrival]
    earlier = from_behind(arrived[-NB_PER:], "ctx", 1)
    extended = jnp.concatenate([earlier, arrived], axis=0)
    return lax.all_gather(extended, "mp", axis=1, tiled=True)


def neighbour_kernel(x_ref, w_ref, out_ref):
    out_ref[0] = jnp.dot(x_ref[...], w_ref[0], preferred_element_type=jnp.float32).astype(
        jnp.bfloat16
    )


def neighbour_kv(fetched, w_cross_kv):
    rows, depth = fetched.shape[0] * fetched.shape[1], fetched.shape[2]
    width = w_cross_kv.shape[2]
    tile = min(width, 256)
    steps = width // tile
    return pl.pallas_call(
        neighbour_kernel,
        grid=(2, steps),
        in_specs=[
            pl.BlockSpec((rows, depth), lambda c, j: (0, 0)),
            pl.BlockSpec((1, depth, tile), lambda c, j: (c, 0, j)),
        ],
        out_specs=pl.BlockSpec((1, rows, tile), lambda c, j: (c, 0, j)),
        out_shape=jax.ShapeDtypeStruct((2, rows, width), jnp.bfloat16),
        compiler_params=params(32, 2),
        cost_estimate=cost(4 * rows * depth * width, 4 * rows * width + 2 * rows * depth),
        name="neighbour_kv",
    )(fetched.reshape(rows, depth), w_cross_kv)


def cross_kernel(q_ref, k_ref, v_ref, out_ref):
    rows = q_ref.shape[0]
    named = NB_PER * NB_TOK
    spans = rows // SPAN
    queries = pltpu.roll(q_ref[...].astype(jnp.float32), 1, 0).astype(jnp.bfloat16)

    def one(part, span):
        keys = k_ref[0, span * named : (span + 1) * named, :]
        values = v_ref[0, span * named : (span + 1) * named, :]
        s = lax.dot_general(
            part, keys, (((1,), (1,)), ((), ())), preferred_element_type=jnp.float32
        ) * (HEAD**-0.5 * LOG2E)
        weights = jnp.exp2(s - jnp.max(s, axis=1, keepdims=True))
        total = jnp.sum(weights, axis=1, keepdims=True)
        out = jnp.dot(weights.astype(jnp.bfloat16), values, preferred_element_type=jnp.float32)
        return out / total

    outs = [one(queries[c * SPAN : (c + 1) * SPAN], c) for c in range(spans)]
    last = one(queries[:16], spans)
    whole = jnp.concatenate(outs, axis=0)
    last_row = jnp.broadcast_to(last[:1], whole.shape)
    row = lax.broadcasted_iota(jnp.int32, whole.shape, 0)
    whole = jnp.where(row == 0, last_row, whole)
    out_ref[...] = pltpu.roll(whole, rows - 1, 0).astype(jnp.bfloat16)


def cross_attention(queries, kv):
    rows, width = queries.shape
    heads = width // HEAD
    return pl.pallas_call(
        cross_kernel,
        grid=(heads,),
        in_specs=[
            pl.BlockSpec((rows, HEAD), lambda h: (0, h)),
            pl.BlockSpec((1, kv.shape[1], HEAD), lambda h: (0, 0, h)),
            pl.BlockSpec((1, kv.shape[1], HEAD), lambda h: (1, 0, h)),
        ],
        out_specs=pl.BlockSpec((rows, HEAD), lambda h: (0, h)),
        out_shape=jax.ShapeDtypeStruct((rows, width), jnp.bfloat16),
        compiler_params=params(24),
        cost_estimate=cost(1024 * rows * width, 4 * kv.shape[1] * width, 2 * rows * width),
        name="cross_attention",
    )(queries, kv, kv)


def per_device(
    tokens,
    norm_gain,
    cross_gain,
    w_query,
    w_key,
    w_value,
    w_out,
    w_cross_query,
    w_cross_kv,
    w_cross_out,
    encoded,
    owners,
    slots,
):
    own = tokens[0]
    normed = normalised(gather_blocks(own), norm_gain)
    fetched = fetch_neighbours(encoded, owners, slots)
    attended = self_attention(normed, w_query, w_key, w_value)
    kv = neighbour_kv(fetched, w_cross_kv)
    share = project_scattered(attended, w_out)
    residual = (own.astype(jnp.float32) + share).astype(jnp.bfloat16)
    cross_in = normalised(gather_blocks(residual), cross_gain)
    cross_queries = project(cross_in, w_cross_query, 0, w_cross_query.shape[1])
    crossed = cross_attention(cross_queries, kv)
    cross_part = project_scattered(crossed, w_cross_out)
    return (residual.astype(jnp.float32) + cross_part).astype(jnp.bfloat16)[None]


def solution(mesh):
    placed = (
        P("pool", "ctx", "mp"),
        P(),
        P(),
        P(None, "mp"),
        P(None, "mp"),
        P(None, "mp"),
        P("mp", None),
        P(None, "mp"),
        P(None, None, "mp"),
        P("mp", None),
        P(("pool", "ctx"), "mp", None),
        P(),
        P(),
    )
    return jax.shard_map(
        per_device, mesh=mesh, in_specs=placed, out_specs=P("pool", "ctx", "mp"), check_vma=False
    )
```

time: 525 us -> 337 us (0.64); the launches traced: 516 us -> 334 us
  waiting for transfers between devices: 315 us -> 126 us
  Pallas kernels: 0 us -> 112 us
  matrix products: 104 us -> 0 us
  starting transfers between devices: 10.6 us -> 40.6 us
  other arithmetic: 35.1 us -> 9.96 us
  local copies, waits for them, and re-layouts: 38 us -> 31.1 us
    all_gather x5 -> x1, waiting for transfers between devices: 206 us -> 0.02 us  [fetch_neighbours(): return lax.all_gather(extended, 'mp', axis=1, tiled=True)]
    ppermute x0 -> x28, waiting for transfers between devices: none -> 123 us  [the longest x12 89.1 us: swap(): lax.ppermute(block, 'mp', [(i, i ^ bit) for i in range(lax.axis_size('mp'...]
    pallas_call x0 -> x25, Pallas kernels: none -> 112 us  [the longest x6 32.5 us: head_call(): pl.pallas_call(kernel, grid_spec=pltpu.PrefetchScalarGridSpec(num_scalar_...]
    dot_general x10 -> x0, matrix products: 86.8 us -> none  [the longest x1 16.2 us: update(): jnp.einsum('qhe,khe->hqk', queries, keys_here, preferred_element_type=jnp...]
    reduce_scatter x2 -> x0, waiting for transfers between devices: 44.7 us -> none  [the longest x1 44.7 us: per_device(): lax.psum_scatter(cross_terms.astype(jnp.bfloat16), 'mp', scatter_dimensio...]
    all_to_all x1, waiting for transfers between devices: 39.5 us -> 0.01 us  [fetch_neighbours(): lax.all_to_all(outgoing, ('pool', 'ctx'), split_axis=0, concat_axis=0, ti...]
    ppermute x0 -> x28, starting transfers between devices: none -> 32.3 us  [the longest x4 8.67 us: self_attention(): far_a = [lax.ppermute(x, 'ctx', [(1, 2)]) for x in (oa, la)]]
    reduce_sum x5 -> x1, other arithmetic: 23.7 us -> 0.15 us  [fetch_neighbours(): source_rows = jnp.sum(picked * slot_table[:, None, :], axis=2).reshape(-1)]
  transfers between devices with their start and end apart: 9 -> 31, of which waited for: 7 -> 11; matrix products, arithmetic and copies ran while one was open for 14% -> 5% of each run, Pallas kernels for 0% -> 23%
where the time goes in v1:
time: 337 us; the launch traced here: 334 us
  waiting for transfers between devices  126 us (37%)
  Pallas kernels  112 us (33%)
  starting transfers between devices  40.6 us (12%)
  local copies, waits for them, and re-layouts  31.1 us (9%)
  between operations  14.1 us (4%)
  other arithmetic  9.96 us (3%)
    ppermute x12, waiting for transfers between devices, swap(): lax.ppermute(block, 'mp', [(i, i ^ bit) for i in range(lax.axis_size('mp'...  89.1 us
    pallas_call x6, Pallas kernels, head_call(): pl.pallas_call(kernel, grid_spec=pltpu.PrefetchScalarGridSpec(num_scalar_...  32.5 us
    pallas_call x7, Pallas kernels, project(): pl.pallas_call(functools.partial(project_kernel, flip), grid=(width // ti...  25.5 us
    ppermute x2, waiting for transfers between devices, self_attention(): qa = lax.ppermute(q, 'ctx', [(2, 1)])  24 us
    unnamed x44, local copies, waits for them, and re-layouts  22.8 us
    pallas_call x1, Pallas kernels, cross_attention(): pl.pallas_call(cross_kernel, grid=(heads,), in_specs=[pl.BlockSpec((rows,...  20.9 us
    pallas_call x8, Pallas kernels, project_block(): pl.pallas_call(block_kernel, grid_spec=pltpu.PrefetchScalarGridSpec(num_s...  13.5 us
    pallas_call x1, Pallas kernels, neighbour_kv(): pl.pallas_call(neighbour_kernel, grid=(2, steps), in_specs=[pl.BlockSpec(...  13 us
  transfers between devices with their start and end apart: 31, of which 11 were waited for; matrix products, arithmetic and copies ran while one was open for 5% of the time, Pallas kernels for 23%

profile of v1, /device:TPU:12, one launch (start us, length us, event | category | flops | bytes accessed | tf_op | source)
XLA Modules:
  0.0 334.1 jit_solution(6692425227539439698)
XLA Ops:
  6.5 1.5 collective-permute-start.1
  10.2 4.0 %gather_fusion = bf16[32,32,896]{2,1,0:T(8,128)(2,1)} fusion(bf16[64,32,896]{2,1,0:T(8,128)(2,1)} %param.23, s32[1024]{0:T(1024)S(1)} %pad_clamp_fusion.1), kind=kCustom, calls=%fused_computation | custom fusion | bytes 3670144 | tf_op jit(solution)/shard_map/gather | solution.py:317
  14.3 6.4 %all-to-all-start = ((bf16[8,4,32,896]{3,2,1,0:T(8,128)(2,1)}), bf16[8,4,32,896]{3,2,1,0:T(8,128)(2,1)}, u32[]{:S(2)}, u32[]{:S(2)}) async-start(bf16[8,4,32,896]{3,2,1,0:T(8,128)(2,1)} %bitcast.42), calls=%async_computation | async-start | bytes 3670016 | tf_op jit(solution)/shard_map/all_to_all | solution.py:318
  20.7 10.9 %collective-permute-done.1.refs_2_ = bf16[512,1024]{1,0:T(8,128)(2,1)S(1)} collective-permute-done((bf16[512,1024]{1,0:T(8,128)(2,1)}, bf16[512,1024]{1,0:T(8,128)(2,1)S(1)}, u32[]{:S(2)}, u32[]{:S(2)}) %collective-permute-start.1) | collective-permute-done | bytes 1048608 | tf_op jit(solution)/shard_map/ppermute | solution.py:37
  31.8 2.6 collective-permute-done.2.refs_3_
  34.4 4.2 %norm.2.x_ref = bf16[512,4096]{1,0:T(8,128)(2,1)S(1)} custom-call(s32[4]{0:T(128)S(1)} %iota_xor_fusion.place_ref, f32[1,4096]{1,0:T(1,128)S(1)} %bitcast.37, bf16[512,1024]{1,0:T(8,128)(2,1)S(1)} %bitcast.36, bf16[512,1024]{1,0:T(8,128)(2,1)S(1)} %collective-permute-done.refs_1_, bf16[512,1024]{1,0:T(8,128)(2,1)S(1)} %collective-permute-done.1.refs_2_, ...), custom_call_target="tpu_custom_call" | custom-call | flops 12582912 | bytes 8388608 | tf_op jit(solution)/shard_map/norm/pallas_call | solution.py:85
  38.6 3.4 %copy-done.3 = bf16[4096,1024]{1,0:T(8,128)(2,1)S(1)} copy-done((bf16[4096,1024]{1,0:T(8,128)(2,1)S(1)}, bf16[4096,1024]{1,0:T(8,128)(2,1)}, u32[]{:S(2)}) %copy-start.3) | copy-done | bytes 8388632
  42.0 3.2 project.7.q
  45.2 1.6 collective-permute-start.6
  46.7 1.3 collective-permute-start.5
  48.1 3.4 %copy-done.4 = bf16[4096,1024]{1,0:T(8,128)(2,1)S(1)} copy-done((bf16[4096,1024]{1,0:T(8,128)(2,1)S(1)}, bf16[4096,1024]{1,0:T(8,128)(2,1)}, u32[]{:S(2)}) %copy-start.4) | copy-done | bytes 8388632
  51.4 3.2 project.8.k1
  54.6 1.6 collective-permute-start.3
  56.2 3.3 project.9.v1
  59.5 1.3 collective-permute-start.4
  60.8 3.2 project.10.q
  64.0 1.3 collective-permute-start.14
  65.3 3.3 project.12.v1
  68.6 3.2 project.11.k1
  71.7 1.3 collective-permute-start.13
  73.0 24.0 %collective-permute-done.5.qa = bf16[512,512]{1,0:T(8,128)(2,1)S(1)} collective-permute-done((bf16[512,512]{1,0:T(8,128)(2,1)S(1)}, bf16[512,512]{1,0:T(8,128)(2,1)S(1)}, u32[]{:S(2)}, u32[]{:S(2)}) %collective-permute-start.5) | collective-permute-done | bytes 524320 | tf_op jit(solution)/shard_map/ppermute | solution.py:277
  97.0 1.3 collective-permute-start.11
  98.3 1.5 collective-permute-start.12
  99.8 10.8 %far_attention.2 = (bf16[512,512]{1,0:T(8,128)(2,1)S(1)}, f32[4,1,512]{2,1,0:T(1,128)S(1)}, bf16[512,512]{1,0:T(8,128)(2,1)}, f32[4,1,512]{2,1,0:T(1,128)S(1)}) custom-call(s32[1]{0:T(128)} %bitcast.2.flag_ref, bf16[512,512]{1,0:T(8,128)(2,1)S(1)} %collective-permute-done.5.qa, bf16[512,512]{1,0:T(8,128)(2,1)S(1)} %collective-permute-done.6.qb, ...), custom_call_target="tpu_custom_call" | custom-call | flops 2147483648 | bytes 3145728 | tf_op jit(solution)/shard_map/far_attention/pallas_call | solution.py:250
  111.9 1.3 collective-permute-start.10
  113.2 2.1 collective-permute-start.7
  115.3 2.1 collective-permute-start.8
  117.4 3.1 collective-permute-done.12.v0
  120.5 10.0 %far_attention.3 = (bf16[512,512]{1,0:T(8,128)(2,1)S(1)}, f32[4,1,512]{2,1,0:T(1,128)S(1)}, bf16[512,512]{1,0:T(8,128)(2,1)S(1)}, f32[4,1,512]{2,1,0:T(1,128)S(1)}) custom-call(s32[1]{0:T(128)} %bitcast.2.flag_ref, bf16[512,512]{1,0:T(8,128)(2,1)S(1)} %collective-permute-done.13.qa, bf16[512,512]{1,0:T(8,128)(2,1)S(1)} %collective-permute-done.14.qb, ...), custom_call_target="tpu_custom_call" | custom-call | flops 2147483648 | bytes 3145728 | tf_op jit(solution)/shard_map/far_attention/pallas_call | solution.py:250
  130.6 2.4 collective-permute-start.17
  133.0 5.1 %near_attention.2 = (bf16[512,512]{1,0:T(8,128)(2,1)S(1)}, f32[4,1,512]{2,1,0:T(1,128)S(1)}) custom-call(s32[1]{0:T(128)} %bitcast.2.flag_ref, bf16[512,512]{1,0:T(8,128)(2,1)S(1)} %project.7.q, bf16[512,512]{1,0:T(8,128)(2,1)S(1)} %collective-permute-done.3.k0, bf16[512,512]{1,0:T(8,128)(2,1)S(1)} %collective-permute-done.4.v0, ...), custom_call_target="tpu_custom_call" | custom-call | flops 1073741824 | bytes 2621440 | tf_op jit(solution)/shard_map/near_attention/pallas_call | solution.py:250
  138.2 5.1 %near_attention.3 = (bf16[512,512]{1,0:T(8,128)(2,1)S(1)}, f32[4,1,512]{2,1,0:T(1,128)S(1)}) custom-call(s32[1]{0:T(128)} %bitcast.2.flag_ref, bf16[512,512]{1,0:T(8,128)(2,1)S(1)} %project.10.q, bf16[512,512]{1,0:T(8,128)(2,1)S(1)} %collective-permute-done.11.k0, bf16[512,512]{1,0:T(8,128)(2,1)S(1)} %collective-permute-done.12.v0, ...), custom_call_target="tpu_custom_call" | custom-call | flops 1073741824 | bytes 2621440 | tf_op jit(solution)/shard_map/near_attention/pallas_call | solution.py:250
  143.3 3.1 gather_fusion.1
  147.3 1.3 collective-permute-start.18
  148.6 1.9 collective-permute-start.25
  150.6 2.1 collective-permute-start.15
  152.7 2.6 collective-permute-done.25
  155.3 4.0 %collective-permute-start.16 = (bf16[512,512]{1,0:T(8,128)(2,1)S(1)}, bf16[512,512]{1,0:T(8,128)(2,1)}, u32[]{:S(2)}, u32[]{:S(2)}) collective-permute-start(bf16[512,512]{1,0:T(8,128)(2,1)S(1)} %get-tuple-element.26), channel_id=1, source_target_pairs={{4,8},{5,9},{6,10},{7,11},{20,24},{21,25},{22,26},{23,27}} | collective-permute-start | bytes 1572872 | tf_op jit(solution)/shard_map/ppermute | solution.py:288
  159.3 2.2 pad_maximum_fusion.1
  163.6 1.6 collective-permute-done.15
  165.3 5.5 %collective-permute-done.16 = bf16[512,512]{1,0:T(8,128)(2,1)} collective-permute-done((bf16[512,512]{1,0:T(8,128)(2,1)S(1)}, bf16[512,512]{1,0:T(8,128)(2,1)}, u32[]{:S(2)}, u32[]{:S(2)}) %collective-permute-start.16) | collective-permute-done | bytes 524320 | tf_op jit(solution)/shard_map/ppermute | solution.py:288
  172.7 3.4 %copy-done = bf16[1024,4096]{1,0:T(8,128)(2,1)S(1)} copy-done((bf16[1024,4096]{1,0:T(8,128)(2,1)S(1)}, bf16[1024,4096]{1,0:T(8,128)(2,1)}, u32[]{:S(2)}) %copy-start) | copy-done | bytes 8388632
  176.1 1.7 project_block.11
  177.9 3.4 %copy-done.1 = bf16[1024,4096]{1,0:T(8,128)(2,1)S(1)} copy-done((bf16[1024,4096]{1,0:T(8,128)(2,1)S(1)}, bf16[1024,4096]{1,0:T(8,128)(2,1)}, u32[]{:S(2)}) %copy-start.1) | copy-done | bytes 8388632
  181.3 1.7 project_block.9
  183.6 1.7 project_block.10
  185.3 1.6 add_convert_fusion.4
  187.5 1.7 project_block.8
  189.3 25.6 %collective-permute-done.21 = bf16[512,1024]{1,0:T(8,128)(2,1)S(1)} collective-permute-done((bf16[512,1024]{1,0:T(8,128)(2,1)S(1)}, bf16[512,1024]{1,0:T(8,128)(2,1)S(1)}, u32[]{:S(2)}, u32[]{:S(2)}) %collective-permute-start.21) | collective-permute-done | bytes 1048608 | tf_op jit(solution)/shard_map/ppermute | solution.py:37
  216.4 24.3 %collective-permute-done.23.refs_2_ = bf16[512,1024]{1,0:T(8,128)(2,1)S(1)} collective-permute-done((bf16[512,1024]{1,0:T(8,128)(2,1)S(1)}, bf16[512,1024]{1,0:T(8,128)(2,1)S(1)}, u32[]{:S(2)}, u32[]{:S(2)}) %collective-permute-start.23) | collective-permute-done | bytes 1048608 | tf_op jit(solution)/shard_map/ppermute | solution.py:37
  240.8 2.7 collective-permute-done.24.refs_3_
  243.4 2.8 norm.3.x_ref
  246.3 6.3 %project.13.q_ref = bf16[512,1024]{1,0:T(8,128)(2,1)S(1)} custom-call(bf16[512,4096]{1,0:T(8,128)(2,1)S(1)} %norm.3.x_ref, bf16[4096,1024]{1,0:T(8,128)(2,1)S(1)} %bitcast.40), custom_call_target="tpu_custom_call" | custom-call | flops 4294967296 | bytes 12582912 | tf_op jit(solution)/shard_map/project/pallas_call | solution.py:116
  252.6 2.2 copy-done.8
  254.8 2.0 copy-done.9
  256.8 13.0 %neighbour_kv.1.k_ref.v_ref = bf16[2,2304,1024]{2,1,0:T(8,128)(2,1)S(1)} custom-call(bf16[2304,896]{1,0:T(8,128)(2,1)S(1)} %bitcast.41, bf16[2,896,1024]{2,1,0:T(8,128)(2,1)S(1)} %copy-done.9), custom_call_target="tpu_custom_call" | custom-call | flops 8455716864 | bytes 13565952 | tf_op jit(solution)/shard_map/neighbour_kv/pallas_call | solution.py:341
  269.8 20.9 %cross_attention.1.x_ref = bf16[512,1024]{1,0:T(8,128)(2,1)S(1)} custom-call(bf16[512,1024]{1,0:T(8,128)(2,1)S(1)} %project.13.q_ref, bf16[2,2304,1024]{2,1,0:T(8,128)(2,1)S(1)} %neighbour_kv.1.k_ref.v_ref, bf16[2,2304,1024]{2,1,0:T(8,128)(2,1)S(1)} %neighbour_kv.1.k_ref.v_ref), custom_call_target="tpu_custom_call" | custom-call | flops 536870912 | bytes 9437184 | tf_op jit(solution)/shard_map/cross_attention/pallas_call | solution.py:385
  290.7 3.4 %copy-done.2 = bf16[1024,4096]{1,0:T(8,128)(2,1)S(1)} copy-done((bf16[1024,4096]{1,0:T(8,128)(2,1)S(1)}, bf16[1024,4096]{1,0:T(8,128)(2,1)}, u32[]{:S(2)}) %copy-start.2) | copy-done | bytes 8388632
  294.0 1.7 project_block.15
  295.9 1.7 project_block.13
  298.1 1.7 project_block.14
  300.8 1.7 project_block.12
  302.5 22.9 %collective-permute-done.28 = bf16[512,1024]{1,0:T(8,128)(2,1)S(1)} collective-permute-done((bf16[512,1024]{1,0:T(8,128)(2,1)S(1)}, bf16[512,1024]{1,0:T(8,128)(2,1)S(1)}, u32[]{:S(2)}, u32[]{:S(2)}) %collective-permute-start.28) | collective-permute-done | bytes 1048608 | tf_op jit(solution)/shard_map/ppermute | solution.py:37
  325.4 1.9 fusion
  (101 shorter events, 13.1 us)
Async XLA Ops:
  6.5 25.1 %collective-permute-start.1 = (bf16[512,1024]{1,0:T(8,128)(2,1)}, bf16[512,1024]{1,0:T(8,128)(2,1)S(1)}, u32[]{:S(2)}, u32[]{:S(2)}) collective-permute-start(bf16[512,1024]{1,0:T(8,128)(2,1)} %bitcast.34), channel_id=1, source_target_pairs={{0,2},{1,3},{2,0},{3,1},{4,6},{5,7},{6,4},{7,5},{8,10},{9,11},{10,... | collective-permute-start | bytes 3145736 | tf_op jit(solution)/shard_map/ppermute | solution.py:37
  14.3 6.4 %copy-start.5 = (bf16[1,512,1024]{2,1,0:T(8,128)(2,1)S(1)}, bf16[1,512,1024]{2,1,0:T(8,128)(2,1)}, u32[]{:S(2)}) copy-start(bf16[1,512,1024]{2,1,0:T(8,128)(2,1)} %param.13) | copy-start | bytes 3145732
  14.3 20.2 %copy-start.6 = (f32[4096]{0:T(1024)S(1)}, f32[4096]{0:T(1024)}, u32[]{:S(2)}) copy-start(f32[4096]{0:T(1024)} %param.14) | copy-start | bytes 49156
  14.3 129.1 %all-to-all-start = ((bf16[8,4,32,896]{3,2,1,0:T(8,128)(2,1)}), bf16[8,4,32,896]{3,2,1,0:T(8,128)(2,1)}, u32[]{:S(2)}, u32[]{:S(2)}) async-start(bf16[8,4,32,896]{3,2,1,0:T(8,128)(2,1)} %bitcast.42), calls=%async_computation | async-start | bytes 3670016 | tf_op jit(solution)/shard_map/all_to_all | solution.py:318
  20.6 232.0 %all-gather.2.cloned.1.call-start = ((), (), s32[]{:S(2)}) async-start(), calls=%async_computation.1 | async-start | bytes 5160960 | tf_op jit(solution)/shard_map/all_gather | solution.py:327
  20.6 11.2 %collective-permute-start = (bf16[512,1024]{1,0:T(8,128)(2,1)S(1)}, bf16[512,1024]{1,0:T(8,128)(2,1)S(1)}, u32[]{:S(2)}, u32[]{:S(2)}) collective-permute-start(bf16[512,1024]{1,0:T(8,128)(2,1)S(1)} %bitcast.35), channel_id=1, source_target_pairs={{0,1},{1,0},{2,3},{3,2},{4,5},{5,4},{6,7},{7,6},{8,9},{9,8},{10,11... | collective-permute-start | bytes 3145736 | tf_op jit(solution)/shard_map/ppermute | solution.py:37
  31.6 2.8 collective-permute-start.2
  38.6 3.4 %copy-start.3 = (bf16[4096,1024]{1,0:T(8,128)(2,1)S(1)}, bf16[4096,1024]{1,0:T(8,128)(2,1)}, u32[]{:S(2)}) copy-start(bf16[4096,1024]{1,0:T(8,128)(2,1)} %w_ref.19) | copy-start | bytes 25165828
  42.0 14.2 %slice-start.6 = ((s8[8388608]{0:T(1024)(128)(4,1)}), s8[4194304]{0:T(1024)(128)(4,1)S(1)}, s32[]{:S(2)}) async-start(s8[8388608]{0:T(1024)(128)(4,1)} %bitcast.32), calls=%async_computation.8 | async-start | bytes 8388608
  45.2 11.0 %slice-start.7 = ((s8[8388608]{0:T(1024)(128)(4,1)}), s8[4194304]{0:T(1024)(128)(4,1)S(1)}, s32[]{:S(2)}) async-start(s8[8388608]{0:T(1024)(128)(4,1)} %bitcast.32), calls=%async_computation.9 | async-start | bytes 8388608
  45.2 26.6 %collective-permute-start.6 = (bf16[512,512]{1,0:T(8,128)(2,1)S(1)}, bf16[512,512]{1,0:T(8,128)(2,1)S(1)}, u32[]{:S(2)}, u32[]{:S(2)}) collective-permute-start(bf16[512,512]{1,0:T(8,128)(2,1)S(1)} %project.7.q), channel_id=1, source_target_pairs={{12,4},{13,5},{14,6},{15,7},{28,20},{29,21},{30,22},{31,23}} | collective-permute-start | bytes 1572872 | tf_op jit(solution)/shard_map/ppermute | solution.py:278
  46.7 50.2 %collective-permute-start.5 = (bf16[512,512]{1,0:T(8,128)(2,1)S(1)}, bf16[512,512]{1,0:T(8,128)(2,1)S(1)}, u32[]{:S(2)}, u32[]{:S(2)}) collective-permute-start(bf16[512,512]{1,0:T(8,128)(2,1)S(1)} %project.7.q), channel_id=1, source_target_pairs={{8,4},{9,5},{10,6},{11,7},{24,20},{25,21},{26,22},{27,23}} | collective-permute-start | bytes 1572872 | tf_op jit(solution)/shard_map/ppermute | solution.py:277
  48.0 3.4 %copy-start.4 = (bf16[4096,1024]{1,0:T(8,128)(2,1)S(1)}, bf16[4096,1024]{1,0:T(8,128)(2,1)}, u32[]{:S(2)}) copy-start(bf16[4096,1024]{1,0:T(8,128)(2,1)} %w_ref.20) | copy-start | bytes 25165828
  51.4 9.4 %slice-start.4 = ((s8[8388608]{0:T(1024)(128)(4,1)}), s8[4194304]{0:T(1024)(128)(4,1)S(1)}, s32[]{:S(2)}) async-start(s8[8388608]{0:T(1024)(128)(4,1)} %bitcast.30), calls=%async_computation.6 | async-start | bytes 8388608
  54.6 6.2 %slice-start.5 = ((s8[8388608]{0:T(1024)(128)(4,1)}), s8[4194304]{0:T(1024)(128)(4,1)S(1)}, s32[]{:S(2)}) async-start(s8[8388608]{0:T(1024)(128)(4,1)} %bitcast.30), calls=%async_computation.7 | async-start | bytes 8388608
  54.6 43.7 %collective-permute-start.3 = (bf16[512,512]{1,0:T(8,128)(2,1)S(1)}, bf16[512,512]{1,0:T(8,128)(2,1)S(1)}, u32[]{:S(2)}, u32[]{:S(2)}) collective-permute-start(bf16[512,512]{1,0:T(8,128)(2,1)S(1)} %project.8.k1), channel_id=1, source_target_pairs={{0,4},{8,12},{1,5},{9,13},{2,6},{10,14},{3,7},{11,15},{16,20},{24,... | collective-permute-start | bytes 1572872 | tf_op jit(solution)/shard_map/ppermute | solution.py:280
  59.5 40.3 %collective-permute-start.4 = (bf16[512,512]{1,0:T(8,128)(2,1)S(1)}, bf16[512,512]{1,0:T(8,128)(2,1)S(1)}, u32[]{:S(2)}, u32[]{:S(2)}) collective-permute-start(bf16[512,512]{1,0:T(8,128)(2,1)S(1)} %project.9.v1), channel_id=1, source_target_pairs={{0,4},{8,12},{1,5},{9,13},{2,6},{10,14},{3,7},{11,15},{16,20},{24,... | collective-permute-start | bytes 1572872 | tf_op jit(solution)/shard_map/ppermute | solution.py:282
  64.0 47.9 %collective-permute-start.14 = (bf16[512,512]{1,0:T(8,128)(2,1)S(1)}, bf16[512,512]{1,0:T(8,128)(2,1)S(1)}, u32[]{:S(2)}, u32[]{:S(2)}) collective-permute-start(bf16[512,512]{1,0:T(8,128)(2,1)S(1)} %project.10.q), channel_id=1, source_target_pairs={{12,4},{13,5},{14,6},{15,7},{28,20},{29,21},{30,22},{31,23}} | collective-permute-start | bytes 1572872 | tf_op jit(solution)/shard_map/ppermute | solution.py:278
  71.7 41.4 %collective-permute-start.13 = (bf16[512,512]{1,0:T(8,128)(2,1)S(1)}, bf16[512,512]{1,0:T(8,128)(2,1)S(1)}, u32[]{:S(2)}, u32[]{:S(2)}) collective-permute-start(bf16[512,512]{1,0:T(8,128)(2,1)S(1)} %project.10.q), channel_id=1, source_target_pairs={{8,4},{9,5},{10,6},{11,7},{24,20},{25,21},{26,22},{27,23}} | collective-permute-start | bytes 1572872 | tf_op jit(solution)/shard_map/ppermute | solution.py:277
  97.0 18.3 %collective-permute-start.11 = (bf16[512,512]{1,0:T(8,128)(2,1)S(1)}, bf16[512,512]{1,0:T(8,128)(2,1)S(1)}, u32[]{:S(2)}, u32[]{:S(2)}) collective-permute-start(bf16[512,512]{1,0:T(8,128)(2,1)S(1)} %project.11.k1), channel_id=1, source_target_pairs={{0,4},{8,12},{1,5},{9,13},{2,6},{10,14},{3,7},{11,15},{16,20},{24,... | collective-permute-start | bytes 1572872 | tf_op jit(solution)/shard_map/ppermute | solution.py:280
  98.3 22.2 %collective-permute-start.12 = (bf16[512,512]{1,0:T(8,128)(2,1)S(1)}, bf16[512,512]{1,0:T(8,128)(2,1)S(1)}, u32[]{:S(2)}, u32[]{:S(2)}) collective-permute-start(bf16[512,512]{1,0:T(8,128)(2,1)S(1)} %project.12.v1), channel_id=1, source_target_pairs={{0,4},{8,12},{1,5},{9,13},{2,6},{10,14},{3,7},{11,15},{16,20},{24,... | collective-permute-start | bytes 1572872 | tf_op jit(solution)/shard_map/ppermute | solution.py:282
  110.6 36.7 %collective-permute-start.9 = (f32[4,1,512]{2,1,0:T(1,128)S(1)}, f32[4,1,512]{2,1,0:T(1,128)S(1)}, u32[]{:S(2)}, u32[]{:S(2)}) collective-permute-start(f32[4,1,512]{2,1,0:T(1,128)S(1)} %get-tuple-element.21), channel_id=1, source_target_pairs={{4,12},{5,13},{6,14},{7,15},{20,28},{21,29},{22,30},{23,31}} | collective-permute-start | bytes 24584 | tf_op jit(solution)/shard_map/ppermute | solution.py:289
  111.9 36.8 %collective-permute-start.10 = (f32[4,1,512]{2,1,0:T(1,128)S(1)}, f32[4,1,512]{2,1,0:T(1,128)S(1)}, u32[]{:S(2)}, u32[]{:S(2)}) collective-permute-start(f32[4,1,512]{2,1,0:T(1,128)S(1)} %get-tuple-element.22), channel_id=1, source_target_pairs={{4,8},{5,9},{6,10},{7,11},{20,24},{21,25},{22,26},{23,27}} | collective-permute-start | bytes 24584 | tf_op jit(solution)/shard_map/ppermute | solution.py:288
  113.2 48.4 %collective-permute-start.7 = (bf16[512,512]{1,0:T(8,128)(2,1)}, bf16[512,512]{1,0:T(8,128)(2,1)}, u32[]{:S(2)}, u32[]{:S(2)}) collective-permute-start(bf16[512,512]{1,0:T(8,128)(2,1)} %get-tuple-element.19), channel_id=1, source_target_pairs={{4,12},{5,13},{6,14},{7,15},{20,28},{21,29},{22,30},{23,31}} | collective-permute-start | bytes 1572872 | tf_op jit(solution)/shard_map/ppermute | solution.py:289
  115.3 46.3 %collective-permute-start.8 = (bf16[512,512]{1,0:T(8,128)(2,1)S(1)}, bf16[512,512]{1,0:T(8,128)(2,1)}, u32[]{:S(2)}, u32[]{:S(2)}) collective-permute-start(bf16[512,512]{1,0:T(8,128)(2,1)S(1)} %get-tuple-element.20), channel_id=1, source_target_pairs={{4,8},{5,9},{6,10},{7,11},{20,24},{21,25},{22,26},{23,27}} | collective-permute-start | bytes 1572872 | tf_op jit(solution)/shard_map/ppermute | solution.py:288
  130.6 7.6 %copy-start.10 = (bf16[512,512]{1,0:T(8,128)(2,1)}, bf16[512,512]{1,0:T(8,128)(2,1)S(1)}, u32[]{:S(2)}) copy-start(bf16[512,512]{1,0:T(8,128)(2,1)S(1)} %get-tuple-element.25) | copy-start | bytes 1572868
  130.6 20.0 %collective-permute-start.17 = (f32[4,1,512]{2,1,0:T(1,128)S(1)}, f32[4,1,512]{2,1,0:T(1,128)S(1)}, u32[]{:S(2)}, u32[]{:S(2)}) collective-permute-start(f32[4,1,512]{2,1,0:T(1,128)S(1)} %get-tuple-element.27), channel_id=1, source_target_pairs={{4,12},{5,13},{6,14},{7,15},{20,28},{21,29},{22,30},{23,31}} | collective-permute-start | bytes 24584 | tf_op jit(solution)/shard_map/ppermute | solution.py:289
  147.3 14.3 %collective-permute-start.18 = (f32[4,1,512]{2,1,0:T(1,128)S(1)}, f32[4,1,512]{2,1,0:T(1,128)S(1)}, u32[]{:S(2)}, u32[]{:S(2)}) collective-permute-start(f32[4,1,512]{2,1,0:T(1,128)S(1)} %get-tuple-element.28), channel_id=1, source_target_pairs={{4,8},{5,9},{6,10},{7,11},{20,24},{21,25},{22,26},{23,27}} | collective-permute-start | bytes 24584 | tf_op jit(solution)/shard_map/ppermute | solution.py:288
  148.6 6.7 %collective-permute-start.25 = (bf16[2,32,896]{2,1,0:T(8,128)(2,1)S(1)}, bf16[2,32,896]{2,1,0:T(8,128)(2,1)S(1)}, u32[]{:S(2)}, u32[]{:S(2)}) collective-permute-start(bf16[2,32,896]{2,1,0:T(8,128)(2,1)S(1)} %slice.8), channel_id=1, source_target_pairs={{0,4},{4,8},{8,12},{1,5},{5,9},{9,13},{2,6},{6,10},{10,14},{3,7},{... | collective-permute-start | bytes 344072 | tf_op jit(solution)/shard_map/ppermute | solution.py:33
  150.6 14.7 %collective-permute-start.15 = (bf16[512,512]{1,0:T(8,128)(2,1)}, bf16[512,512]{1,0:T(8,128)(2,1)}, u32[]{:S(2)}, u32[]{:S(2)}) collective-permute-start(bf16[512,512]{1,0:T(8,128)(2,1)} %copy-done.10), channel_id=1, source_target_pairs={{4,12},{5,13},{6,14},{7,15},{20,28},{21,29},{22,30},{23,31}} | collective-permute-start | bytes 1572872 | tf_op jit(solution)/shard_map/ppermute | solution.py:289
  155.3 15.4 %collective-permute-start.16 = (bf16[512,512]{1,0:T(8,128)(2,1)S(1)}, bf16[512,512]{1,0:T(8,128)(2,1)}, u32[]{:S(2)}, u32[]{:S(2)}) collective-permute-start(bf16[512,512]{1,0:T(8,128)(2,1)S(1)} %get-tuple-element.26), channel_id=1, source_target_pairs={{4,8},{5,9},{6,10},{7,11},{20,24},{21,25},{22,26},{23,27}} | collective-permute-start | bytes 1572872 | tf_op jit(solution)/shard_map/ppermute | solution.py:288
  172.6 3.4 %copy-start = (bf16[1024,4096]{1,0:T(8,128)(2,1)S(1)}, bf16[1024,4096]{1,0:T(8,128)(2,1)}, u32[]{:S(2)}) copy-start(bf16[1024,4096]{1,0:T(8,128)(2,1)} %w_ref.25) | copy-start | bytes 25165828
  177.8 7.5 %collective-permute-start.20 = (bf16[512,1024]{1,0:T(8,128)(2,1)S(1)}, bf16[512,1024]{1,0:T(8,128)(2,1)}, u32[]{:S(2)}, u32[]{:S(2)}) collective-permute-start(bf16[512,1024]{1,0:T(8,128)(2,1)S(1)} %project_block.11), channel_id=1, source_target_pairs={{0,1},{1,0},{2,3},{3,2},{4,5},{5,4},{6,7},{7,6},{8,9},{9,8},{10,11... | collective-permute-start | bytes 3145736 | tf_op jit(solution)/shard_map/ppermute | solution.py:37
  177.9 3.4 %copy-start.1 = (bf16[1024,4096]{1,0:T(8,128)(2,1)S(1)}, bf16[1024,4096]{1,0:T(8,128)(2,1)}, u32[]{:S(2)}) copy-start(bf16[1024,4096]{1,0:T(8,128)(2,1)} %w_ref.25) | copy-start | bytes 25165828
  181.3 6.2 %slice-start = ((s8[8388608]{0:T(1024)(128)(4,1)}), s8[4194304]{0:T(1024)(128)(4,1)S(1)}, s32[]{:S(2)}) async-start(s8[8388608]{0:T(1024)(128)(4,1)} %bitcast.26), calls=%async_computation.2 | async-start | bytes 8388608
  183.0 6.3 %collective-permute-start.19 = (bf16[512,1024]{1,0:T(8,128)(2,1)S(1)}, bf16[512,1024]{1,0:T(8,128)(2,1)S(1)}, u32[]{:S(2)}, u32[]{:S(2)}) collective-permute-start(bf16[512,1024]{1,0:T(8,128)(2,1)S(1)} %project_block.9), channel_id=1, source_target_pairs={{0,1},{1,0},{2,3},{3,2},{4,5},{5,4},{6,7},{7,6},{8,9},{9,8},{10,11... | collective-permute-start | bytes 3145736 | tf_op jit(solution)/shard_map/ppermute | solution.py:37
  183.6 3.9 %slice-start.1 = ((s8[8388608]{0:T(1024)(128)(4,1)}), s8[4194304]{0:T(1024)(128)(4,1)S(1)}, s32[]{:S(2)}) async-start(s8[8388608]{0:T(1024)(128)(4,1)} %bitcast.26), calls=%async_computation.3 | async-start | bytes 8388608
  186.9 28.0 %collective-permute-start.21 = (bf16[512,1024]{1,0:T(8,128)(2,1)S(1)}, bf16[512,1024]{1,0:T(8,128)(2,1)S(1)}, u32[]{:S(2)}, u32[]{:S(2)}) collective-permute-start(bf16[512,1024]{1,0:T(8,128)(2,1)S(1)} %add_convert_fusion.4), channel_id=1, source_target_pairs={{0,2},{1,3},{2,0},{3,1},{4,6},{5,7},{6,4},{7,5},{8,10},{9,11},{10,... | collective-permute-start | bytes 3145736 | tf_op jit(solution)/shard_map/ppermute | solution.py:37
  187.5 58.7 %slice-start.8 = ((s8[8388608]{0:T(1024)(128)(4,1)}), s8[4194304]{0:T(1024)(128)(4,1)S(1)}, s32[]{:S(2)}) async-start(s8[8388608]{0:T(1024)(128)(4,1)} %bitcast.39), calls=%async_computation.10 | async-start | bytes 8388608
  189.2 54.2 %copy-start.7 = (f32[4096]{0:T(1024)S(1)}, f32[4096]{0:T(1024)}, u32[]{:S(2)}) copy-start(f32[4096]{0:T(1024)} %param.15) | copy-start | bytes 49156
  189.2 57.0 %slice-start.9 = ((s8[8388608]{0:T(1024)(128)(4,1)}), s8[4194304]{0:T(1024)(128)(4,1)S(1)}, s32[]{:S(2)}) async-start(s8[8388608]{0:T(1024)(128)(4,1)} %bitcast.39), calls=%async_computation.11 | async-start | bytes 8388608
  215.8 24.9 %collective-permute-start.23 = (bf16[512,1024]{1,0:T(8,128)(2,1)S(1)}, bf16[512,1024]{1,0:T(8,128)(2,1)S(1)}, u32[]{:S(2)}, u32[]{:S(2)}) collective-permute-start(bf16[512,1024]{1,0:T(8,128)(2,1)S(1)} %add_convert_fusion.3.refs_0_), channel_id=1, source_target_pairs={{0,2},{1,3},{2,0},{3,1},{4,6},{5,7},{6,4},{7,5},{8,10},{9,11},{10,... | collective-permute-start | bytes 3145736 | tf_op jit(solution)/shard_map/ppermute | solution.py:37
  216.4 24.3 %collective-permute-start.22 = (bf16[512,1024]{1,0:T(8,128)(2,1)S(1)}, bf16[512,1024]{1,0:T(8,128)(2,1)S(1)}, u32[]{:S(2)}, u32[]{:S(2)}) collective-permute-start(bf16[512,1024]{1,0:T(8,128)(2,1)S(1)} %add_convert_fusion.3.refs_0_), channel_id=1, source_target_pairs={{0,1},{1,0},{2,3},{3,2},{4,5},{5,4},{6,7},{7,6},{8,9},{9,8},{10,11... | collective-permute-start | bytes 3145736 | tf_op jit(solution)/shard_map/ppermute | solution.py:37
  240.7 2.7 collective-permute-start.24
  252.6 2.2 copy-start.8
  254.8 2.0 copy-start.9
  290.6 3.4 %copy-start.2 = (bf16[1024,4096]{1,0:T(8,128)(2,1)S(1)}, bf16[1024,4096]{1,0:T(8,128)(2,1)}, u32[]{:S(2)}) copy-start(bf16[1024,4096]{1,0:T(8,128)(2,1)} %w_ref.31) | copy-start | bytes 25165828
  295.7 4.0 %collective-permute-start.27 = (bf16[512,1024]{1,0:T(8,128)(2,1)S(1)}, bf16[512,1024]{1,0:T(8,128)(2,1)S(1)}, u32[]{:S(2)}, u32[]{:S(2)}) collective-permute-start(bf16[512,1024]{1,0:T(8,128)(2,1)S(1)} %project_block.15), channel_id=1, source_target_pairs={{0,1},{1,0},{2,3},{3,2},{4,5},{5,4},{6,7},{7,6},{8,9},{9,8},{10,11... | collective-permute-start | bytes 3145736 | tf_op jit(solution)/shard_map/ppermute | solution.py:37
  295.9 4.9 %slice-start.2 = ((s8[8388608]{0:T(1024)(128)(4,1)}), s8[4194304]{0:T(1024)(128)(4,1)S(1)}, s32[]{:S(2)}) async-start(s8[8388608]{0:T(1024)(128)(4,1)} %bitcast.28), calls=%async_computation.4 | async-start | bytes 8388608
  297.6 3.2 slice-start.3
  297.6 4.9 %collective-permute-start.26 = (bf16[512,1024]{1,0:T(8,128)(2,1)S(1)}, bf16[512,1024]{1,0:T(8,128)(2,1)S(1)}, u32[]{:S(2)}, u32[]{:S(2)}) collective-permute-start(bf16[512,1024]{1,0:T(8,128)(2,1)S(1)} %project_block.13), channel_id=1, source_target_pairs={{0,1},{1,0},{2,3},{3,2},{4,5},{5,4},{6,7},{7,6},{8,9},{9,8},{10,11... | collective-permute-start | bytes 3145736 | tf_op jit(solution)/shard_map/ppermute | solution.py:37
  300.2 25.3 %collective-permute-start.28 = (bf16[512,1024]{1,0:T(8,128)(2,1)S(1)}, bf16[512,1024]{1,0:T(8,128)(2,1)S(1)}, u32[]{:S(2)}, u32[]{:S(2)}) collective-permute-start(bf16[512,1024]{1,0:T(8,128)(2,1)S(1)} %add_convert_fusion.1), channel_id=1, source_target_pairs={{0,2},{1,3},{2,0},{3,1},{4,6},{5,7},{6,4},{7,5},{8,10},{9,11},{10,... | collective-permute-start | bytes 3145736 | tf_op jit(solution)/shard_map/ppermute | solution.py:37
Sparse Core Ops, SparseCore 0:
  161.7 35.0 all-gather.1

commit v2 on v1

--- a/solution.py
+++ b/solution.py
@@ -25,6 +25,10 @@
 
 def cost(flops, moved, exps=0):
     return pl.CostEstimate(flops=int(flops), bytes_accessed=int(moved), transcendentals=int(exps))
+
+
+def in_hbm(weight):
+    return pltpu.with_memory_space_constraint(weight, pltpu.HBM)
 
 
 def from_behind(block, axis, distance):
@@ -125,7 +129,7 @@
         compiler_params=params(24),
         cost_estimate=cost(2 * rows * depth * width, 2 * depth * (rows + width)),
         name="project",
-    )(x, w)
+    )(x, in_hbm(w))
 
 
 def block_kernel(place_ref, x_ref, w_ref, out_ref):
@@ -153,7 +157,7 @@
         compiler_params=params(16),
         cost_estimate=cost(2 * rows * depth * width, 2 * depth * (rows + width)),
         name="project_block",
-    )(place.reshape(1), x, w)
+    )(place.reshape(1), x, in_hbm(w))
 
 
 def project_scattered(x, w):
@@ -264,7 +268,7 @@
     )(flag, *[x for _, x in ins])
 
 
-def self_attention(normed, w_query, w_key, w_value):
+def self_attention(normed, w_query, w_key, w_value, neighbours, w_cross_kv):
     rows = normed.shape[0]
     assert lax.axis_size("ctx") == 4
     ctx = lax.axis_index("ctx")
@@ -280,6 +284,9 @@
         k0 = lax.ppermute(k, "ctx", [(0, 1), (2, 3)])
         v = project(normed, w_value, first, width, flip=True)
         v0 = lax.ppermute(v, "ctx", [(0, 1), (2, 3)])
+        if first == 0:
+            qa, neighbours = lax.optimization_barrier((qa, neighbours))
+            fetched = lax.all_gather(neighbours, "mp", axis=1, tiled=True)
         keys = [("rows", k0), ("flat", v0), ("rows", k), ("flat", v)]
         oa, la, ob, lb = head_call(
             far_kernel, "far_attention", flag, rows, heads,
@@ -291,13 +298,15 @@
             near_kernel, "near_attention", flag, rows, heads,
             [("rows", q)] + keys, ["flat", "log"], 2 * rows * rows,
         )
+        if first == 0:
+            kv, far_a = lax.optimization_barrier((neighbour_kv(fetched, w_cross_kv), far_a))
         far_o, far_l = [jnp.where(ctx == 3, b, a) for a, b in zip(far_a, far_b)]
         (out,) = head_call(
             merge_kernel, "merge", flag, rows, heads,
             [("flat", o), ("log", l), ("flat", far_o), ("log", far_l)], ["rows"], rows,
         )
         merged.append(out)
-    return jnp.concatenate(merged, axis=1)
+    return jnp.concatenate(merged, axis=1), kv
 
 
 def fetch_neighbours(encoded, owners, slots):
@@ -324,7 +333,7 @@
     arrived = incoming.reshape((group_count * capacity,) + encoded.shape[1:])[arrival]
     earlier = from_behind(arrived[-NB_PER:], "ctx", 1)
     extended = jnp.concatenate([earlier, arrived], axis=0)
-    return lax.all_gather(extended, "mp", axis=1, tiled=True)
+    return extended
 
 
 def neighbour_kernel(x_ref, w_ref, out_ref):
@@ -350,7 +359,7 @@
         compiler_params=params(32, 2),
         cost_estimate=cost(4 * rows * depth * width, 4 * rows * width + 2 * rows * depth),
         name="neighbour_kv",
-    )(fetched.reshape(rows, depth), w_cross_kv)
+    )(in_hbm(fetched.reshape(rows, depth)), in_hbm(w_cross_kv))
 
 
 def cross_kernel(q_ref, k_ref, v_ref, out_ref):
@@ -359,20 +368,32 @@
     spans = rows // SPAN
     queries = pltpu.roll(q_ref[...].astype(jnp.float32), 1, 0).astype(jnp.bfloat16)
 
-    def one(part, span):
-        keys = k_ref[0, span * named : (span + 1) * named, :]
-        values = v_ref[0, span * named : (span + 1) * named, :]
-        s = lax.dot_general(
-            part, keys, (((1,), (1,)), ((), ())), preferred_element_type=jnp.float32
-        ) * (HEAD**-0.5 * LOG2E)
-        weights = jnp.exp2(s - jnp.max(s, axis=1, keepdims=True))
-        total = jnp.sum(weights, axis=1, keepdims=True)
-        out = jnp.dot(weights.astype(jnp.bfloat16), values, preferred_element_type=jnp.float32)
-        return out / total
-
-    outs = [one(queries[c * SPAN : (c + 1) * SPAN], c) for c in range(spans)]
-    last = one(queries[:16], spans)
-    whole = jnp.concatenate(outs, axis=0)
+    parts = [queries[c * SPAN : (c + 1) * SPAN] for c in range(spans)] + [queries[:16]]
+    scores = jnp.concatenate(
+        [
+            lax.dot_general(
+                part,
+                k_ref[0, c * named : (c + 1) * named, :],
+                (((1,), (1,)), ((), ())),
+                preferred_element_type=jnp.float32,
+            )
+            for c, part in enumerate(parts)
+        ],
+        axis=0,
+    ) * (HEAD**-0.5 * LOG2E)
+    weights = jnp.exp2(scores - jnp.max(scores, axis=1, keepdims=True))
+    totals = jnp.sum(weights, axis=1, keepdims=True)
+    weights = weights.astype(jnp.bfloat16)
+    outs = [
+        jnp.dot(
+            weights[c * SPAN : c * SPAN + part.shape[0]],
+            v_ref[0, c * named : (c + 1) * named, :],
+            preferred_element_type=jnp.float32,
+        )
+        for c, part in enumerate(parts)
+    ]
+    whole = jnp.concatenate(outs, axis=0) / totals
+    last, whole = whole[rows:], whole[:rows]
     last_row = jnp.broadcast_to(last[:1], whole.shape)
     row = lax.broadcasted_iota(jnp.int32, whole.shape, 0)
     whole = jnp.where(row == 0, last_row, whole)
@@ -415,9 +436,8 @@
 ):
     own = tokens[0]
     normed = normalised(gather_blocks(own), norm_gain)
-    fetched = fetch_neighbours(encoded, owners, slots)
-    attended = self_attention(normed, w_query, w_key, w_value)
-    kv = neighbour_kv(fetched, w_cross_kv)
+    neighbours = fetch_neighbours(encoded, owners, slots)
+    attended, kv = self_attention(normed, w_query, w_key, w_value, neighbours, w_cross_kv)
     share = project_scattered(attended, w_out)
     residual = (own.astype(jnp.float32) + share).astype(jnp.bfloat16)
     cross_in = normalised(gather_blocks(residual), cross_gain)

time: 337 us -> 320 us (0.950)
  waiting for transfers between devices: 126 us -> 111 us
  local copies, waits for them, and re-layouts: 31.1 us -> 18.4 us
  Pallas kernels: 112 us -> 119 us
  starting transfers between devices: 40.6 us -> 47.3 us
    ppermute x2, waiting for transfers between devices: 24 us -> 5.36 us  [self_attention(): qa = lax.ppermute(q, 'ctx', [(2, 1)])]
    pallas_call x1, Pallas kernels: 20.9 us -> 7.47 us  [cross_attention(): pl.pallas_call(cross_kernel, grid=(heads,), in_specs=[pl.BlockSpec((rows,...]
    unnamed x44, local copies, waits for them, and re-layouts: 22.8 us -> 11.8 us
    pallas_call x7, Pallas kernels: 25.5 us -> 33.8 us  [project(): pl.pallas_call(functools.partial(project_kernel, flip), grid=(width // ti...]
    pallas_call x8, Pallas kernels: 13.5 us -> 21.8 us  [project_block(): pl.pallas_call(block_kernel, grid_spec=pltpu.PrefetchScalarGridSpec(num_s...]
    ppermute x2, waiting for transfers between devices: 3.13 us -> 7.6 us  [self_attention(): v0 = lax.ppermute(v, 'ctx', [(0, 1), (2, 3)])]
    ppermute x4, waiting for transfers between devices: 5.52 us -> 1.24 us  [self_attention(): far_a = [lax.ppermute(x, 'ctx', [(1, 2)]) for x in (oa, la)]]
    ppermute x12, waiting for transfers between devices: 89.1 us -> 92.7 us  [swap(): lax.ppermute(block, 'mp', [(i, i ^ bit) for i in range(lax.axis_size('mp'...]
  transfers between devices with their start and end apart: 31 -> 31, of which waited for: 11 -> 12; matrix products, arithmetic and copies ran while one was open for 5% -> 2% of each run, Pallas kernels for 23% -> 30%
where the time goes in v2:
time: 320 us; the launch traced here: 318 us
  Pallas kernels  119 us (37%)
  waiting for transfers between devices  111 us (35%)
  starting transfers between devices  47.3 us (15%)
  local copies, waits for them, and re-layouts  18.4 us (6%)
  between operations  14.1 us (4%)
  other arithmetic  7.97 us (2%)
    ppermute x12, waiting for transfers between devices, swap(): lax.ppermute(block, 'mp', [(i, i ^ bit) for i in range(lax.axis_size('mp'...  92.7 us
    pallas_call x6, Pallas kernels, head_call(): pl.pallas_call(kernel, grid_spec=pltpu.PrefetchScalarGridSpec(num_scalar_...  34.4 us
    pallas_call x7, Pallas kernels, project(): pl.pallas_call(functools.partial(project_kernel, flip), grid=(width // ti...  33.8 us
    pallas_call x8, Pallas kernels, project_block(): pl.pallas_call(block_kernel, grid_spec=pltpu.PrefetchScalarGridSpec(num_s...  21.8 us
    pallas_call x1, Pallas kernels, neighbour_kv(): pl.pallas_call(neighbour_kernel, grid=(2, steps), in_specs=[pl.BlockSpec(...  14.8 us
    unnamed x44, local copies, waits for them, and re-layouts  11.8 us
    ppermute x4, starting transfers between devices, self_attention(): far_b = [lax.ppermute(x, 'ctx', [(1, 3)]) for x in (ob, lb)]  10.2 us
    ppermute x4, starting transfers between devices, self_attention(): far_a = [lax.ppermute(x, 'ctx', [(1, 2)]) for x in (oa, la)]  8.41 us
  transfers between devices with their start and end apart: 31, of which 12 were waited for; matrix products, arithmetic and copies ran while one was open for 2% of the time, Pallas kernels for 30%

profile of v2, /device:TPU:12, one launch (start us, length us, event | category | flops | bytes accessed | tf_op | source)
XLA Modules:
  0.0 317.9 jit_solution(9243858160101588735)
XLA Ops:
  8.8 4.1 %gather_fusion = bf16[32,32,896]{2,1,0:T(8,128)(2,1)} fusion(bf16[64,32,896]{2,1,0:T(8,128)(2,1)} %param.23, s32[1024]{0:T(1024)S(1)} %pad_clamp_fusion.1), kind=kCustom, calls=%fused_computation | custom fusion | bytes 3670144 | tf_op jit(solution)/shard_map/gather | solution.py:326
  12.8 6.4 %all-to-all-start = ((bf16[8,4,32,896]{3,2,1,0:T(8,128)(2,1)}), bf16[8,4,32,896]{3,2,1,0:T(8,128)(2,1)}, u32[]{:S(2)}, u32[]{:S(2)}) async-start(bf16[8,4,32,896]{3,2,1,0:T(8,128)(2,1)} %bitcast.33), calls=%async_computation | async-start | bytes 3670016 | tf_op jit(solution)/shard_map/all_to_all | solution.py:327
  19.2 1.6 collective-permute-start.1
  20.8 22.8 %collective-permute-done.1.refs_2_ = bf16[512,1024]{1,0:T(8,128)(2,1)S(1)} collective-permute-done((bf16[512,1024]{1,0:T(8,128)(2,1)S(1)}, bf16[512,1024]{1,0:T(8,128)(2,1)S(1)}, u32[]{:S(2)}, u32[]{:S(2)}) %collective-permute-start.1) | collective-permute-done | bytes 1048608 | tf_op jit(solution)/shard_map/ppermute | solution.py:41
  43.8 2.6 collective-permute-done.2.refs_3_
  46.4 4.2 %norm.2.x_ref = bf16[512,4096]{1,0:T(8,128)(2,1)S(1)} custom-call(s32[4]{0:T(128)S(1)} %iota_xor_fusion.place_ref, f32[1,4096]{1,0:T(1,128)S(1)} %bitcast.31, bf16[512,1024]{1,0:T(8,128)(2,1)S(1)} %bitcast.30, bf16[512,1024]{1,0:T(8,128)(2,1)S(1)} %collective-permute-done.refs_1_, bf16[512,1024]{1,0:T(8,128)(2,1)S(1)} %collective-permute-done.1.refs_2_, ...), custom_call_target="tpu_custom_call" | custom-call | flops 12582912 | bytes 8388608 | tf_op jit(solution)/shard_map/norm/pallas_call | solution.py:89
  50.6 5.7 %project.7.q = bf16[512,512]{1,0:T(8,128)(2,1)S(1)} custom-call(bf16[512,4096]{1,0:T(8,128)(2,1)S(1)} %norm.2.x_ref, bf16[4096,1024]{1,0:T(8,128)(2,1)} %w_ref.20), custom_call_target="tpu_custom_call" | custom-call | flops 2147483648 | bytes 8388608 | tf_op jit(solution)/shard_map/project/pallas_call | solution.py:120
  56.2 1.3 collective-permute-start.5
  58.6 2.2 gather_fusion.1
  60.8 4.4 %collective-permute-start.6 = (bf16[2,32,896]{2,1,0:T(8,128)(2,1)S(1)}, bf16[2,32,896]{2,1,0:T(8,128)(2,1)S(1)}, u32[]{:S(2)}, u32[]{:S(2)}) collective-permute-start(bf16[2,32,896]{2,1,0:T(8,128)(2,1)S(1)} %slice.8), channel_id=1, source_target_pairs={{0,4},{4,8},{8,12},{1,5},{5,9},{9,13},{2,6},{6,10},{10,14},{3,7},{... | collective-permute-start | bytes 344072 | tf_op jit(solution)/shard_map/ppermute | solution.py:37
  65.2 2.9 collective-permute-done.6
  68.1 1.1 pad_maximum_fusion.1
  69.2 2.9 collective-permute-done.5.qa
  72.1 2.4 copy-done.1
  74.5 4.1 %project.10.q = bf16[512,512]{1,0:T(8,128)(2,1)S(1)} custom-call(bf16[512,4096]{1,0:T(8,128)(2,1)S(1)} %copy-done.1, bf16[4096,1024]{1,0:T(8,128)(2,1)} %w_ref.20), custom_call_target="tpu_custom_call" | custom-call | flops 2147483648 | bytes 8388608 | tf_op jit(solution)/shard_map/project/pallas_call | solution.py:120
  78.7 1.3 collective-permute-start.15
  80.0 1.3 collective-permute-start.14
  81.3 4.2 %project.11.k1 = bf16[512,512]{1,0:T(8,128)(2,1)S(1)} custom-call(bf16[512,4096]{1,0:T(8,128)(2,1)S(1)} %copy-done.1, bf16[4096,1024]{1,0:T(8,128)(2,1)} %w_ref.21), custom_call_target="tpu_custom_call" | custom-call | flops 2147483648 | bytes 8388608 | tf_op jit(solution)/shard_map/project/pallas_call | solution.py:120
  85.4 1.3 collective-permute-start.12
  86.7 4.3 %project.12.v1 = bf16[512,512]{1,0:T(8,128)(2,1)S(1)} custom-call(bf16[512,4096]{1,0:T(8,128)(2,1)S(1)} %copy-done.1, bf16[4096,1024]{1,0:T(8,128)(2,1)} %w_ref.22), custom_call_target="tpu_custom_call" | custom-call | flops 2147483648 | bytes 8388608 | tf_op jit(solution)/shard_map/project/pallas_call | solution.py:120
  91.0 1.3 collective-permute-start.13
  92.3 4.1 %project.8.k1 = bf16[512,512]{1,0:T(8,128)(2,1)S(1)} custom-call(bf16[512,4096]{1,0:T(8,128)(2,1)S(1)} %copy-done.1, bf16[4096,1024]{1,0:T(8,128)(2,1)} %w_ref.21), custom_call_target="tpu_custom_call" | custom-call | flops 2147483648 | bytes 8388608 | tf_op jit(solution)/shard_map/project/pallas_call | solution.py:120
  96.5 1.3 collective-permute-start.3
  97.8 4.3 %project.9.v1 = bf16[512,512]{1,0:T(8,128)(2,1)S(1)} custom-call(bf16[512,4096]{1,0:T(8,128)(2,1)S(1)} %copy-done.1, bf16[4096,1024]{1,0:T(8,128)(2,1)} %w_ref.22), custom_call_target="tpu_custom_call" | custom-call | flops 2147483648 | bytes 8388608 | tf_op jit(solution)/shard_map/project/pallas_call | solution.py:120
  102.1 1.3 collective-permute-start.4
  103.4 2.5 collective-permute-done.14.qa
  105.8 7.6 %collective-permute-done.13.v0 = bf16[512,512]{1,0:T(8,128)(2,1)S(1)} collective-permute-done((bf16[512,512]{1,0:T(8,128)(2,1)S(1)}, bf16[512,512]{1,0:T(8,128)(2,1)S(1)}, u32[]{:S(2)}, u32[]{:S(2)}) %collective-permute-start.13) | collective-permute-done | bytes 524320 | tf_op jit(solution)/shard_map/ppermute | solution.py:286
  113.4 10.7 %far_attention.3 = (bf16[512,512]{1,0:T(8,128)(2,1)}, f32[4,1,512]{2,1,0:T(1,128)S(1)}, bf16[512,512]{1,0:T(8,128)(2,1)}, f32[4,1,512]{2,1,0:T(1,128)S(1)}) custom-call(s32[1]{0:T(128)} %bitcast.2.flag_ref, bf16[512,512]{1,0:T(8,128)(2,1)S(1)} %collective-permute-done.14.qa, bf16[512,512]{1,0:T(8,128)(2,1)S(1)} %collective-permute-done.15.qb, ...), custom_call_target="tpu_custom_call" | custom-call | flops 2147483648 | bytes 3145728 | tf_op jit(solution)/shard_map/far_attention/pallas_call | solution.py:254
  124.2 2.1 collective-permute-start.16
  126.2 2.1 collective-permute-start.17
  128.3 1.5 collective-permute-start.7
  133.9 5.1 %near_attention.3 = (bf16[512,512]{1,0:T(8,128)(2,1)S(1)}, f32[4,1,512]{2,1,0:T(1,128)S(1)}) custom-call(s32[1]{0:T(128)} %bitcast.2.flag_ref, bf16[512,512]{1,0:T(8,128)(2,1)S(1)} %project.10.q, bf16[512,512]{1,0:T(8,128)(2,1)S(1)} %copy-done.15, bf16[512,512]{1,0:T(8,128)(2,1)S(1)} %copy-done.17, bf16[512,512]{1,0:T(8,128)(2,1)S(1)} %copy-done.5, ...), custom_call_target="tpu_custom_call" | custom-call | flops 1073741824 | bytes 2621440 | tf_op jit(solution)/shard_map/near_attention/pallas_call | solution.py:254
  139.1 5.5 %collective-permute-start.18 = (f32[4,1,512]{2,1,0:T(1,128)S(1)}, f32[4,1,512]{2,1,0:T(1,128)S(1)}, u32[]{:S(2)}, u32[]{:S(2)}) collective-permute-start(f32[4,1,512]{2,1,0:T(1,128)S(1)} %get-tuple-element.36), channel_id=1, source_target_pairs={{4,12},{5,13},{6,14},{7,15},{20,28},{21,29},{22,30},{23,31}} | collective-permute-start | bytes 24584 | tf_op jit(solution)/shard_map/ppermute | solution.py:296
  144.6 3.7 %collective-permute-start.19 = (f32[4,1,512]{2,1,0:T(1,128)S(1)}, f32[4,1,512]{2,1,0:T(1,128)S(1)}, u32[]{:S(2)}, u32[]{:S(2)}) collective-permute-start(f32[4,1,512]{2,1,0:T(1,128)S(1)} %get-tuple-element.37), channel_id=1, source_target_pairs={{4,8},{5,9},{6,10},{7,11},{20,24},{21,25},{22,26},{23,27}} | collective-permute-start | bytes 24584 | tf_op jit(solution)/shard_map/ppermute | solution.py:295
  148.3 5.9 %near_attention.2 = (bf16[512,512]{1,0:T(8,128)(2,1)S(1)}, f32[4,1,512]{2,1,0:T(1,128)S(1)}) custom-call(s32[1]{0:T(128)} %bitcast.2.flag_ref, bf16[512,512]{1,0:T(8,128)(2,1)S(1)} %project.7.q, bf16[512,512]{1,0:T(8,128)(2,1)} %collective-permute-done.3.k0, bf16[512,512]{1,0:T(8,128)(2,1)} %collective-permute-done.4.v0, bf16[512,512]{1,0:T(8,128)(2,1)S(1)} %project.8.k1, ...), custom_call_target="tpu_custom_call" | custom-call | flops 1073741824 | bytes 2621440 | tf_op jit(solution)/shard_map/near_attention/pallas_call | solution.py:254
  154.3 1.4 broadcast_select_fusion.far_o
  156.3 11.4 %far_attention.2 = (bf16[512,512]{1,0:T(8,128)(2,1)}, f32[4,1,512]{2,1,0:T(1,128)S(1)}, bf16[512,512]{1,0:T(8,128)(2,1)S(1)}, f32[4,1,512]{2,1,0:T(1,128)S(1)}) custom-call(s32[1]{0:T(128)} %bitcast.2.flag_ref, bf16[512,512]{1,0:T(8,128)(2,1)S(1)} %copy-done.13, bf16[512,512]{1,0:T(8,128)(2,1)S(1)} %collective-permute-done.7.qb, ...), custom_call_target="tpu_custom_call" | custom-call | flops 2147483648 | bytes 3145728 | tf_op jit(solution)/shard_map/far_attention/pallas_call | solution.py:254
  167.7 1.3 collective-permute-start.10
  169.0 1.3 collective-permute-start.11
  170.3 1.3 collective-permute-start.8
  171.6 1.3 collective-permute-start.9
  173.0 14.8 %neighbour_kv.1.k_ref.v_ref = bf16[2,2304,1024]{2,1,0:T(8,128)(2,1)S(1)} custom-call(bf16[2304,896]{1,0:T(8,128)(2,1)} %bitcast.34, bf16[2,896,1024]{2,1,0:T(8,128)(2,1)} %w_ref.19), custom_call_target="tpu_custom_call" | custom-call | flops 8455716864 | bytes 13565952 | tf_op jit(solution)/shard_map/neighbour_kv/pallas_call | solution.py:350
  187.8 3.6 %copy-done.2 = bf16[2,2304,1024]{2,1,0:T(8,128)(2,1)} copy-done((bf16[2,2304,1024]{2,1,0:T(8,128)(2,1)}, bf16[2,2304,1024]{2,1,0:T(8,128)(2,1)S(1)}, u32[]{:S(2)}) %copy-start.2) | copy-done | bytes 9437208
  191.5 1.2 collective-permute-done.9
  193.6 2.7 project_block.11
  196.4 2.7 project_block.9
  199.7 2.7 project_block.10
  202.4 1.6 add_convert_fusion.4
  204.1 1.6 collective-permute-start.22
  205.6 2.7 project_block.8
  208.4 20.8 %collective-permute-done.22 = bf16[512,1024]{1,0:T(8,128)(2,1)S(1)} collective-permute-done((bf16[512,1024]{1,0:T(8,128)(2,1)S(1)}, bf16[512,1024]{1,0:T(8,128)(2,1)S(1)}, u32[]{:S(2)}, u32[]{:S(2)}) %collective-permute-start.22) | collective-permute-done | bytes 1048608 | tf_op jit(solution)/shard_map/ppermute | solution.py:41
  230.1 1.6 collective-permute-start.24
  231.7 22.7 %collective-permute-done.24.refs_2_ = bf16[512,1024]{1,0:T(8,128)(2,1)S(1)} collective-permute-done((bf16[512,1024]{1,0:T(8,128)(2,1)S(1)}, bf16[512,1024]{1,0:T(8,128)(2,1)S(1)}, u32[]{:S(2)}, u32[]{:S(2)}) %collective-permute-start.24) | collective-permute-done | bytes 1048608 | tf_op jit(solution)/shard_map/ppermute | solution.py:41
  254.4 2.7 collective-permute-done.25.refs_3_
  257.1 2.8 norm.3.x_ref
  259.9 7.2 %project.13.q_ref = bf16[512,1024]{1,0:T(8,128)(2,1)S(1)} custom-call(bf16[512,4096]{1,0:T(8,128)(2,1)S(1)} %norm.3.x_ref, bf16[4096,1024]{1,0:T(8,128)(2,1)} %w_ref.27), custom_call_target="tpu_custom_call" | custom-call | flops 4294967296 | bytes 12582912 | tf_op jit(solution)/shard_map/project/pallas_call | solution.py:120
  267.2 7.5 %cross_attention.1.x_ref = bf16[512,1024]{1,0:T(8,128)(2,1)S(1)} custom-call(bf16[512,1024]{1,0:T(8,128)(2,1)S(1)} %project.13.q_ref, bf16[2,2304,1024]{2,1,0:T(8,128)(2,1)S(1)} %bitcast.27, bf16[2,2304,1024]{2,1,0:T(8,128)(2,1)S(1)} %bitcast.27), custom_call_target="tpu_custom_call" | custom-call | flops 536870912 | bytes 9437184 | tf_op jit(solution)/shard_map/cross_attention/pallas_call | solution.py:406
  274.7 2.7 project_block.15
  277.6 2.7 project_block.13
  280.8 2.7 project_block.14
  283.9 1.6 collective-permute-start.28
  285.5 2.7 project_block.12
  288.2 21.0 %collective-permute-done.28 = bf16[512,1024]{1,0:T(8,128)(2,1)S(1)} collective-permute-done((bf16[512,1024]{1,0:T(8,128)(2,1)S(1)}, bf16[512,1024]{1,0:T(8,128)(2,1)S(1)}, u32[]{:S(2)}, u32[]{:S(2)}) %collective-permute-start.28) | collective-permute-done | bytes 1048608 | tf_op jit(solution)/shard_map/ppermute | solution.py:41
  309.2 1.9 fusion
  (97 shorter events, 11.8 us)
Async XLA Ops:
  12.8 6.4 %copy-start.3 = (bf16[1,512,1024]{2,1,0:T(8,128)(2,1)S(1)}, bf16[1,512,1024]{2,1,0:T(8,128)(2,1)}, u32[]{:S(2)}) copy-start(bf16[1,512,1024]{2,1,0:T(8,128)(2,1)} %param.13) | copy-start | bytes 3145732
  12.8 33.6 %copy-start.10 = (f32[4096]{0:T(1024)S(1)}, f32[4096]{0:T(1024)}, u32[]{:S(2)}) copy-start(f32[4096]{0:T(1024)} %param.14) | copy-start | bytes 49156
  12.8 45.7 %all-to-all-start = ((bf16[8,4,32,896]{3,2,1,0:T(8,128)(2,1)}), bf16[8,4,32,896]{3,2,1,0:T(8,128)(2,1)}, u32[]{:S(2)}, u32[]{:S(2)}) async-start(bf16[8,4,32,896]{3,2,1,0:T(8,128)(2,1)} %bitcast.33), calls=%async_computation | async-start | bytes 3670016 | tf_op jit(solution)/shard_map/all_to_all | solution.py:327
  19.2 153.8 %all-gather.2.cloned.1.call-start = ((), (), s32[]{:S(2)}) async-start(), calls=%async_computation.1 | async-start | bytes 5160960 | tf_op jit(solution)/shard_map/all_gather | solution.py:289
  19.2 24.4 %collective-permute-start.1 = (bf16[512,1024]{1,0:T(8,128)(2,1)S(1)}, bf16[512,1024]{1,0:T(8,128)(2,1)S(1)}, u32[]{:S(2)}, u32[]{:S(2)}) collective-permute-start(bf16[512,1024]{1,0:T(8,128)(2,1)S(1)} %bitcast.28), channel_id=1, source_target_pairs={{0,2},{1,3},{2,0},{3,1},{4,6},{5,7},{6,4},{7,5},{8,10},{9,11},{10,... | collective-permute-start | bytes 3145736 | tf_op jit(solution)/shard_map/ppermute | solution.py:41
  20.8 23.0 %collective-permute-start = (bf16[512,1024]{1,0:T(8,128)(2,1)S(1)}, bf16[512,1024]{1,0:T(8,128)(2,1)S(1)}, u32[]{:S(2)}, u32[]{:S(2)}) collective-permute-start(bf16[512,1024]{1,0:T(8,128)(2,1)S(1)} %bitcast.29), channel_id=1, source_target_pairs={{0,1},{1,0},{2,3},{3,2},{4,5},{5,4},{6,7},{7,6},{8,9},{9,8},{10,11... | collective-permute-start | bytes 3145736 | tf_op jit(solution)/shard_map/ppermute | solution.py:41
  43.6 2.8 collective-permute-start.2
  50.6 5.7 %copy-start = (bf16[512,4096]{1,0:T(8,128)(2,1)}, bf16[512,4096]{1,0:T(8,128)(2,1)S(1)}, u32[]{:S(2)}) copy-start(bf16[512,4096]{1,0:T(8,128)(2,1)S(1)} %norm.2.x_ref) | copy-start | bytes 12582916
  56.2 15.9 %collective-permute-start.5 = (bf16[512,512]{1,0:T(8,128)(2,1)S(1)}, bf16[512,512]{1,0:T(8,128)(2,1)S(1)}, u32[]{:S(2)}, u32[]{:S(2)}) collective-permute-start(bf16[512,512]{1,0:T(8,128)(2,1)S(1)} %project.7.q), channel_id=1, source_target_pairs={{8,4},{9,5},{10,6},{11,7},{24,20},{25,21},{26,22},{27,23}} | collective-permute-start | bytes 1572872 | tf_op jit(solution)/shard_map/ppermute | solution.py:281
  60.8 7.3 %collective-permute-start.6 = (bf16[2,32,896]{2,1,0:T(8,128)(2,1)S(1)}, bf16[2,32,896]{2,1,0:T(8,128)(2,1)S(1)}, u32[]{:S(2)}, u32[]{:S(2)}) collective-permute-start(bf16[2,32,896]{2,1,0:T(8,128)(2,1)S(1)} %slice.8), channel_id=1, source_target_pairs={{0,4},{4,8},{8,12},{1,5},{5,9},{9,13},{2,6},{6,10},{10,14},{3,7},{... | collective-permute-start | bytes 344072 | tf_op jit(solution)/shard_map/ppermute | solution.py:37
  72.1 6.5 %copy-start.12 = (bf16[512,512]{1,0:T(8,128)(2,1)}, bf16[512,512]{1,0:T(8,128)(2,1)S(1)}, u32[]{:S(2)}) copy-start(bf16[512,512]{1,0:T(8,128)(2,1)S(1)} %collective-permute-done.5.qa) | copy-start | bytes 1572868
  72.1 2.4 copy-start.1
  78.7 23.4 %collective-permute-start.15 = (bf16[512,512]{1,0:T(8,128)(2,1)S(1)}, bf16[512,512]{1,0:T(8,128)(2,1)S(1)}, u32[]{:S(2)}, u32[]{:S(2)}) collective-permute-start(bf16[512,512]{1,0:T(8,128)(2,1)S(1)} %project.10.q), channel_id=1, source_target_pairs={{12,4},{13,5},{14,6},{15,7},{28,20},{29,21},{30,22},{31,23}} | collective-permute-start | bytes 1572872 | tf_op jit(solution)/shard_map/ppermute | solution.py:282
  80.0 25.9 %collective-permute-start.14 = (bf16[512,512]{1,0:T(8,128)(2,1)S(1)}, bf16[512,512]{1,0:T(8,128)(2,1)S(1)}, u32[]{:S(2)}, u32[]{:S(2)}) collective-permute-start(bf16[512,512]{1,0:T(8,128)(2,1)S(1)} %project.10.q), channel_id=1, source_target_pairs={{8,4},{9,5},{10,6},{11,7},{24,20},{25,21},{26,22},{27,23}} | collective-permute-start | bytes 1572872 | tf_op jit(solution)/shard_map/ppermute | solution.py:281
  85.4 28.0 %copy-start.4 = (bf16[512,512]{1,0:T(8,128)(2,1)}, bf16[512,512]{1,0:T(8,128)(2,1)S(1)}, u32[]{:S(2)}) copy-start(bf16[512,512]{1,0:T(8,128)(2,1)S(1)} %project.11.k1) | copy-start | bytes 1572868
  85.4 20.4 %collective-permute-start.12 = (bf16[512,512]{1,0:T(8,128)(2,1)S(1)}, bf16[512,512]{1,0:T(8,128)(2,1)S(1)}, u32[]{:S(2)}, u32[]{:S(2)}) collective-permute-start(bf16[512,512]{1,0:T(8,128)(2,1)S(1)} %project.11.k1), channel_id=1, source_target_pairs={{0,4},{8,12},{1,5},{9,13},{2,6},{10,14},{3,7},{11,15},{16,20},{24,... | collective-permute-start | bytes 1572872 | tf_op jit(solution)/shard_map/ppermute | solution.py:284
  91.0 22.4 %copy-start.6 = (bf16[512,512]{1,0:T(8,128)(2,1)}, bf16[512,512]{1,0:T(8,128)(2,1)S(1)}, u32[]{:S(2)}) copy-start(bf16[512,512]{1,0:T(8,128)(2,1)S(1)} %project.12.v1) | copy-start | bytes 1572868
  91.0 22.4 %collective-permute-start.13 = (bf16[512,512]{1,0:T(8,128)(2,1)S(1)}, bf16[512,512]{1,0:T(8,128)(2,1)S(1)}, u32[]{:S(2)}, u32[]{:S(2)}) collective-permute-start(bf16[512,512]{1,0:T(8,128)(2,1)S(1)} %project.12.v1), channel_id=1, source_target_pairs={{0,4},{8,12},{1,5},{9,13},{2,6},{10,14},{3,7},{11,15},{16,20},{24,... | collective-permute-start | bytes 1572872 | tf_op jit(solution)/shard_map/ppermute | solution.py:286
  96.5 42.6 %collective-permute-start.3 = (bf16[512,512]{1,0:T(8,128)(2,1)S(1)}, bf16[512,512]{1,0:T(8,128)(2,1)}, u32[]{:S(2)}, u32[]{:S(2)}) collective-permute-start(bf16[512,512]{1,0:T(8,128)(2,1)S(1)} %project.8.k1), channel_id=1, source_target_pairs={{0,4},{8,12},{1,5},{9,13},{2,6},{10,14},{3,7},{11,15},{16,20},{24,... | collective-permute-start | bytes 1572872 | tf_op jit(solution)/shard_map/ppermute | solution.py:284
  102.1 42.5 %collective-permute-start.4 = (bf16[512,512]{1,0:T(8,128)(2,1)S(1)}, bf16[512,512]{1,0:T(8,128)(2,1)}, u32[]{:S(2)}, u32[]{:S(2)}) collective-permute-start(bf16[512,512]{1,0:T(8,128)(2,1)S(1)} %project.9.v1), channel_id=1, source_target_pairs={{0,4},{8,12},{1,5},{9,13},{2,6},{10,14},{3,7},{11,15},{16,20},{24,... | collective-permute-start | bytes 1572872 | tf_op jit(solution)/shard_map/ppermute | solution.py:286
  105.8 18.3 %copy-start.14 = (bf16[512,512]{1,0:T(8,128)(2,1)}, bf16[512,512]{1,0:T(8,128)(2,1)S(1)}, u32[]{:S(2)}) copy-start(bf16[512,512]{1,0:T(8,128)(2,1)S(1)} %collective-permute-done.12.k0) | copy-start | bytes 1572868
  113.4 10.7 %copy-start.16 = (bf16[512,512]{1,0:T(8,128)(2,1)}, bf16[512,512]{1,0:T(8,128)(2,1)S(1)}, u32[]{:S(2)}) copy-start(bf16[512,512]{1,0:T(8,128)(2,1)S(1)} %collective-permute-done.13.v0) | copy-start | bytes 1572868
  124.2 30.1 %collective-permute-start.16 = (bf16[512,512]{1,0:T(8,128)(2,1)}, bf16[512,512]{1,0:T(8,128)(2,1)}, u32[]{:S(2)}, u32[]{:S(2)}) collective-permute-start(bf16[512,512]{1,0:T(8,128)(2,1)} %get-tuple-element.34), channel_id=1, source_target_pairs={{4,12},{5,13},{6,14},{7,15},{20,28},{21,29},{22,30},{23,31}} | collective-permute-start | bytes 1572872 | tf_op jit(solution)/shard_map/ppermute | solution.py:296
  126.2 28.1 %collective-permute-start.17 = (bf16[512,512]{1,0:T(8,128)(2,1)}, bf16[512,512]{1,0:T(8,128)(2,1)}, u32[]{:S(2)}, u32[]{:S(2)}) collective-permute-start(bf16[512,512]{1,0:T(8,128)(2,1)} %get-tuple-element.35), channel_id=1, source_target_pairs={{4,8},{5,9},{6,10},{7,11},{20,24},{21,25},{22,26},{23,27}} | collective-permute-start | bytes 1572872 | tf_op jit(solution)/shard_map/ppermute | solution.py:295
  128.3 28.0 %collective-permute-start.7 = (bf16[512,512]{1,0:T(8,128)(2,1)S(1)}, bf16[512,512]{1,0:T(8,128)(2,1)S(1)}, u32[]{:S(2)}, u32[]{:S(2)}) collective-permute-start(bf16[512,512]{1,0:T(8,128)(2,1)S(1)} %project.7.q), channel_id=1, source_target_pairs={{12,4},{13,5},{14,6},{15,7},{28,20},{29,21},{30,22},{31,23}} | collective-permute-start | bytes 1572872 | tf_op jit(solution)/shard_map/ppermute | solution.py:282
  129.8 1.0 copy-start.5
  130.8 1.0 copy-start.7
  131.9 1.0 copy-start.15
  132.9 1.0 copy-start.17
  139.1 15.2 %collective-permute-start.18 = (f32[4,1,512]{2,1,0:T(1,128)S(1)}, f32[4,1,512]{2,1,0:T(1,128)S(1)}, u32[]{:S(2)}, u32[]{:S(2)}) collective-permute-start(f32[4,1,512]{2,1,0:T(1,128)S(1)} %get-tuple-element.36), channel_id=1, source_target_pairs={{4,12},{5,13},{6,14},{7,15},{20,28},{21,29},{22,30},{23,31}} | collective-permute-start | bytes 24584 | tf_op jit(solution)/shard_map/ppermute | solution.py:296
  144.6 9.7 %collective-permute-start.19 = (f32[4,1,512]{2,1,0:T(1,128)S(1)}, f32[4,1,512]{2,1,0:T(1,128)S(1)}, u32[]{:S(2)}, u32[]{:S(2)}) collective-permute-start(f32[4,1,512]{2,1,0:T(1,128)S(1)} %get-tuple-element.37), channel_id=1, source_target_pairs={{4,8},{5,9},{6,10},{7,11},{20,24},{21,25},{22,26},{23,27}} | collective-permute-start | bytes 24584 | tf_op jit(solution)/shard_map/ppermute | solution.py:295
  154.2 2.1 copy-start.8
  154.2 2.1 copy-start.13
  167.7 23.7 %collective-permute-start.10 = (f32[4,1,512]{2,1,0:T(1,128)S(1)}, f32[4,1,512]{2,1,0:T(1,128)S(1)}, u32[]{:S(2)}, u32[]{:S(2)}) collective-permute-start(f32[4,1,512]{2,1,0:T(1,128)S(1)} %get-tuple-element.28), channel_id=1, source_target_pairs={{4,8},{5,9},{6,10},{7,11},{20,24},{21,25},{22,26},{23,27}} | collective-permute-start | bytes 24584 | tf_op jit(solution)/shard_map/ppermute | solution.py:295
  169.0 23.8 %collective-permute-start.11 = (f32[4,1,512]{2,1,0:T(1,128)S(1)}, f32[4,1,512]{2,1,0:T(1,128)S(1)}, u32[]{:S(2)}, u32[]{:S(2)}) collective-permute-start(f32[4,1,512]{2,1,0:T(1,128)S(1)} %get-tuple-element.30), channel_id=1, source_target_pairs={{4,12},{5,13},{6,14},{7,15},{20,28},{21,29},{22,30},{23,31}} | collective-permute-start | bytes 24584 | tf_op jit(solution)/shard_map/ppermute | solution.py:296
  170.3 22.4 %collective-permute-start.8 = (bf16[512,512]{1,0:T(8,128)(2,1)S(1)}, bf16[512,512]{1,0:T(8,128)(2,1)S(1)}, u32[]{:S(2)}, u32[]{:S(2)}) collective-permute-start(bf16[512,512]{1,0:T(8,128)(2,1)S(1)} %get-tuple-element.25), channel_id=1, source_target_pairs={{4,12},{5,13},{6,14},{7,15},{20,28},{21,29},{22,30},{23,31}} | collective-permute-start | bytes 1572872 | tf_op jit(solution)/shard_map/ppermute | solution.py:296
  171.6 21.1 %collective-permute-start.9 = (bf16[512,512]{1,0:T(8,128)(2,1)}, bf16[512,512]{1,0:T(8,128)(2,1)S(1)}, u32[]{:S(2)}, u32[]{:S(2)}) collective-permute-start(bf16[512,512]{1,0:T(8,128)(2,1)} %get-tuple-element.27), channel_id=1, source_target_pairs={{4,8},{5,9},{6,10},{7,11},{20,24},{21,25},{22,26},{23,27}} | collective-permute-start | bytes 1572872 | tf_op jit(solution)/shard_map/ppermute | solution.py:295
  173.0 19.8 %copy-start.9 = (bf16[512,512]{1,0:T(8,128)(2,1)S(1)}, bf16[512,512]{1,0:T(8,128)(2,1)}, u32[]{:S(2)}) copy-start(bf16[512,512]{1,0:T(8,128)(2,1)} %copy-done.8) | copy-start | bytes 1572868
  187.8 3.7 %copy-start.2 = (bf16[2,2304,1024]{2,1,0:T(8,128)(2,1)}, bf16[2,2304,1024]{2,1,0:T(8,128)(2,1)S(1)}, u32[]{:S(2)}) copy-start(bf16[2,2304,1024]{2,1,0:T(8,128)(2,1)S(1)} %neighbour_kv.1.k_ref.v_ref) | copy-start | bytes 28311556
  196.3 6.1 %collective-permute-start.21 = (bf16[512,1024]{1,0:T(8,128)(2,1)S(1)}, bf16[512,1024]{1,0:T(8,128)(2,1)}, u32[]{:S(2)}, u32[]{:S(2)}) collective-permute-start(bf16[512,1024]{1,0:T(8,128)(2,1)S(1)} %project_block.11), channel_id=1, source_target_pairs={{0,1},{1,0},{2,3},{3,2},{4,5},{5,4},{6,7},{7,6},{8,9},{9,8},{10,11... | collective-permute-start | bytes 3145736 | tf_op jit(solution)/shard_map/ppermute | solution.py:41
  199.1 9.2 %collective-permute-start.20 = (bf16[512,1024]{1,0:T(8,128)(2,1)S(1)}, bf16[512,1024]{1,0:T(8,128)(2,1)S(1)}, u32[]{:S(2)}, u32[]{:S(2)}) collective-permute-start(bf16[512,1024]{1,0:T(8,128)(2,1)S(1)} %project_block.9), channel_id=1, source_target_pairs={{0,1},{1,0},{2,3},{3,2},{4,5},{5,4},{6,7},{7,6},{8,9},{9,8},{10,11... | collective-permute-start | bytes 3145736 | tf_op jit(solution)/shard_map/ppermute | solution.py:41
  204.1 25.2 %collective-permute-start.22 = (bf16[512,1024]{1,0:T(8,128)(2,1)S(1)}, bf16[512,1024]{1,0:T(8,128)(2,1)S(1)}, u32[]{:S(2)}, u32[]{:S(2)}) collective-permute-start(bf16[512,1024]{1,0:T(8,128)(2,1)S(1)} %add_convert_fusion.4), channel_id=1, source_target_pairs={{0,2},{1,3},{2,0},{3,1},{4,6},{5,7},{6,4},{7,5},{8,10},{9,11},{10,... | collective-permute-start | bytes 3145736 | tf_op jit(solution)/shard_map/ppermute | solution.py:41
  208.3 48.8 %copy-start.11 = (f32[4096]{0:T(1024)S(1)}, f32[4096]{0:T(1024)}, u32[]{:S(2)}) copy-start(f32[4096]{0:T(1024)} %param.15) | copy-start | bytes 49156
  230.1 24.3 %collective-permute-start.24 = (bf16[512,1024]{1,0:T(8,128)(2,1)S(1)}, bf16[512,1024]{1,0:T(8,128)(2,1)S(1)}, u32[]{:S(2)}, u32[]{:S(2)}) collective-permute-start(bf16[512,1024]{1,0:T(8,128)(2,1)S(1)} %add_convert_fusion.3.refs_0_), channel_id=1, source_target_pairs={{0,2},{1,3},{2,0},{3,1},{4,6},{5,7},{6,4},{7,5},{8,10},{9,11},{10,... | collective-permute-start | bytes 3145736 | tf_op jit(solution)/shard_map/ppermute | solution.py:41
  231.7 22.8 %collective-permute-start.23 = (bf16[512,1024]{1,0:T(8,128)(2,1)S(1)}, bf16[512,1024]{1,0:T(8,128)(2,1)S(1)}, u32[]{:S(2)}, u32[]{:S(2)}) collective-permute-start(bf16[512,1024]{1,0:T(8,128)(2,1)S(1)} %add_convert_fusion.3.refs_0_), channel_id=1, source_target_pairs={{0,1},{1,0},{2,3},{3,2},{4,5},{5,4},{6,7},{7,6},{8,9},{9,8},{10,11... | collective-permute-start | bytes 3145736 | tf_op jit(solution)/shard_map/ppermute | solution.py:41
  254.4 2.7 collective-permute-start.25
  257.1 10.0 %slice-start = ((s8[9437184]{0:T(1024)(128)(4,1)}), s8[4194304]{0:T(1024)(128)(4,1)S(1)}, s32[]{:S(2)}) async-start(s8[9437184]{0:T(1024)(128)(4,1)} %bitcast.26), calls=%async_computation.2 | async-start | bytes 8388608
  257.1 10.0 %slice-start.1 = ((s8[9437184]{0:T(1024)(128)(4,1)}), s8[4194304]{0:T(1024)(128)(4,1)S(1)}, s32[]{:S(2)}) async-start(s8[9437184]{0:T(1024)(128)(4,1)} %bitcast.26), calls=%async_computation.3 | async-start | bytes 8388608
  259.9 7.2 %slice-start.2 = ((s8[9437184]{0:T(1024)(128)(4,1)}), s8[1048576]{0:T(1024)(128)(4,1)S(1)}, s32[]{:S(2)}) async-start(s8[9437184]{0:T(1024)(128)(4,1)} %bitcast.26), calls=%async_computation.4 | async-start | bytes 2097152
  277.4 6.1 %collective-permute-start.27 = (bf16[512,1024]{1,0:T(8,128)(2,1)S(1)}, bf16[512,1024]{1,0:T(8,128)(2,1)S(1)}, u32[]{:S(2)}, u32[]{:S(2)}) collective-permute-start(bf16[512,1024]{1,0:T(8,128)(2,1)S(1)} %project_block.15), channel_id=1, source_target_pairs={{0,1},{1,0},{2,3},{3,2},{4,5},{5,4},{6,7},{7,6},{8,9},{9,8},{10,11... | collective-permute-start | bytes 3145736 | tf_op jit(solution)/shard_map/ppermute | solution.py:41
  280.3 7.9 %collective-permute-start.26 = (bf16[512,1024]{1,0:T(8,128)(2,1)S(1)}, bf16[512,1024]{1,0:T(8,128)(2,1)S(1)}, u32[]{:S(2)}, u32[]{:S(2)}) collective-permute-start(bf16[512,1024]{1,0:T(8,128)(2,1)S(1)} %project_block.13), channel_id=1, source_target_pairs={{0,1},{1,0},{2,3},{3,2},{4,5},{5,4},{6,7},{7,6},{8,9},{9,8},{10,11... | collective-permute-start | bytes 3145736 | tf_op jit(solution)/shard_map/ppermute | solution.py:41
  283.9 25.3 %collective-permute-start.28 = (bf16[512,1024]{1,0:T(8,128)(2,1)S(1)}, bf16[512,1024]{1,0:T(8,128)(2,1)S(1)}, u32[]{:S(2)}, u32[]{:S(2)}) collective-permute-start(bf16[512,1024]{1,0:T(8,128)(2,1)S(1)} %add_convert_fusion.1), channel_id=1, source_target_pairs={{0,2},{1,3},{2,0},{3,1},{4,6},{5,7},{6,4},{7,5},{8,10},{9,11},{10,... | collective-permute-start | bytes 3145736 | tf_op jit(solution)/shard_map/ppermute | solution.py:41
Sparse Core Ops, SparseCore 0:
  72.3 33.1 all-gather.1

commit v3 on v2

--- a/solution.py
+++ b/solution.py
@@ -29,12 +29,6 @@
 
 def in_hbm(weight):
     return pltpu.with_memory_space_constraint(weight, pltpu.HBM)
-
-
-def from_behind(block, axis, distance):
-    devices = range(lax.axis_size(axis))
-    route = [(i - distance, i) for i in devices if i - distance in devices]
-    return lax.ppermute(block, axis, route)
 
 
 def swap(block, bit):
@@ -102,34 +96,64 @@
     )(places, gain.reshape(1, features), *blocks)
 
 
-def project_kernel(flip, x_ref, w_ref, out_ref):
-    product = jnp.dot(x_ref[...], w_ref[...], preferred_element_type=jnp.float32)
-    if flip:
-        product = jnp.transpose(product)
-    out_ref[...] = product.astype(jnp.bfloat16)
-
-
-def project(x, w, first, width, flip=False):
+def project_kernel(x_ref, w_ref, out_ref):
+    out_ref[...] = jnp.dot(x_ref[...], w_ref[...], preferred_element_type=jnp.float32).astype(
+        jnp.bfloat16
+    )
+
+
+def project(x, w, first, width):
     rows, depth = x.shape
     tile = min(width, 256)
     base = first // tile
-    if flip:
-        out_spec, out_dims = pl.BlockSpec((tile, rows), lambda j: (j, 0)), (width, rows)
-    else:
-        out_spec, out_dims = pl.BlockSpec((rows, tile), lambda j: (0, j)), (rows, width)
     return pl.pallas_call(
-        functools.partial(project_kernel, flip),
+        project_kernel,
         grid=(width // tile,),
         in_specs=[
             pl.BlockSpec((rows, depth), lambda j: (0, 0)),
             pl.BlockSpec((depth, tile), lambda j: (0, base + j)),
         ],
-        out_specs=out_spec,
-        out_shape=jax.ShapeDtypeStruct(out_dims, jnp.bfloat16),
+        out_specs=pl.BlockSpec((rows, tile), lambda j: (0, j)),
+        out_shape=jax.ShapeDtypeStruct((rows, width), jnp.bfloat16),
         compiler_params=params(24),
         cost_estimate=cost(2 * rows * depth * width, 2 * depth * (rows + width)),
         name="project",
     )(x, in_hbm(w))
+
+
+def pair_kernel(steps, x_ref, wk_ref, wv_ref, out_ref):
+    def write(w_ref):
+        out_ref[...] = jnp.dot(
+            x_ref[...], w_ref[...], preferred_element_type=jnp.float32
+        ).astype(jnp.bfloat16)
+
+    @pl.when(pl.program_id(0) < steps)
+    def _():
+        write(wk_ref)
+
+    @pl.when(pl.program_id(0) >= steps)
+    def _():
+        write(wv_ref)
+
+
+def project_pair(x, w_key, w_value, first, width):
+    rows, depth = x.shape
+    tile = min(width, 256)
+    base, steps = first // tile, width // tile
+    return pl.pallas_call(
+        functools.partial(pair_kernel, steps),
+        grid=(2 * steps,),
+        in_specs=[
+            pl.BlockSpec((rows, depth), lambda j: (0, 0)),
+            pl.BlockSpec((depth, tile), lambda j: (0, base + jnp.minimum(j, steps - 1))),
+            pl.BlockSpec((depth, tile), lambda j: (0, base + jnp.maximum(j - steps, 0))),
+        ],
+        out_specs=pl.BlockSpec((rows, tile), lambda j: (0, j)),
+        out_shape=jax.ShapeDtypeStruct((rows, 2 * width), jnp.bfloat16),
+        compiler_params=params(28),
+        cost_estimate=cost(4 * rows * depth * width, 2 * depth * (rows + 2 * width)),
+        name="project_pair",
+    )(x, in_hbm(w_key), in_hbm(w_value))
 
 
 def block_kernel(place_ref, x_ref, w_ref, out_ref):
@@ -186,17 +210,22 @@
     return out / total, peak + jnp.log2(total)
 
 
+def turned(values):
+    return jnp.transpose(values[...].astype(jnp.float32)).astype(jnp.bfloat16)
+
+
 def far_kernel(flag_ref, qa, qb, k0, v0, k1, v1, oa, la, ob, lb):
     rows = qa.shape[0]
     tile = min(rows, 256)
 
     @pl.when(flag_ref[0] == 1)
     def _():
+        flat0, flat1 = turned(v0), turned(v1)
         for q, o, l in ((qa, oa, la), (qb, ob, lb)):
             for at in range(0, rows, tile):
                 queries = q[at : at + tile, :]
                 out, log = attend(
-                    [(scores_of(k0[...], queries), v0[...]), (scores_of(k1[...], queries), v1[...])]
+                    [(scores_of(k0[...], queries), flat0), (scores_of(k1[...], queries), flat1)]
                 )
                 o[:, at : at + tile] = out.astype(jnp.bfloat16)
                 l[0, :, at : at + tile] = log
@@ -207,6 +236,8 @@
     tile = min(rows, 256)
 
     def run(with_earlier):
+        flat1 = turned(v1)
+        flat0 = turned(v0) if with_earlier else None
         for at in range(0, rows, tile):
             queries = q[at : at + tile, :]
             end = at + tile
@@ -214,9 +245,9 @@
             key_pos = lax.broadcasted_iota(jnp.int32, own.shape, 0)
             query_pos = at + lax.broadcasted_iota(jnp.int32, own.shape, 1)
             own = jnp.where(key_pos <= query_pos, own, -1e30)
-            parts = [(own, v1[:, :end])]
+            parts = [(own, flat1[:, :end])]
             if with_earlier:
-                parts.append((scores_of(k0[...], queries), v0[...]))
+                parts.append((scores_of(k0[...], queries), flat0))
             out, log = attend(parts)
             o[:, at:end] = out.astype(jnp.bfloat16)
             l[0, :, at:end] = log
@@ -248,10 +279,11 @@
 def head_call(kernel, name, flag, rows, heads, ins, outs, work):
     specs = {
         "rows": (pl.BlockSpec((rows, HEAD), lambda h, f: (0, h)), (rows, heads * HEAD), jnp.bfloat16),
+        "values": (pl.BlockSpec((rows, HEAD), lambda h, f: (0, heads + h)), None, None),
         "flat": (pl.BlockSpec((HEAD, rows), lambda h, f: (h, 0)), (heads * HEAD, rows), jnp.bfloat16),
         "log": (pl.BlockSpec((1, 1, rows), lambda h, f: (h, 0, 0)), (heads, 1, rows), jnp.float32),
     }
-    return pl.pallas_call(
+    call = pl.pallas_call(
         kernel,
         grid_spec=pltpu.PrefetchScalarGridSpec(
             num_scalar_prefetch=1,
@@ -265,7 +297,8 @@
             4 * HEAD * work * heads, 2 * rows * HEAD * heads * len(ins), work * heads
         ),
         name=name,
-    )(flag, *[x for _, x in ins])
+    )
+    return list(call(flag, *[x for _, x in ins]))
 
 
 def self_attention(normed, w_query, w_key, w_value, neighbours, w_cross_kv):
@@ -275,32 +308,50 @@
     width = w_query.shape[1] // 2
     heads = width // HEAD
     flag = ctx.reshape(1)
+    q = project(normed, w_query, 0, 2 * width)
+    qa = lax.ppermute(q, "ctx", [(2, 1)])
+    qb = lax.ppermute(q, "ctx", [(3, 1)])
+    normed, q = lax.optimization_barrier((normed, q))
+    halves = []
+    for first in (0, width):
+        pair = project_pair(normed, w_key, w_value, first, width)
+        pair0 = lax.ppermute(pair, "ctx", [(0, 1), (2, 3)])
+        normed, pair = lax.optimization_barrier((normed, pair))
+        halves.append([pair, pair0])
+    incoming, arrival, wanted = neighbours
+    incoming, halves[1][0] = lax.optimization_barrier((incoming, halves[1][0]))
+    arrived = jnp.where((wanted >= 0)[:, None, None], incoming[arrival], jnp.zeros((), incoming.dtype))
+    fetched = lax.all_gather(arrived, "mp", axis=1, tiled=True)
+    arrived, qa = lax.optimization_barrier((arrived, qa))
+    fars = []
+    for part, (pair, pair0) in zip(("rows", "values"), halves):
+        if fars:
+            qa, fars[0][0] = lax.optimization_barrier((qa, fars[0][0]))
+        keys = [("rows", pair0), ("values", pair0), ("rows", pair), ("values", pair)]
+        fars.append(
+            head_call(
+                far_kernel, "far_attention", flag, rows, heads,
+                [(part, qa), (part, qb)] + keys, ["flat", "log"] * 2, 4 * rows * rows,
+            )
+        )
+    fars[1][0], q = lax.optimization_barrier((fars[1][0], q))
+    sent = [
+        [lax.ppermute(x, "ctx", [(1, 2 + at // 2)]) for at, x in enumerate(far)] for far in fars
+    ]
+    nears = []
+    for part, (pair, pair0) in zip(("rows", "values"), halves):
+        keys = [("rows", pair0), ("values", pair0), ("rows", pair), ("values", pair)]
+        nears.append(
+            head_call(
+                near_kernel, "near_attention", flag, rows, heads,
+                [(part, q)] + keys, ["flat", "log"], 2 * rows * rows,
+            )
+        )
+    fetched, nears = lax.optimization_barrier((fetched, nears))
+    kv, nears = lax.optimization_barrier((neighbour_kv(fetched, w_cross_kv), nears))
     merged = []
-    for first in (0, width):
-        q = project(normed, w_query, first, width)
-        qa = lax.ppermute(q, "ctx", [(2, 1)])
-        qb = lax.ppermute(q, "ctx", [(3, 1)])
-        k = project(normed, w_key, first, width)
-        k0 = lax.ppermute(k, "ctx", [(0, 1), (2, 3)])
-        v = project(normed, w_value, first, width, flip=True)
-        v0 = lax.ppermute(v, "ctx", [(0, 1), (2, 3)])
-        if first == 0:
-            qa, neighbours = lax.optimization_barrier((qa, neighbours))
-            fetched = lax.all_gather(neighbours, "mp", axis=1, tiled=True)
-        keys = [("rows", k0), ("flat", v0), ("rows", k), ("flat", v)]
-        oa, la, ob, lb = head_call(
-            far_kernel, "far_attention", flag, rows, heads,
-            [("rows", qa), ("rows", qb)] + keys, ["flat", "log"] * 2, 4 * rows * rows,
-        )
-        far_a = [lax.ppermute(x, "ctx", [(1, 2)]) for x in (oa, la)]
-        far_b = [lax.ppermute(x, "ctx", [(1, 3)]) for x in (ob, lb)]
-        o, l = head_call(
-            near_kernel, "near_attention", flag, rows, heads,
-            [("rows", q)] + keys, ["flat", "log"], 2 * rows * rows,
-        )
-        if first == 0:
-            kv, far_a = lax.optimization_barrier((neighbour_kv(fetched, w_cross_kv), far_a))
-        far_o, far_l = [jnp.where(ctx == 3, b, a) for a, b in zip(far_a, far_b)]
+    for (o, l), (oa, la, ob, lb) in zip(nears, sent):
+        far_o, far_l = jnp.where(ctx == 3, ob, oa), jnp.where(ctx == 3, lb, la)
         (out,) = head_call(
             merge_kernel, "merge", flag, rows, heads,
             [("flat", o), ("log", l), ("flat", far_o), ("log", far_l)], ["rows"], rows,
@@ -313,9 +364,17 @@
     group_count = lax.axis_size(("pool", "ctx"))
     my_group = lax.axis_index(("pool", "ctx"))
     per_group = owners.size // group_count
-    capacity = max(2, 2 * per_group // group_count)
-    owner_table = owners.reshape(group_count, per_group)
-    slot_table = slots.reshape(group_count, per_group)
+    capacity = max(2, 2 * per_group // group_count) + 1
+
+    def with_earlier(table, missing):
+        grouped = table.reshape(-1, lax.axis_size("ctx"), per_group)
+        earlier = jnp.pad(
+            grouped[:, :-1, -NB_PER:], ((0, 0), (1, 0), (0, 0)), constant_values=missing
+        )
+        return jnp.concatenate([earlier, grouped], axis=2).reshape(group_count, -1)
+
+    owner_table = with_earlier(owners, -1)
+    slot_table = with_earlier(slots, 0)
     matched = (owner_table == my_group).astype(jnp.int32)
     order_rank = jnp.cumsum(matched, axis=1) - 1
     slot_index = jnp.arange(capacity, dtype=jnp.int32)
@@ -326,14 +385,11 @@
     outgoing = encoded[source_rows].reshape((group_count, capacity) + encoded.shape[1:])
     incoming = lax.all_to_all(outgoing, ("pool", "ctx"), split_axis=0, concat_axis=0, tiled=True)
     wanted = lax.dynamic_index_in_dim(owner_table, my_group, 0, keepdims=False)
-    positions = jnp.arange(per_group, dtype=jnp.int32)
+    positions = jnp.arange(wanted.shape[0], dtype=jnp.int32)
     same_owner = (wanted[:, None] == wanted[None, :]).astype(jnp.int32)
     before_this = (positions[None, :] < positions[:, None]).astype(jnp.int32)
-    arrival = wanted * capacity + jnp.sum(same_owner * before_this, axis=1)
-    arrived = incoming.reshape((group_count * capacity,) + encoded.shape[1:])[arrival]
-    earlier = from_behind(arrived[-NB_PER:], "ctx", 1)
-    extended = jnp.concatenate([earlier, arrived], axis=0)
-    return extended
+    arrival = jnp.maximum(wanted, 0) * capacity + jnp.sum(same_owner * before_this, axis=1)
+    return incoming.reshape((group_count * capacity,) + encoded.shape[1:]), arrival, wanted
 
 
 def neighbour_kernel(x_ref, w_ref, out_ref):
@@ -435,7 +491,9 @@
     slots,
 ):
     own = tokens[0]
-    normed = normalised(gather_blocks(own), norm_gain)
+    blocks = gather_blocks(own)
+    blocks[1], owners, slots = lax.optimization_barrier((blocks[1], owners, slots))
+    normed = normalised(blocks, norm_gain)
     neighbours = fetch_neighbours(encoded, owners, slots)
     attended, kv = self_attention(normed, w_query, w_key, w_value, neighbours, w_cross_kv)
     share = project_scattered(attended, w_out)

time: 320 us -> 353 us (1.10)
  waiting for transfers between devices: 111 us -> 168 us
  starting transfers between devices: 47.3 us -> 29.6 us
  local copies, waits for them, and re-layouts: 18.4 us -> 14.7 us
    ppermute x2 -> x1, waiting for transfers between devices: 5.36 us -> 44.7 us  [self_attention(): qa = lax.ppermute(q, 'ctx', [(2, 1)])]
    ppermute x13 -> x10, waiting for transfers between devices: 11.8 us -> 27.1 us  [the longest x8 27.1 us: self_attention(): lax.ppermute(x, 'ctx', [(1, 2 + at // 2)])]
    ppermute x13 -> x10, starting transfers between devices: 28.1 us -> 13.2 us  [the longest x8 10.6 us: self_attention(): lax.ppermute(x, 'ctx', [(1, 2 + at // 2)])]
    unnamed x44 -> x22, local copies, waits for them, and re-layouts: 11.8 us -> 4.65 us
    pallas_call x13 -> x10, Pallas kernels: 68.2 us -> 65.6 us  [the longest x6 35.5 us: head_call(): return list(call(flag, *[x for _, x in ins]))]
  transfers between devices with their start and end apart: 31 -> 26, of which waited for: 12 -> 11; matrix products, arithmetic and copies ran while one was open for 2% -> 1% of each run, Pallas kernels for 30% -> 22%
where the time goes in v3:
time: 353 us; the launch traced here: 351 us
  waiting for transfers between devices  168 us (48%)
  Pallas kernels  117 us (33%)
  starting transfers between devices  29.6 us (8%)
  local copies, waits for them, and re-layouts  14.7 us (4%)
  between operations  14 us (4%)
  other arithmetic  8.12 us (2%)
    ppermute x12, waiting for transfers between devices, swap(): lax.ppermute(block, 'mp', [(i, i ^ bit) for i in range(lax.axis_size('mp'...  95.8 us
    ppermute x1, waiting for transfers between devices, self_attention(): qa = lax.ppermute(q, 'ctx', [(2, 1)])  44.7 us
    pallas_call x6, Pallas kernels, head_call(): return list(call(flag, *[x for _, x in ins]))  35.5 us
    ppermute x8, waiting for transfers between devices, self_attention(): lax.ppermute(x, 'ctx', [(1, 2 + at // 2)])  27.1 us
    pallas_call x8, Pallas kernels, project_block(): pl.pallas_call(block_kernel, grid_spec=pltpu.PrefetchScalarGridSpec(num_s...  21.9 us
    pallas_call x2, Pallas kernels, project_pair(): pl.pallas_call(functools.partial(pair_kernel, steps), grid=(2 * steps,),...  15.6 us
    pallas_call x1, Pallas kernels, neighbour_kv(): pl.pallas_call(neighbour_kernel, grid=(2, steps), in_specs=[pl.BlockSpec(...  14.8 us
    pallas_call x2, Pallas kernels, project(): pl.pallas_call(project_kernel, grid=(width // tile,), in_specs=[pl.BlockS...  14.4 us
  transfers between devices with their start and end apart: 26, of which 11 were waited for; matrix products, arithmetic and copies ran while one was open for 1% of the time, Pallas kernels for 22%

profile of v3, /device:TPU:12, one launch (start us, length us, event | category | flops | bytes accessed | tf_op | source)
XLA Modules:
  0.0 350.8 jit_solution(13662143558747825869)
XLA Ops:
  6.5 2.9 collective-permute-done.refs_1_
  9.4 0.8 copy.30
  10.3 0.8 copy.34
  12.1 4.5 %gather_fusion = bf16[40,32,896]{2,1,0:T(8,128)(2,1)} fusion(bf16[64,32,896]{2,1,0:T(8,128)(2,1)} %param.23, s32[1024]{0:T(1024)S(1)} %pad_clamp_fusion.1), kind=kCustom, calls=%fused_computation | custom fusion | bytes 4587680 | tf_op jit(solution)/shard_map/gather | solution.py:385
  16.6 6.4 %all-to-all-start = ((bf16[8,5,32,896]{3,2,1,0:T(8,128)(2,1)}), bf16[8,5,32,896]{3,2,1,0:T(8,128)(2,1)}, u32[]{:S(2)}, u32[]{:S(2)}) async-start(bf16[8,5,32,896]{3,2,1,0:T(8,128)(2,1)} %bitcast.38), calls=%async_computation | async-start | bytes 4587520 | tf_op jit(solution)/shard_map/all_to_all | solution.py:386
  23.0 1.6 collective-permute-start.1
  24.6 23.1 %collective-permute-done.1.refs_2_ = bf16[512,1024]{1,0:T(8,128)(2,1)S(1)} collective-permute-done((bf16[512,1024]{1,0:T(8,128)(2,1)S(1)}, bf16[512,1024]{1,0:T(8,128)(2,1)S(1)}, u32[]{:S(2)}, u32[]{:S(2)}) %collective-permute-start.1) | collective-permute-done | bytes 1048608 | tf_op jit(solution)/shard_map/ppermute | solution.py:35
  47.9 2.6 collective-permute-done.2.refs_3_
  50.5 4.2 %norm.2.x_ref = bf16[512,4096]{1,0:T(8,128)(2,1)S(1)} custom-call(s32[4]{0:T(128)S(1)} %iota_xor_fusion.place_ref, f32[1,4096]{1,0:T(1,128)S(1)} %bitcast.36, bf16[512,1024]{1,0:T(8,128)(2,1)S(1)} %bitcast.35, bf16[512,1024]{1,0:T(8,128)(2,1)S(1)} %collective-permute-done.refs_1_, bf16[512,1024]{1,0:T(8,128)(2,1)S(1)} %collective-permute-done.1.refs_2_, ...), custom_call_target="tpu_custom_call" | custom-call | flops 12582912 | bytes 8388608 | tf_op jit(solution)/shard_map/norm/pallas_call | solution.py:83
  54.7 7.2 %project.2.q = bf16[512,1024]{1,0:T(8,128)(2,1)S(1)} custom-call(bf16[512,4096]{1,0:T(8,128)(2,1)S(1)} %norm.2.x_ref, bf16[4096,1024]{1,0:T(8,128)(2,1)} %w_ref.11), custom_call_target="tpu_custom_call" | custom-call | flops 4294967296 | bytes 12582912 | tf_op jit(solution)/shard_map/project/pallas_call | solution.py:109
  61.8 1.0 copy-done.2
  62.8 7.8 %project_pair.2.k1.v1 = bf16[512,1024]{1,0:T(8,128)(2,1)S(1)} custom-call(bf16[512,4096]{1,0:T(8,128)(2,1)S(1)} %norm.2.x_ref, bf16[4096,1024]{1,0:T(8,128)(2,1)} %wk_ref.3, bf16[4096,1024]{1,0:T(8,128)(2,1)} %wv_ref.3), custom_call_target="tpu_custom_call" | custom-call | flops 4294967296 | bytes 12582912 | tf_op jit(solution)/shard_map/project_pair/pallas_call | solution.py:143
  70.6 7.8 %project_pair.3.k1.v1 = bf16[512,1024]{1,0:T(8,128)(2,1)S(1)} custom-call(bf16[512,4096]{1,0:T(8,128)(2,1)S(1)} %norm.2.x_ref, bf16[4096,1024]{1,0:T(8,128)(2,1)} %wk_ref.3, bf16[4096,1024]{1,0:T(8,128)(2,1)} %wv_ref.3), custom_call_target="tpu_custom_call" | custom-call | flops 4294967296 | bytes 12582912 | tf_op jit(solution)/shard_map/project_pair/pallas_call | solution.py:143
  78.5 3.4 gather_fusion.1
  81.9 2.4 broadcast_select_fusion
  84.3 1.3 collective-permute-start.3
  85.6 1.3 collective-permute-start.5
  86.9 1.3 collective-permute-start.4
  88.2 1.3 collective-permute-start.6
  89.5 44.7 %collective-permute-done.3.qa = bf16[512,1024]{1,0:T(8,128)(2,1)} collective-permute-done((bf16[512,1024]{1,0:T(8,128)(2,1)}, bf16[512,1024]{1,0:T(8,128)(2,1)}, u32[]{:S(2)}, u32[]{:S(2)}) %collective-permute-start.3) | collective-permute-done | bytes 1048608 | tf_op jit(solution)/shard_map/ppermute | solution.py:312
  134.2 11.0 %far_attention.2 = (bf16[512,512]{1,0:T(8,128)(2,1)S(1)}, f32[4,1,512]{2,1,0:T(1,128)S(1)}, bf16[512,512]{1,0:T(8,128)(2,1)S(1)}, f32[4,1,512]{2,1,0:T(1,128)S(1)}) custom-call(s32[1]{0:T(128)} %bitcast.2.flag_ref, bf16[512,1024]{1,0:T(8,128)(2,1)} %collective-permute-done.3.qa, bf16[512,1024]{1,0:T(8,128)(2,1)} %collective-permute-done.4.qb, ...), custom_call_target="tpu_custom_call" | custom-call | flops 2147483648 | bytes 3145728 | tf_op jit(solution)/shard_map/far_attention/pallas_call | solution.py:301
  145.2 11.1 %far_attention.3 = (bf16[512,512]{1,0:T(8,128)(2,1)S(1)}, f32[4,1,512]{2,1,0:T(1,128)S(1)}, bf16[512,512]{1,0:T(8,128)(2,1)S(1)}, f32[4,1,512]{2,1,0:T(1,128)S(1)}) custom-call(s32[1]{0:T(128)} %bitcast.2.flag_ref, bf16[512,1024]{1,0:T(8,128)(2,1)} %collective-permute-done.3.qa, bf16[512,1024]{1,0:T(8,128)(2,1)} %collective-permute-done.4.qb, ...), custom_call_target="tpu_custom_call" | custom-call | flops 2147483648 | bytes 3145728 | tf_op jit(solution)/shard_map/far_attention/pallas_call | solution.py:301
  156.2 1.5 collective-permute-start.13
  157.7 1.3 collective-permute-start.14
  159.0 1.3 collective-permute-start.9
  160.3 1.3 collective-permute-start.12
  161.6 1.3 collective-permute-start.11
  163.0 6.1 %near_attention.3 = (bf16[512,512]{1,0:T(8,128)(2,1)S(1)}, f32[4,1,512]{2,1,0:T(1,128)S(1)}) custom-call(s32[1]{0:T(128)} %bitcast.2.flag_ref, bf16[512,1024]{1,0:T(8,128)(2,1)S(1)} %copy-done.3, bf16[512,1024]{1,0:T(8,128)(2,1)} %collective-permute-done.6.k0.v0, bf16[512,1024]{1,0:T(8,128)(2,1)} %collective-permute-done.6.k0.v0, ...), custom_call_target="tpu_custom_call" | custom-call | flops 1073741824 | bytes 2621440 | tf_op jit(solution)/shard_map/near_attention/pallas_call | solution.py:301
  169.1 6.2 %near_attention.2 = (bf16[512,512]{1,0:T(8,128)(2,1)S(1)}, f32[4,1,512]{2,1,0:T(1,128)S(1)}) custom-call(s32[1]{0:T(128)} %bitcast.2.flag_ref, bf16[512,1024]{1,0:T(8,128)(2,1)S(1)} %copy-done.3, bf16[512,1024]{1,0:T(8,128)(2,1)} %collective-permute-done.5.k0.v0, bf16[512,1024]{1,0:T(8,128)(2,1)} %collective-permute-done.5.k0.v0, ...), custom_call_target="tpu_custom_call" | custom-call | flops 1073741824 | bytes 2621440 | tf_op jit(solution)/shard_map/near_attention/pallas_call | solution.py:301
  175.3 1.3 collective-permute-start.10
  176.7 1.3 collective-permute-start.8
  178.0 1.3 collective-permute-start.7
  179.3 6.0 %collective-permute-done.10 = f32[4,1,512]{2,1,0:T(1,128)S(1)} collective-permute-done((f32[4,1,512]{2,1,0:T(1,128)S(1)}, f32[4,1,512]{2,1,0:T(1,128)S(1)}, u32[]{:S(2)}, u32[]{:S(2)}) %collective-permute-start.10) | collective-permute-done | bytes 8224 | tf_op jit(solution)/shard_map/ppermute | solution.py:339
  185.5 11.1 %collective-permute-done.8 = bf16[512,512]{1,0:T(8,128)(2,1)S(1)} collective-permute-done((bf16[512,512]{1,0:T(8,128)(2,1)S(1)}, bf16[512,512]{1,0:T(8,128)(2,1)S(1)}, u32[]{:S(2)}, u32[]{:S(2)}) %collective-permute-start.8) | collective-permute-done | bytes 524320 | tf_op jit(solution)/shard_map/ppermute | solution.py:339
  196.6 9.9 %collective-permute-done.7 = bf16[512,512]{1,0:T(8,128)(2,1)S(1)} collective-permute-done((bf16[512,512]{1,0:T(8,128)(2,1)S(1)}, bf16[512,512]{1,0:T(8,128)(2,1)S(1)}, u32[]{:S(2)}, u32[]{:S(2)}) %collective-permute-start.7) | collective-permute-done | bytes 524320 | tf_op jit(solution)/shard_map/ppermute | solution.py:339
  206.6 14.8 %neighbour_kv.1.k_ref.v_ref = bf16[2,2304,1024]{2,1,0:T(8,128)(2,1)S(1)} custom-call(bf16[2304,896]{1,0:T(8,128)(2,1)} %bitcast.41, bf16[2,896,1024]{2,1,0:T(8,128)(2,1)} %w_ref.12), custom_call_target="tpu_custom_call" | custom-call | flops 8455716864 | bytes 13565952 | tf_op jit(solution)/shard_map/neighbour_kv/pallas_call | solution.py:406
  221.4 3.6 %copy-done = bf16[2,2304,1024]{2,1,0:T(8,128)(2,1)} copy-done((bf16[2,2304,1024]{2,1,0:T(8,128)(2,1)}, bf16[2,2304,1024]{2,1,0:T(8,128)(2,1)S(1)}, u32[]{:S(2)}) %copy-start) | copy-done | bytes 9437208
  225.1 0.6 merge.3
  225.6 0.6 merge.2
  226.4 2.8 project_block.11
  229.3 2.8 project_block.9
  232.0 0.5 collective-permute-start.15
  232.6 2.7 project_block.10
  235.3 1.5 add_convert_fusion.4
  236.8 1.6 collective-permute-start.17
  238.4 2.7 project_block.8
  241.2 20.8 %collective-permute-done.17 = bf16[512,1024]{1,0:T(8,128)(2,1)S(1)} collective-permute-done((bf16[512,1024]{1,0:T(8,128)(2,1)S(1)}, bf16[512,1024]{1,0:T(8,128)(2,1)S(1)}, u32[]{:S(2)}, u32[]{:S(2)}) %collective-permute-start.17) | collective-permute-done | bytes 1048608 | tf_op jit(solution)/shard_map/ppermute | solution.py:35
  262.0 0.9 add_convert_fusion.3.refs_0_
  262.9 1.6 collective-permute-start.19
  264.5 22.8 %collective-permute-done.19.refs_2_ = bf16[512,1024]{1,0:T(8,128)(2,1)S(1)} collective-permute-done((bf16[512,1024]{1,0:T(8,128)(2,1)S(1)}, bf16[512,1024]{1,0:T(8,128)(2,1)S(1)}, u32[]{:S(2)}, u32[]{:S(2)}) %collective-permute-start.19) | collective-permute-done | bytes 1048608 | tf_op jit(solution)/shard_map/ppermute | solution.py:35
  287.2 2.7 collective-permute-done.20.refs_3_
  289.9 2.8 norm.3.x_ref
  292.7 7.2 %project.3.q_ref = bf16[512,1024]{1,0:T(8,128)(2,1)S(1)} custom-call(bf16[512,4096]{1,0:T(8,128)(2,1)S(1)} %norm.3.x_ref, bf16[4096,1024]{1,0:T(8,128)(2,1)} %w_ref.17), custom_call_target="tpu_custom_call" | custom-call | flops 4294967296 | bytes 12582912 | tf_op jit(solution)/shard_map/project/pallas_call | solution.py:109
  300.0 7.5 %cross_attention.1.x_ref = bf16[512,1024]{1,0:T(8,128)(2,1)S(1)} custom-call(bf16[512,1024]{1,0:T(8,128)(2,1)S(1)} %project.3.q_ref, bf16[2,2304,1024]{2,1,0:T(8,128)(2,1)S(1)} %bitcast.32, bf16[2,2304,1024]{2,1,0:T(8,128)(2,1)S(1)} %bitcast.32), custom_call_target="tpu_custom_call" | custom-call | flops 536870912 | bytes 9437184 | tf_op jit(solution)/shard_map/cross_attention/pallas_call | solution.py:462
  307.5 2.7 project_block.15
  310.2 0.2 collective-permute-start.22
  310.5 2.7 project_block.13
  313.2 0.4 collective-permute-start.21
  313.6 2.7 project_block.14
  316.4 0.4 add_convert_fusion.1
  316.8 1.6 collective-permute-start.23
  318.3 2.7 project_block.12
  321.1 21.0 %collective-permute-done.23 = bf16[512,1024]{1,0:T(8,128)(2,1)S(1)} collective-permute-done((bf16[512,1024]{1,0:T(8,128)(2,1)S(1)}, bf16[512,1024]{1,0:T(8,128)(2,1)S(1)}, u32[]{:S(2)}, u32[]{:S(2)}) %collective-permute-start.23) | collective-permute-done | bytes 1048608 | tf_op jit(solution)/shard_map/ppermute | solution.py:35
  342.0 1.9 fusion
  (70 shorter events, 1.9 us)
Async XLA Ops:
  6.5 2.9 collective-permute-start
  16.6 6.4 %copy-start.1 = (bf16[1,512,1024]{2,1,0:T(8,128)(2,1)S(1)}, bf16[1,512,1024]{2,1,0:T(8,128)(2,1)}, u32[]{:S(2)}) copy-start(bf16[1,512,1024]{2,1,0:T(8,128)(2,1)} %param.13) | copy-start | bytes 3145732
  16.6 33.9 %copy-start.6 = (f32[4096]{0:T(1024)S(1)}, f32[4096]{0:T(1024)}, u32[]{:S(2)}) copy-start(f32[4096]{0:T(1024)} %param.14) | copy-start | bytes 49156
  16.6 61.8 %all-to-all-start = ((bf16[8,5,32,896]{3,2,1,0:T(8,128)(2,1)}), bf16[8,5,32,896]{3,2,1,0:T(8,128)(2,1)}, u32[]{:S(2)}, u32[]{:S(2)}) async-start(bf16[8,5,32,896]{3,2,1,0:T(8,128)(2,1)} %bitcast.38), calls=%async_computation | async-start | bytes 4587520 | tf_op jit(solution)/shard_map/all_to_all | solution.py:386
  23.0 183.6 %all-gather.2.cloned.1.call-start = ((), (), s32[]{:S(2)}) async-start(), calls=%async_computation.1 | async-start | bytes 5160960 | tf_op jit(solution)/shard_map/all_gather | solution.py:324
  23.0 24.7 %collective-permute-start.1 = (bf16[512,1024]{1,0:T(8,128)(2,1)S(1)}, bf16[512,1024]{1,0:T(8,128)(2,1)S(1)}, u32[]{:S(2)}, u32[]{:S(2)}) collective-permute-start(bf16[512,1024]{1,0:T(8,128)(2,1)S(1)} %bitcast.34), channel_id=1, source_target_pairs={{0,2},{1,3},{2,0},{3,1},{4,6},{5,7},{6,4},{7,5},{8,10},{9,11},{10,... | collective-permute-start | bytes 3145736 | tf_op jit(solution)/shard_map/ppermute | solution.py:35
  47.7 2.8 collective-permute-start.2
  61.8 1.0 copy-start.2
  84.3 49.9 %collective-permute-start.3 = (bf16[512,1024]{1,0:T(8,128)(2,1)}, bf16[512,1024]{1,0:T(8,128)(2,1)}, u32[]{:S(2)}, u32[]{:S(2)}) collective-permute-start(bf16[512,1024]{1,0:T(8,128)(2,1)} %copy-done.2), channel_id=1, source_target_pairs={{8,4},{9,5},{10,6},{11,7},{24,20},{25,21},{26,22},{27,23}} | collective-permute-start | bytes 3145736 | tf_op jit(solution)/shard_map/ppermute | solution.py:312
  85.6 48.6 %collective-permute-start.5 = (bf16[512,1024]{1,0:T(8,128)(2,1)S(1)}, bf16[512,1024]{1,0:T(8,128)(2,1)}, u32[]{:S(2)}, u32[]{:S(2)}) collective-permute-start(bf16[512,1024]{1,0:T(8,128)(2,1)S(1)} %project_pair.2.k1.v1), channel_id=1, source_target_pairs={{0,4},{8,12},{1,5},{9,13},{2,6},{10,14},{3,7},{11,15},{16,20},{24,... | collective-permute-start | bytes 3145736 | tf_op jit(solution)/shard_map/ppermute | solution.py:318
  86.9 47.3 %collective-permute-start.4 = (bf16[512,1024]{1,0:T(8,128)(2,1)}, bf16[512,1024]{1,0:T(8,128)(2,1)}, u32[]{:S(2)}, u32[]{:S(2)}) collective-permute-start(bf16[512,1024]{1,0:T(8,128)(2,1)} %copy-done.2), channel_id=1, source_target_pairs={{12,4},{13,5},{14,6},{15,7},{28,20},{29,21},{30,22},{31,23}} | collective-permute-start | bytes 3145736 | tf_op jit(solution)/shard_map/ppermute | solution.py:313
  88.2 57.0 %collective-permute-start.6 = (bf16[512,1024]{1,0:T(8,128)(2,1)S(1)}, bf16[512,1024]{1,0:T(8,128)(2,1)}, u32[]{:S(2)}, u32[]{:S(2)}) collective-permute-start(bf16[512,1024]{1,0:T(8,128)(2,1)S(1)} %project_pair.3.k1.v1), channel_id=1, source_target_pairs={{0,4},{8,12},{1,5},{9,13},{2,6},{10,14},{3,7},{11,15},{16,20},{24,... | collective-permute-start | bytes 3145736 | tf_op jit(solution)/shard_map/ppermute | solution.py:318
  145.2 17.8 %copy-start.3 = (bf16[512,1024]{1,0:T(8,128)(2,1)S(1)}, bf16[512,1024]{1,0:T(8,128)(2,1)}, u32[]{:S(2)}) copy-start(bf16[512,1024]{1,0:T(8,128)(2,1)} %copy-done.2) | copy-start | bytes 3145732
  156.2 19.1 %collective-permute-start.13 = (f32[4,1,512]{2,1,0:T(1,128)S(1)}, f32[4,1,512]{2,1,0:T(1,128)S(1)}, u32[]{:S(2)}, u32[]{:S(2)}) collective-permute-start(f32[4,1,512]{2,1,0:T(1,128)S(1)} %get-tuple-element.76), channel_id=1, source_target_pairs={{4,12},{5,13},{6,14},{7,15},{20,28},{21,29},{22,30},{23,31}} | collective-permute-start | bytes 24584 | tf_op jit(solution)/shard_map/ppermute | solution.py:339
  157.7 18.9 %collective-permute-start.14 = (f32[4,1,512]{2,1,0:T(1,128)S(1)}, f32[4,1,512]{2,1,0:T(1,128)S(1)}, u32[]{:S(2)}, u32[]{:S(2)}) collective-permute-start(f32[4,1,512]{2,1,0:T(1,128)S(1)} %get-tuple-element.77), channel_id=1, source_target_pairs={{4,8},{5,9},{6,10},{7,11},{20,24},{21,25},{22,26},{23,27}} | collective-permute-start | bytes 24584 | tf_op jit(solution)/shard_map/ppermute | solution.py:339
  159.0 19.0 %collective-permute-start.9 = (f32[4,1,512]{2,1,0:T(1,128)S(1)}, f32[4,1,512]{2,1,0:T(1,128)S(1)}, u32[]{:S(2)}, u32[]{:S(2)}) collective-permute-start(f32[4,1,512]{2,1,0:T(1,128)S(1)} %get-tuple-element.70), channel_id=1, source_target_pairs={{4,12},{5,13},{6,14},{7,15},{20,28},{21,29},{22,30},{23,31}} | collective-permute-start | bytes 24584 | tf_op jit(solution)/shard_map/ppermute | solution.py:339
  160.3 25.1 %collective-permute-start.12 = (bf16[512,512]{1,0:T(8,128)(2,1)S(1)}, bf16[512,512]{1,0:T(8,128)(2,1)S(1)}, u32[]{:S(2)}, u32[]{:S(2)}) collective-permute-start(bf16[512,512]{1,0:T(8,128)(2,1)S(1)} %get-tuple-element.75), channel_id=1, source_target_pairs={{4,8},{5,9},{6,10},{7,11},{20,24},{21,25},{22,26},{23,27}} | collective-permute-start | bytes 1572872 | tf_op jit(solution)/shard_map/ppermute | solution.py:339
  161.6 23.7 %collective-permute-start.11 = (bf16[512,512]{1,0:T(8,128)(2,1)S(1)}, bf16[512,512]{1,0:T(8,128)(2,1)S(1)}, u32[]{:S(2)}, u32[]{:S(2)}) collective-permute-start(bf16[512,512]{1,0:T(8,128)(2,1)S(1)} %get-tuple-element.74), channel_id=1, source_target_pairs={{4,12},{5,13},{6,14},{7,15},{20,28},{21,29},{22,30},{23,31}} | collective-permute-start | bytes 1572872 | tf_op jit(solution)/shard_map/ppermute | solution.py:339
  169.1 6.2 %copy-start.4 = (bf16[512,512]{1,0:T(8,128)(2,1)}, bf16[512,512]{1,0:T(8,128)(2,1)S(1)}, u32[]{:S(2)}) copy-start(bf16[512,512]{1,0:T(8,128)(2,1)S(1)} %get-tuple-element.72.o) | copy-start | bytes 1572868
  175.3 10.0 %collective-permute-start.10 = (f32[4,1,512]{2,1,0:T(1,128)S(1)}, f32[4,1,512]{2,1,0:T(1,128)S(1)}, u32[]{:S(2)}, u32[]{:S(2)}) collective-permute-start(f32[4,1,512]{2,1,0:T(1,128)S(1)} %get-tuple-element.71), channel_id=1, source_target_pairs={{4,8},{5,9},{6,10},{7,11},{20,24},{21,25},{22,26},{23,27}} | collective-permute-start | bytes 24584 | tf_op jit(solution)/shard_map/ppermute | solution.py:339
  176.7 19.9 %collective-permute-start.8 = (bf16[512,512]{1,0:T(8,128)(2,1)S(1)}, bf16[512,512]{1,0:T(8,128)(2,1)S(1)}, u32[]{:S(2)}, u32[]{:S(2)}) collective-permute-start(bf16[512,512]{1,0:T(8,128)(2,1)S(1)} %get-tuple-element.69), channel_id=1, source_target_pairs={{4,8},{5,9},{6,10},{7,11},{20,24},{21,25},{22,26},{23,27}} | collective-permute-start | bytes 1572872 | tf_op jit(solution)/shard_map/ppermute | solution.py:339
  178.0 28.5 %collective-permute-start.7 = (bf16[512,512]{1,0:T(8,128)(2,1)S(1)}, bf16[512,512]{1,0:T(8,128)(2,1)S(1)}, u32[]{:S(2)}, u32[]{:S(2)}) collective-permute-start(bf16[512,512]{1,0:T(8,128)(2,1)S(1)} %get-tuple-element.68), channel_id=1, source_target_pairs={{4,12},{5,13},{6,14},{7,15},{20,28},{21,29},{22,30},{23,31}} | collective-permute-start | bytes 1572872 | tf_op jit(solution)/shard_map/ppermute | solution.py:339
  206.6 18.5 %copy-start.5 = (bf16[512,512]{1,0:T(8,128)(2,1)S(1)}, bf16[512,512]{1,0:T(8,128)(2,1)}, u32[]{:S(2)}) copy-start(bf16[512,512]{1,0:T(8,128)(2,1)} %copy-done.4) | copy-start | bytes 1572868
  221.4 3.6 %copy-start = (bf16[2,2304,1024]{2,1,0:T(8,128)(2,1)}, bf16[2,2304,1024]{2,1,0:T(8,128)(2,1)S(1)}, u32[]{:S(2)}) copy-start(bf16[2,2304,1024]{2,1,0:T(8,128)(2,1)S(1)} %neighbour_kv.1.k_ref.v_ref) | copy-start | bytes 28311556
  229.2 6.1 %collective-permute-start.16 = (bf16[512,1024]{1,0:T(8,128)(2,1)S(1)}, bf16[512,1024]{1,0:T(8,128)(2,1)}, u32[]{:S(2)}, u32[]{:S(2)}) collective-permute-start(bf16[512,1024]{1,0:T(8,128)(2,1)S(1)} %project_block.11), channel_id=1, source_target_pairs={{0,1},{1,0},{2,3},{3,2},{4,5},{5,4},{6,7},{7,6},{8,9},{9,8},{10,11... | collective-permute-start | bytes 3145736 | tf_op jit(solution)/shard_map/ppermute | solution.py:35
  232.0 9.1 %collective-permute-start.15 = (bf16[512,1024]{1,0:T(8,128)(2,1)S(1)}, bf16[512,1024]{1,0:T(8,128)(2,1)S(1)}, u32[]{:S(2)}, u32[]{:S(2)}) collective-permute-start(bf16[512,1024]{1,0:T(8,128)(2,1)S(1)} %project_block.9), channel_id=1, source_target_pairs={{0,1},{1,0},{2,3},{3,2},{4,5},{5,4},{6,7},{7,6},{8,9},{9,8},{10,11... | collective-permute-start | bytes 3145736 | tf_op jit(solution)/shard_map/ppermute | solution.py:35
  236.8 25.2 %collective-permute-start.17 = (bf16[512,1024]{1,0:T(8,128)(2,1)S(1)}, bf16[512,1024]{1,0:T(8,128)(2,1)S(1)}, u32[]{:S(2)}, u32[]{:S(2)}) collective-permute-start(bf16[512,1024]{1,0:T(8,128)(2,1)S(1)} %add_convert_fusion.4), channel_id=1, source_target_pairs={{0,2},{1,3},{2,0},{3,1},{4,6},{5,7},{6,4},{7,5},{8,10},{9,11},{10,... | collective-permute-start | bytes 3145736 | tf_op jit(solution)/shard_map/ppermute | solution.py:35
  241.2 48.7 %copy-start.7 = (f32[4096]{0:T(1024)S(1)}, f32[4096]{0:T(1024)}, u32[]{:S(2)}) copy-start(f32[4096]{0:T(1024)} %param.15) | copy-start | bytes 49156
  262.9 24.3 %collective-permute-start.19 = (bf16[512,1024]{1,0:T(8,128)(2,1)S(1)}, bf16[512,1024]{1,0:T(8,128)(2,1)S(1)}, u32[]{:S(2)}, u32[]{:S(2)}) collective-permute-start(bf16[512,1024]{1,0:T(8,128)(2,1)S(1)} %add_convert_fusion.3.refs_0_), channel_id=1, source_target_pairs={{0,2},{1,3},{2,0},{3,1},{4,6},{5,7},{6,4},{7,5},{8,10},{9,11},{10,... | collective-permute-start | bytes 3145736 | tf_op jit(solution)/shard_map/ppermute | solution.py:35
  264.5 22.8 %collective-permute-start.18 = (bf16[512,1024]{1,0:T(8,128)(2,1)S(1)}, bf16[512,1024]{1,0:T(8,128)(2,1)S(1)}, u32[]{:S(2)}, u32[]{:S(2)}) collective-permute-start(bf16[512,1024]{1,0:T(8,128)(2,1)S(1)} %add_convert_fusion.3.refs_0_), channel_id=1, source_target_pairs={{0,1},{1,0},{2,3},{3,2},{4,5},{5,4},{6,7},{7,6},{8,9},{9,8},{10,11... | collective-permute-start | bytes 3145736 | tf_op jit(solution)/shard_map/ppermute | solution.py:35
  287.2 2.7 collective-permute-start.20
  289.9 10.1 %slice-start = ((s8[9437184]{0:T(1024)(128)(4,1)}), s8[4194304]{0:T(1024)(128)(4,1)S(1)}, s32[]{:S(2)}) async-start(s8[9437184]{0:T(1024)(128)(4,1)} %bitcast.31), calls=%async_computation.2 | async-start | bytes 8388608
  289.9 10.1 %slice-start.1 = ((s8[9437184]{0:T(1024)(128)(4,1)}), s8[4194304]{0:T(1024)(128)(4,1)S(1)}, s32[]{:S(2)}) async-start(s8[9437184]{0:T(1024)(128)(4,1)} %bitcast.31), calls=%async_computation.3 | async-start | bytes 8388608
  292.7 7.3 %slice-start.2 = ((s8[9437184]{0:T(1024)(128)(4,1)}), s8[1048576]{0:T(1024)(128)(4,1)S(1)}, s32[]{:S(2)}) async-start(s8[9437184]{0:T(1024)(128)(4,1)} %bitcast.31), calls=%async_computation.4 | async-start | bytes 2097152
  310.2 6.1 %collective-permute-start.22 = (bf16[512,1024]{1,0:T(8,128)(2,1)S(1)}, bf16[512,1024]{1,0:T(8,128)(2,1)S(1)}, u32[]{:S(2)}, u32[]{:S(2)}) collective-permute-start(bf16[512,1024]{1,0:T(8,128)(2,1)S(1)} %project_block.15), channel_id=1, source_target_pairs={{0,1},{1,0},{2,3},{3,2},{4,5},{5,4},{6,7},{7,6},{8,9},{9,8},{10,11... | collective-permute-start | bytes 3145736 | tf_op jit(solution)/shard_map/ppermute | solution.py:35
  313.2 7.9 %collective-permute-start.21 = (bf16[512,1024]{1,0:T(8,128)(2,1)S(1)}, bf16[512,1024]{1,0:T(8,128)(2,1)S(1)}, u32[]{:S(2)}, u32[]{:S(2)}) collective-permute-start(bf16[512,1024]{1,0:T(8,128)(2,1)S(1)} %project_block.13), channel_id=1, source_target_pairs={{0,1},{1,0},{2,3},{3,2},{4,5},{5,4},{6,7},{7,6},{8,9},{9,8},{10,11... | collective-permute-start | bytes 3145736 | tf_op jit(solution)/shard_map/ppermute | solution.py:35
  316.8 25.3 %collective-permute-start.23 = (bf16[512,1024]{1,0:T(8,128)(2,1)S(1)}, bf16[512,1024]{1,0:T(8,128)(2,1)S(1)}, u32[]{:S(2)}, u32[]{:S(2)}) collective-permute-start(bf16[512,1024]{1,0:T(8,128)(2,1)S(1)} %add_convert_fusion.1), channel_id=1, source_target_pairs={{0,2},{1,3},{2,0},{3,1},{4,6},{5,7},{6,4},{7,5},{8,10},{9,11},{10,... | collective-permute-start | bytes 3145736 | tf_op jit(solution)/shard_map/ppermute | solution.py:35
Sparse Core Ops, SparseCore 0:
  84.4 34.9 all-gather.1

commit v4 on v2

--- a/solution.py
+++ b/solution.py
@@ -13,6 +13,7 @@
 NB_PER = 2
 MIB = 1 << 20
 LOG2E = 1.4426950408889634
+EXTRA = 16
 
 norm_eps = 1e-05
 
@@ -29,12 +30,6 @@
 
 def in_hbm(weight):
     return pltpu.with_memory_space_constraint(weight, pltpu.HBM)
-
-
-def from_behind(block, axis, distance):
-    devices = range(lax.axis_size(axis))
-    route = [(i - distance, i) for i in devices if i - distance in devices]
-    return lax.ppermute(block, axis, route)
 
 
 def swap(block, bit):
@@ -165,8 +160,9 @@
     width = w.shape[1] // count
     me = lax.axis_index("mp")
     partials = {}
-    for o in sorted(range(count), key=lambda o: (1 - o % 2, -o)):
+    for o in reversed(range(count)):
         partials[o] = project_block(x, w, me ^ o, width)
+        partials[o], x = lax.optimization_barrier((partials[o], x))
     return scatter_sum([partials[o] for o in range(count)])
 
 
@@ -186,20 +182,28 @@
     return out / total, peak + jnp.log2(total)
 
 
-def far_kernel(flag_ref, qa, qb, k0, v0, k1, v1, oa, la, ob, lb):
+def far_kernel(flag_ref, qa, qb, k0, v0, k1, v1, oa, ob):
     rows = qa.shape[0]
     tile = min(rows, 256)
 
     @pl.when(flag_ref[0] == 1)
     def _():
-        for q, o, l in ((qa, oa, la), (qb, ob, lb)):
+        for q, o in ((qa, oa), (qb, ob)):
             for at in range(0, rows, tile):
                 queries = q[at : at + tile, :]
                 out, log = attend(
                     [(scores_of(k0[...], queries), v0[...]), (scores_of(k1[...], queries), v1[...])]
                 )
-                o[:, at : at + tile] = out.astype(jnp.bfloat16)
-                l[0, :, at : at + tile] = log
+                o[:HEAD, at : at + tile] = out.astype(jnp.bfloat16)
+                high = log.astype(jnp.bfloat16).astype(jnp.float32)
+                middle = (log - high).astype(jnp.bfloat16).astype(jnp.float32)
+                row = lax.broadcasted_iota(jnp.int32, (EXTRA, tile), 0)
+                pieces = jnp.where(
+                    row == 0,
+                    high,
+                    jnp.where(row == 1, middle, jnp.where(row == 2, log - high - middle, 0.0)),
+                )
+                o[HEAD:, at : at + tile] = pieces.astype(jnp.bfloat16)
 
 
 def near_kernel(flag_ref, q, k0, v0, k1, v1, o, l):
@@ -230,12 +234,14 @@
         run(False)
 
 
-def merge_kernel(flag_ref, o, l, far_o, far_l, out):
+def merge_kernel(flag_ref, o, l, far_o, out):
     @pl.when(flag_ref[0] >= 2)
     def _():
-        peak = jnp.maximum(l[0], far_l[0])
-        here, there = jnp.exp2(l[0] - peak), jnp.exp2(far_l[0] - peak)
-        mixed = (o[...].astype(jnp.float32) * here + far_o[...].astype(jnp.float32) * there) / (
+        pieces = far_o[HEAD:, :].astype(jnp.float32)
+        far_l = pieces[0:1] + pieces[1:2] + pieces[2:3]
+        peak = jnp.maximum(l[0], far_l)
+        here, there = jnp.exp2(l[0] - peak), jnp.exp2(far_l - peak)
+        mixed = (o[...].astype(jnp.float32) * here + far_o[:HEAD, :].astype(jnp.float32) * there) / (
             here + there
         )
         out[...] = jnp.transpose(mixed).astype(jnp.bfloat16)
@@ -249,9 +255,14 @@
     specs = {
         "rows": (pl.BlockSpec((rows, HEAD), lambda h, f: (0, h)), (rows, heads * HEAD), jnp.bfloat16),
         "flat": (pl.BlockSpec((HEAD, rows), lambda h, f: (h, 0)), (heads * HEAD, rows), jnp.bfloat16),
+        "sent": (
+            pl.BlockSpec((HEAD + EXTRA, rows), lambda h, f: (h, 0)),
+            (heads * (HEAD + EXTRA), rows),
+            jnp.bfloat16,
+        ),
         "log": (pl.BlockSpec((1, 1, rows), lambda h, f: (h, 0, 0)), (heads, 1, rows), jnp.float32),
     }
-    return pl.pallas_call(
+    call = pl.pallas_call(
         kernel,
         grid_spec=pltpu.PrefetchScalarGridSpec(
             num_scalar_prefetch=1,
@@ -265,7 +276,8 @@
             4 * HEAD * work * heads, 2 * rows * HEAD * heads * len(ins), work * heads
         ),
         name=name,
-    )(flag, *[x for _, x in ins])
+    )
+    return list(call(flag, *[x for _, x in ins]))
 
 
 def self_attention(normed, w_query, w_key, w_value, neighbours, w_cross_kv):
@@ -275,7 +287,7 @@
     width = w_query.shape[1] // 2
     heads = width // HEAD
     flag = ctx.reshape(1)
-    merged = []
+    halves, fars = [], []
     for first in (0, width):
         q = project(normed, w_query, first, width)
         qa = lax.ppermute(q, "ctx", [(2, 1)])
@@ -284,26 +296,42 @@
         k0 = lax.ppermute(k, "ctx", [(0, 1), (2, 3)])
         v = project(normed, w_value, first, width, flip=True)
         v0 = lax.ppermute(v, "ctx", [(0, 1), (2, 3)])
-        if first == 0:
-            qa, neighbours = lax.optimization_barrier((qa, neighbours))
-            fetched = lax.all_gather(neighbours, "mp", axis=1, tiled=True)
+        normed, v = lax.optimization_barrier((normed, v))
+        halves.append([q, qa, qb, k, k0, v, v0])
+    incoming, arrival, wanted = neighbours
+    incoming, halves[0][5] = lax.optimization_barrier((incoming, halves[0][5]))
+    arrived = jnp.where((wanted >= 0)[:, None, None], incoming[arrival], jnp.zeros((), incoming.dtype))
+    fetched = lax.all_gather(arrived, "mp", axis=1, tiled=True)
+    arrived, halves[0][1] = lax.optimization_barrier((arrived, halves[0][1]))
+    for at, (q, qa, qb, k, k0, v, v0) in enumerate(halves):
         keys = [("rows", k0), ("flat", v0), ("rows", k), ("flat", v)]
-        oa, la, ob, lb = head_call(
+        far = head_call(
             far_kernel, "far_attention", flag, rows, heads,
-            [("rows", qa), ("rows", qb)] + keys, ["flat", "log"] * 2, 4 * rows * rows,
-        )
-        far_a = [lax.ppermute(x, "ctx", [(1, 2)]) for x in (oa, la)]
-        far_b = [lax.ppermute(x, "ctx", [(1, 3)]) for x in (ob, lb)]
-        o, l = head_call(
+            [("rows", qa), ("rows", qb)] + keys, ["sent"] * 2, 4 * rows * rows,
+        )
+        halves[at] = (q, keys)
+        fars.append(far)
+    last, fetched = lax.optimization_barrier((fars[1][1], fetched))
+    kv, queries = lax.optimization_barrier(
+        (neighbour_kv(fetched, w_cross_kv), [q for q, _ in halves])
+    )
+    fars[1][1] = last
+    sent = [
+        [lax.ppermute(x, "ctx", [(1, 2 + at)]) for at, x in enumerate(far)] for far in fars
+    ]
+    nears = [
+        head_call(
             near_kernel, "near_attention", flag, rows, heads,
             [("rows", q)] + keys, ["flat", "log"], 2 * rows * rows,
         )
-        if first == 0:
-            kv, far_a = lax.optimization_barrier((neighbour_kv(fetched, w_cross_kv), far_a))
-        far_o, far_l = [jnp.where(ctx == 3, b, a) for a, b in zip(far_a, far_b)]
+        for q, (_, keys) in zip(queries, halves)
+    ]
+    merged = []
+    for (o, l), (oa, ob) in zip(nears, sent):
+        far_o = jnp.where(ctx == 3, ob, oa)
         (out,) = head_call(
             merge_kernel, "merge", flag, rows, heads,
-            [("flat", o), ("log", l), ("flat", far_o), ("log", far_l)], ["rows"], rows,
+            [("flat", o), ("log", l), ("sent", far_o)], ["rows"], rows,
         )
         merged.append(out)
     return jnp.concatenate(merged, axis=1), kv
@@ -313,9 +341,17 @@
     group_count = lax.axis_size(("pool", "ctx"))
     my_group = lax.axis_index(("pool", "ctx"))
     per_group = owners.size // group_count
-    capacity = max(2, 2 * per_group // group_count)
-    owner_table = owners.reshape(group_count, per_group)
-    slot_table = slots.reshape(group_count, per_group)
+    capacity = max(2, 2 * per_group // group_count) + 1
+
+    def with_earlier(table, missing):
+        grouped = table.reshape(-1, lax.axis_size("ctx"), per_group)
+        earlier = jnp.pad(
+            grouped[:, :-1, -NB_PER:], ((0, 0), (1, 0), (0, 0)), constant_values=missing
+        )
+        return jnp.concatenate([earlier, grouped], axis=2).reshape(group_count, -1)
+
+    owner_table = with_earlier(owners, -1)
+    slot_table = with_earlier(slots, 0)
     matched = (owner_table == my_group).astype(jnp.int32)
     order_rank = jnp.cumsum(matched, axis=1) - 1
     slot_index = jnp.arange(capacity, dtype=jnp.int32)
@@ -326,14 +362,11 @@
     outgoing = encoded[source_rows].reshape((group_count, capacity) + encoded.shape[1:])
     incoming = lax.all_to_all(outgoing, ("pool", "ctx"), split_axis=0, concat_axis=0, tiled=True)
     wanted = lax.dynamic_index_in_dim(owner_table, my_group, 0, keepdims=False)
-    positions = jnp.arange(per_group, dtype=jnp.int32)
+    positions = jnp.arange(wanted.shape[0], dtype=jnp.int32)
     same_owner = (wanted[:, None] == wanted[None, :]).astype(jnp.int32)
     before_this = (positions[None, :] < positions[:, None]).astype(jnp.int32)
-    arrival = wanted * capacity + jnp.sum(same_owner * before_this, axis=1)
-    arrived = incoming.reshape((group_count * capacity,) + encoded.shape[1:])[arrival]
-    earlier = from_behind(arrived[-NB_PER:], "ctx", 1)
-    extended = jnp.concatenate([earlier, arrived], axis=0)
-    return extended
+    arrival = jnp.maximum(wanted, 0) * capacity + jnp.sum(same_owner * before_this, axis=1)
+    return incoming.reshape((group_count * capacity,) + encoded.shape[1:]), arrival, wanted
 
 
 def neighbour_kernel(x_ref, w_ref, out_ref):

time: 320 us -> 311 us (0.972)
  starting transfers between devices: 47.3 us -> 31.2 us
  waiting for transfers between devices: 111 us -> 117 us
    ppermute x9 -> x4, starting transfers between devices: 23 us -> 7.05 us  [self_attention(): lax.ppermute(x, 'ctx', [(1, 2 + at)])]
    all_to_all x1, waiting for transfers between devices: 1 us -> 11.6 us  [fetch_neighbours(): lax.all_to_all(outgoing, ('pool', 'ctx'), split_axis=0, concat_axis=0, ti...]
    ppermute x2, waiting for transfers between devices: 5.36 us -> 13 us  [self_attention(): qa = lax.ppermute(q, 'ctx', [(2, 1)])]
    ppermute x2, waiting for transfers between devices: 7.6 us -> 0.01 us  [self_attention(): v0 = lax.ppermute(v, 'ctx', [(0, 1), (2, 3)])]
    ppermute x9 -> x4, waiting for transfers between devices: 4.19 us -> 0.01 us  [self_attention(): lax.ppermute(x, 'ctx', [(1, 2 + at)])]
    unnamed x44 -> x48, local copies, waits for them, and re-layouts: 11.8 us -> 12.1 us
  transfers between devices with their start and end apart: 31 -> 26, of which waited for: 12 -> 9; matrix products, arithmetic and copies ran while one was open for 2% -> 1% of each run, Pallas kernels for 30% -> 31%
where the time goes in v4:
time: 311 us; the launch traced here: 309 us
  Pallas kernels  119 us (38%)
  waiting for transfers between devices  117 us (38%)
  starting transfers between devices  31.2 us (10%)
  local copies, waits for them, and re-layouts  19.6 us (6%)
  between operations  14 us (5%)
  other arithmetic  7.92 us (3%)
    ppermute x12, waiting for transfers between devices, swap(): lax.ppermute(block, 'mp', [(i, i ^ bit) for i in range(lax.axis_size('mp'...  92.6 us
    pallas_call x6, Pallas kernels, head_call(): return list(call(flag, *[x for _, x in ins]))  34.5 us
    pallas_call x7, Pallas kernels, project(): pl.pallas_call(functools.partial(project_kernel, flip), grid=(width // ti...  33.7 us
    pallas_call x8, Pallas kernels, project_block(): pl.pallas_call(block_kernel, grid_spec=pltpu.PrefetchScalarGridSpec(num_s...  21.9 us
    pallas_call x1, Pallas kernels, neighbour_kv(): pl.pallas_call(neighbour_kernel, grid=(2, steps), in_specs=[pl.BlockSpec(...  14.8 us
    ppermute x2, waiting for transfers between devices, self_attention(): qa = lax.ppermute(q, 'ctx', [(2, 1)])  13 us
    unnamed x48, local copies, waits for them, and re-layouts  12.1 us
    all_to_all x1, waiting for transfers between devices, fetch_neighbours(): lax.all_to_all(outgoing, ('pool', 'ctx'), split_axis=0, concat_axis=0, ti...  11.6 us
  transfers between devices with their start and end apart: 26, of which 9 were waited for; matrix products, arithmetic and copies ran while one was open for 1% of the time, Pallas kernels for 31%

profile of v4, /device:TPU:12, one launch (start us, length us, event | category | flops | bytes accessed | tf_op | source)
XLA Modules:
  0.0 309.5 jit_solution(5811259675511091103)
XLA Ops:
  6.5 0.8 copy.30
  7.5 0.8 copy.34
  9.3 4.5 %gather_fusion = bf16[40,32,896]{2,1,0:T(8,128)(2,1)} fusion(bf16[64,32,896]{2,1,0:T(8,128)(2,1)} %param.23, s32[1024]{0:T(1024)S(1)} %pad_clamp_fusion.1), kind=kCustom, calls=%fused_computation | custom fusion | bytes 4587680 | tf_op jit(solution)/shard_map/gather | solution.py:362
  13.8 6.3 %all-to-all-start = ((bf16[8,5,32,896]{3,2,1,0:T(8,128)(2,1)}), bf16[8,5,32,896]{3,2,1,0:T(8,128)(2,1)}, u32[]{:S(2)}, u32[]{:S(2)}) async-start(bf16[8,5,32,896]{3,2,1,0:T(8,128)(2,1)} %bitcast.12), calls=%async_computation | async-start | bytes 4587520 | tf_op jit(solution)/shard_map/all_to_all | solution.py:363
  20.1 1.6 collective-permute-start.1
  21.7 22.8 %collective-permute-done.1.refs_2_ = bf16[512,1024]{1,0:T(8,128)(2,1)S(1)} collective-permute-done((bf16[512,1024]{1,0:T(8,128)(2,1)S(1)}, bf16[512,1024]{1,0:T(8,128)(2,1)S(1)}, u32[]{:S(2)}, u32[]{:S(2)}) %collective-permute-start.1) | collective-permute-done | bytes 1048608 | tf_op jit(solution)/shard_map/ppermute | solution.py:36
  44.8 2.6 collective-permute-done.2.refs_3_
  47.3 4.2 %norm.2.x_ref = bf16[512,4096]{1,0:T(8,128)(2,1)S(1)} custom-call(s32[4]{0:T(128)S(1)} %iota_xor_fusion.place_ref, f32[1,4096]{1,0:T(1,128)S(1)} %bitcast.36, bf16[512,1024]{1,0:T(8,128)(2,1)S(1)} %bitcast.35, bf16[512,1024]{1,0:T(8,128)(2,1)S(1)} %collective-permute-done.refs_1_, bf16[512,1024]{1,0:T(8,128)(2,1)S(1)} %collective-permute-done.1.refs_2_, ...), custom_call_target="tpu_custom_call" | custom-call | flops 12582912 | bytes 8388608 | tf_op jit(solution)/shard_map/norm/pallas_call | solution.py:84
  51.5 4.3 %project.7.v1 = bf16[512,512]{1,0:T(8,128)(2,1)S(1)} custom-call(bf16[512,4096]{1,0:T(8,128)(2,1)S(1)} %norm.2.x_ref, bf16[4096,1024]{1,0:T(8,128)(2,1)} %w_ref.19), custom_call_target="tpu_custom_call" | custom-call | flops 2147483648 | bytes 8388608 | tf_op jit(solution)/shard_map/project/pallas_call | solution.py:115
  55.8 2.0 copy-done
  57.8 11.6 %all-to-all-done = bf16[8,5,32,896]{3,2,1,0:T(8,128)(2,1)} async-done(((bf16[8,5,32,896]{3,2,1,0:T(8,128)(2,1)}), bf16[8,5,32,896]{3,2,1,0:T(8,128)(2,1)}, u32[]{:S(2)}, u32[]{:S(2)}) %all-to-all-start) | async-done | bytes 2293792 | tf_op jit(solution)/shard_map/all_to_all | solution.py:363
  69.4 2.4 gather_fusion.1
  71.7 1.1 broadcast_select_fusion
  72.9 1.3 collective-permute-start.8
  74.2 2.2 copy-done.1
  76.4 4.2 %project.11.q = bf16[512,512]{1,0:T(8,128)(2,1)S(1)} custom-call(bf16[512,4096]{1,0:T(8,128)(2,1)S(1)} %copy-done.1, bf16[4096,1024]{1,0:T(8,128)(2,1)} %w_ref.21), custom_call_target="tpu_custom_call" | custom-call | flops 2147483648 | bytes 8388608 | tf_op jit(solution)/shard_map/project/pallas_call | solution.py:115
  80.6 1.3 collective-permute-start.10
  81.9 1.3 collective-permute-start.9
  83.2 4.4 %project.12.k1 = bf16[512,512]{1,0:T(8,128)(2,1)S(1)} custom-call(bf16[512,4096]{1,0:T(8,128)(2,1)S(1)} %copy-done.1, bf16[4096,1024]{1,0:T(8,128)(2,1)} %w_ref.22), custom_call_target="tpu_custom_call" | custom-call | flops 2147483648 | bytes 8388608 | tf_op jit(solution)/shard_map/project/pallas_call | solution.py:115
  87.5 1.3 collective-permute-start.7
  88.8 4.3 %project.10.v1 = bf16[512,512]{1,0:T(8,128)(2,1)S(1)} custom-call(bf16[512,4096]{1,0:T(8,128)(2,1)S(1)} %copy-done.1, bf16[4096,1024]{1,0:T(8,128)(2,1)} %w_ref.19), custom_call_target="tpu_custom_call" | custom-call | flops 2147483648 | bytes 8388608 | tf_op jit(solution)/shard_map/project/pallas_call | solution.py:115
  93.2 1.3 collective-permute-start.6
  94.5 4.2 %project.9.k1 = bf16[512,512]{1,0:T(8,128)(2,1)S(1)} custom-call(bf16[512,4096]{1,0:T(8,128)(2,1)S(1)} %copy-done.1, bf16[4096,1024]{1,0:T(8,128)(2,1)} %w_ref.22), custom_call_target="tpu_custom_call" | custom-call | flops 2147483648 | bytes 8388608 | tf_op jit(solution)/shard_map/project/pallas_call | solution.py:115
  98.7 5.1 %project.8.q = bf16[512,512]{1,0:T(8,128)(2,1)} custom-call(bf16[512,4096]{1,0:T(8,128)(2,1)S(1)} %copy-done.1, bf16[4096,1024]{1,0:T(8,128)(2,1)} %w_ref.21), custom_call_target="tpu_custom_call" | custom-call | flops 2147483648 | bytes 8388608 | tf_op jit(solution)/shard_map/project/pallas_call | solution.py:115
  103.8 4.7 %collective-permute-done.9.qa = bf16[512,512]{1,0:T(8,128)(2,1)S(1)} collective-permute-done((bf16[512,512]{1,0:T(8,128)(2,1)S(1)}, bf16[512,512]{1,0:T(8,128)(2,1)S(1)}, u32[]{:S(2)}, u32[]{:S(2)}) %collective-permute-start.9) | collective-permute-done | bytes 524320 | tf_op jit(solution)/shard_map/ppermute | solution.py:293
  108.4 1.3 collective-permute-start.4
  109.7 1.3 collective-permute-start.3
  111.0 1.3 collective-permute-start.5
  112.4 10.8 %far_attention.3 = (bf16[576,512]{1,0:T(8,128)(2,1)}, bf16[576,512]{1,0:T(8,128)(2,1)}) custom-call(s32[1]{0:T(128)} %bitcast.5.flag_ref, bf16[512,512]{1,0:T(8,128)(2,1)S(1)} %collective-permute-done.9.qa, bf16[512,512]{1,0:T(8,128)(2,1)S(1)} %collective-permute-done.10.qb, bf16[512,512]{1,0:T(8,128)(2,1)S(1)} %collective-permute-done.7.k0, ...), custom_call_target="tpu_custom_call" | custom-call | flops 2147483648 | bytes 3145728 | tf_op jit(solution)/shard_map/far_attention/pallas_call | solution.py:280
  123.2 2.1 collective-permute-start.11
  125.3 0.8 copy-done.15
  126.1 2.1 collective-permute-start.12
  128.2 8.4 %collective-permute-done.3.qa = bf16[512,512]{1,0:T(8,128)(2,1)} collective-permute-done((bf16[512,512]{1,0:T(8,128)(2,1)}, bf16[512,512]{1,0:T(8,128)(2,1)}, u32[]{:S(2)}, u32[]{:S(2)}) %collective-permute-start.3) | collective-permute-done | bytes 524320 | tf_op jit(solution)/shard_map/ppermute | solution.py:293
  136.6 1.0 copy-done.16
  137.7 11.4 %far_attention.2 = (bf16[576,512]{1,0:T(8,128)(2,1)}, bf16[576,512]{1,0:T(8,128)(2,1)S(1)}) custom-call(s32[1]{0:T(128)} %bitcast.5.flag_ref, bf16[512,512]{1,0:T(8,128)(2,1)} %collective-permute-done.3.qa, bf16[512,512]{1,0:T(8,128)(2,1)} %collective-permute-done.4.qb, bf16[512,512]{1,0:T(8,128)(2,1)} %collective-permute-done.5.k0, ...), custom_call_target="tpu_custom_call" | custom-call | flops 2147483648 | bytes 3145728 | tf_op jit(solution)/shard_map/far_attention/pallas_call | solution.py:280
  149.1 0.8 copy-done.12
  149.9 1.3 collective-permute-start.14
  151.3 1.1 broadcast_select_fusion.2.far_o
  152.4 1.5 collective-permute-start.13
  154.0 14.8 %neighbour_kv.1.k_ref.v_ref = bf16[2,2304,1024]{2,1,0:T(8,128)(2,1)S(1)} custom-call(bf16[2304,896]{1,0:T(8,128)(2,1)} %bitcast.40, bf16[2,896,1024]{2,1,0:T(8,128)(2,1)} %w_ref.20), custom_call_target="tpu_custom_call" | custom-call | flops 8455716864 | bytes 13565952 | tf_op jit(solution)/shard_map/neighbour_kv/pallas_call | solution.py:383
  168.8 3.6 %copy-done.2 = bf16[2,2304,1024]{2,1,0:T(8,128)(2,1)} copy-done((bf16[2,2304,1024]{2,1,0:T(8,128)(2,1)}, bf16[2,2304,1024]{2,1,0:T(8,128)(2,1)S(1)}, u32[]{:S(2)}) %copy-start.2) | copy-done | bytes 9437208
  172.5 5.1 %near_attention.2 = (bf16[512,512]{1,0:T(8,128)(2,1)S(1)}, f32[4,1,512]{2,1,0:T(1,128)S(1)}) custom-call(s32[1]{0:T(128)} %bitcast.5.flag_ref, bf16[512,512]{1,0:T(8,128)(2,1)S(1)} %project.11.q, bf16[512,512]{1,0:T(8,128)(2,1)S(1)} %copy-done.19, bf16[512,512]{1,0:T(8,128)(2,1)S(1)} %copy-done.14, bf16[512,512]{1,0:T(8,128)(2,1)S(1)} %copy-done.9, ...), custom_call_target="tpu_custom_call" | custom-call | flops 1073741824 | bytes 2621440 | tf_op jit(solution)/shard_map/near_attention/pallas_call | solution.py:280
  178.3 5.9 %near_attention.3 = (bf16[512,512]{1,0:T(8,128)(2,1)S(1)}, f32[4,1,512]{2,1,0:T(1,128)S(1)}) custom-call(s32[1]{0:T(128)} %bitcast.5.flag_ref, bf16[512,512]{1,0:T(8,128)(2,1)} %project.8.q, bf16[512,512]{1,0:T(8,128)(2,1)} %collective-permute-done.5.k0, bf16[512,512]{1,0:T(8,128)(2,1)S(1)} %copy-done.17, bf16[512,512]{1,0:T(8,128)(2,1)S(1)} %copy-done.7, ...), custom_call_target="tpu_custom_call" | custom-call | flops 1073741824 | bytes 2621440 | tf_op jit(solution)/shard_map/near_attention/pallas_call | solution.py:280
  185.1 2.8 project_block.8
  187.9 2.8 project_block.9
  190.7 2.8 project_block.10
  194.0 1.5 add_convert_fusion.4
  195.5 1.6 collective-permute-start.17
  197.1 2.7 project_block.11
  199.9 20.8 %collective-permute-done.17 = bf16[512,1024]{1,0:T(8,128)(2,1)S(1)} collective-permute-done((bf16[512,1024]{1,0:T(8,128)(2,1)S(1)}, bf16[512,1024]{1,0:T(8,128)(2,1)S(1)}, u32[]{:S(2)}, u32[]{:S(2)}) %collective-permute-start.17) | collective-permute-done | bytes 1048608 | tf_op jit(solution)/shard_map/ppermute | solution.py:36
  220.7 0.9 add_convert_fusion.3.refs_0_
  221.6 1.6 collective-permute-start.19
  223.2 22.8 %collective-permute-done.19.refs_2_ = bf16[512,1024]{1,0:T(8,128)(2,1)S(1)} collective-permute-done((bf16[512,1024]{1,0:T(8,128)(2,1)S(1)}, bf16[512,1024]{1,0:T(8,128)(2,1)S(1)}, u32[]{:S(2)}, u32[]{:S(2)}) %collective-permute-start.19) | collective-permute-done | bytes 1048608 | tf_op jit(solution)/shard_map/ppermute | solution.py:36
  245.9 2.7 collective-permute-done.20.refs_3_
  248.6 2.8 norm.3.x_ref
  251.4 7.2 %project.13.q_ref = bf16[512,1024]{1,0:T(8,128)(2,1)S(1)} custom-call(bf16[512,4096]{1,0:T(8,128)(2,1)S(1)} %norm.3.x_ref, bf16[4096,1024]{1,0:T(8,128)(2,1)} %w_ref.27), custom_call_target="tpu_custom_call" | custom-call | flops 4294967296 | bytes 12582912 | tf_op jit(solution)/shard_map/project/pallas_call | solution.py:115
  258.7 7.5 %cross_attention.1.x_ref = bf16[512,1024]{1,0:T(8,128)(2,1)S(1)} custom-call(bf16[512,1024]{1,0:T(8,128)(2,1)S(1)} %project.13.q_ref, bf16[2,2304,1024]{2,1,0:T(8,128)(2,1)S(1)} %bitcast.32, bf16[2,2304,1024]{2,1,0:T(8,128)(2,1)S(1)} %bitcast.32), custom_call_target="tpu_custom_call" | custom-call | flops 536870912 | bytes 9437184 | tf_op jit(solution)/shard_map/cross_attention/pallas_call | solution.py:439
  266.2 2.7 project_block.12
  269.1 2.7 project_block.13
  271.9 2.7 project_block.14
  275.5 1.6 collective-permute-start.23
  277.0 2.7 project_block.15
  279.8 21.0 %collective-permute-done.23 = bf16[512,1024]{1,0:T(8,128)(2,1)S(1)} collective-permute-done((bf16[512,1024]{1,0:T(8,128)(2,1)S(1)}, bf16[512,1024]{1,0:T(8,128)(2,1)S(1)}, u32[]{:S(2)}, u32[]{:S(2)}) %collective-permute-start.23) | collective-permute-done | bytes 1048608 | tf_op jit(solution)/shard_map/ppermute | solution.py:36
  300.7 1.9 fusion
  (95 shorter events, 4.7 us)
Async XLA Ops:
  13.8 6.4 %copy-start.3 = (bf16[1,512,1024]{2,1,0:T(8,128)(2,1)S(1)}, bf16[1,512,1024]{2,1,0:T(8,128)(2,1)}, u32[]{:S(2)}) copy-start(bf16[1,512,1024]{2,1,0:T(8,128)(2,1)} %param.13) | copy-start | bytes 3145732
  13.8 33.6 %copy-start.10 = (f32[4096]{0:T(1024)S(1)}, f32[4096]{0:T(1024)}, u32[]{:S(2)}) copy-start(f32[4096]{0:T(1024)} %param.14) | copy-start | bytes 49156
  13.8 55.6 %all-to-all-start = ((bf16[8,5,32,896]{3,2,1,0:T(8,128)(2,1)}), bf16[8,5,32,896]{3,2,1,0:T(8,128)(2,1)}, u32[]{:S(2)}, u32[]{:S(2)}) async-start(bf16[8,5,32,896]{3,2,1,0:T(8,128)(2,1)} %bitcast.12), calls=%async_computation | async-start | bytes 4587520 | tf_op jit(solution)/shard_map/all_to_all | solution.py:363
  20.1 132.3 %all-gather.2.cloned.1.call-start = ((), (), s32[]{:S(2)}) async-start(), calls=%async_computation.1 | async-start | bytes 5160960 | tf_op jit(solution)/shard_map/all_gather | solution.py:304
  20.1 24.4 %collective-permute-start.1 = (bf16[512,1024]{1,0:T(8,128)(2,1)S(1)}, bf16[512,1024]{1,0:T(8,128)(2,1)S(1)}, u32[]{:S(2)}, u32[]{:S(2)}) collective-permute-start(bf16[512,1024]{1,0:T(8,128)(2,1)S(1)} %bitcast.33), channel_id=1, source_target_pairs={{0,2},{1,3},{2,0},{3,1},{4,6},{5,7},{6,4},{7,5},{8,10},{9,11},{10,... | collective-permute-start | bytes 3145736 | tf_op jit(solution)/shard_map/ppermute | solution.py:36
  21.7 23.1 %collective-permute-start = (bf16[512,1024]{1,0:T(8,128)(2,1)S(1)}, bf16[512,1024]{1,0:T(8,128)(2,1)S(1)}, u32[]{:S(2)}, u32[]{:S(2)}) collective-permute-start(bf16[512,1024]{1,0:T(8,128)(2,1)S(1)} %bitcast.34), channel_id=1, source_target_pairs={{0,1},{1,0},{2,3},{3,2},{4,5},{5,4},{6,7},{7,6},{8,9},{9,8},{10,11... | collective-permute-start | bytes 3145736 | tf_op jit(solution)/shard_map/ppermute | solution.py:36
  44.6 2.8 collective-permute-start.2
  55.8 2.0 copy-start
  72.9 36.8 %collective-permute-start.8 = (bf16[512,512]{1,0:T(8,128)(2,1)S(1)}, bf16[512,512]{1,0:T(8,128)(2,1)S(1)}, u32[]{:S(2)}, u32[]{:S(2)}) collective-permute-start(bf16[512,512]{1,0:T(8,128)(2,1)S(1)} %project.7.v1), channel_id=1, source_target_pairs={{0,4},{8,12},{1,5},{9,13},{2,6},{10,14},{3,7},{11,15},{16,20},{24,... | collective-permute-start | bytes 1572872 | tf_op jit(solution)/shard_map/ppermute | solution.py:298
  74.2 2.2 copy-start.1
  80.6 30.5 %collective-permute-start.10 = (bf16[512,512]{1,0:T(8,128)(2,1)S(1)}, bf16[512,512]{1,0:T(8,128)(2,1)S(1)}, u32[]{:S(2)}, u32[]{:S(2)}) collective-permute-start(bf16[512,512]{1,0:T(8,128)(2,1)S(1)} %project.11.q), channel_id=1, source_target_pairs={{12,4},{13,5},{14,6},{15,7},{28,20},{29,21},{30,22},{31,23}} | collective-permute-start | bytes 1572872 | tf_op jit(solution)/shard_map/ppermute | solution.py:294
  81.9 26.6 %collective-permute-start.9 = (bf16[512,512]{1,0:T(8,128)(2,1)S(1)}, bf16[512,512]{1,0:T(8,128)(2,1)S(1)}, u32[]{:S(2)}, u32[]{:S(2)}) collective-permute-start(bf16[512,512]{1,0:T(8,128)(2,1)S(1)} %project.11.q), channel_id=1, source_target_pairs={{8,4},{9,5},{10,6},{11,7},{24,20},{25,21},{26,22},{27,23}} | collective-permute-start | bytes 1572872 | tf_op jit(solution)/shard_map/ppermute | solution.py:293
  87.5 24.8 %copy-start.8 = (bf16[512,512]{1,0:T(8,128)(2,1)}, bf16[512,512]{1,0:T(8,128)(2,1)S(1)}, u32[]{:S(2)}) copy-start(bf16[512,512]{1,0:T(8,128)(2,1)S(1)} %project.12.k1) | copy-start | bytes 1572868
  87.5 24.8 %collective-permute-start.7 = (bf16[512,512]{1,0:T(8,128)(2,1)S(1)}, bf16[512,512]{1,0:T(8,128)(2,1)S(1)}, u32[]{:S(2)}, u32[]{:S(2)}) collective-permute-start(bf16[512,512]{1,0:T(8,128)(2,1)S(1)} %project.12.k1), channel_id=1, source_target_pairs={{0,4},{8,12},{1,5},{9,13},{2,6},{10,14},{3,7},{11,15},{16,20},{24,... | collective-permute-start | bytes 1572872 | tf_op jit(solution)/shard_map/ppermute | solution.py:296
  93.1 43.5 %copy-start.4 = (bf16[512,512]{1,0:T(8,128)(2,1)}, bf16[512,512]{1,0:T(8,128)(2,1)S(1)}, u32[]{:S(2)}) copy-start(bf16[512,512]{1,0:T(8,128)(2,1)S(1)} %project.10.v1) | copy-start | bytes 1572868
  93.2 32.2 %collective-permute-start.6 = (bf16[512,512]{1,0:T(8,128)(2,1)S(1)}, bf16[512,512]{1,0:T(8,128)(2,1)S(1)}, u32[]{:S(2)}, u32[]{:S(2)}) collective-permute-start(bf16[512,512]{1,0:T(8,128)(2,1)S(1)} %project.10.v1), channel_id=1, source_target_pairs={{0,4},{8,12},{1,5},{9,13},{2,6},{10,14},{3,7},{11,15},{16,20},{24,... | collective-permute-start | bytes 1572872 | tf_op jit(solution)/shard_map/ppermute | solution.py:298
  98.7 38.0 %copy-start.6 = (bf16[512,512]{1,0:T(8,128)(2,1)}, bf16[512,512]{1,0:T(8,128)(2,1)S(1)}, u32[]{:S(2)}) copy-start(bf16[512,512]{1,0:T(8,128)(2,1)S(1)} %project.9.k1) | copy-start | bytes 1572868
  108.4 19.8 %collective-permute-start.4 = (bf16[512,512]{1,0:T(8,128)(2,1)}, bf16[512,512]{1,0:T(8,128)(2,1)}, u32[]{:S(2)}, u32[]{:S(2)}) collective-permute-start(bf16[512,512]{1,0:T(8,128)(2,1)} %project.8.q), channel_id=1, source_target_pairs={{12,4},{13,5},{14,6},{15,7},{28,20},{29,21},{30,22},{31,23}} | collective-permute-start | bytes 1572872 | tf_op jit(solution)/shard_map/ppermute | solution.py:294
  109.7 13.5 %copy-start.13 = (bf16[512,512]{1,0:T(8,128)(2,1)}, bf16[512,512]{1,0:T(8,128)(2,1)S(1)}, u32[]{:S(2)}) copy-start(bf16[512,512]{1,0:T(8,128)(2,1)S(1)} %collective-permute-done.8.v0) | copy-start | bytes 1572868
  109.7 26.9 %collective-permute-start.3 = (bf16[512,512]{1,0:T(8,128)(2,1)}, bf16[512,512]{1,0:T(8,128)(2,1)}, u32[]{:S(2)}, u32[]{:S(2)}) collective-permute-start(bf16[512,512]{1,0:T(8,128)(2,1)} %project.8.q), channel_id=1, source_target_pairs={{8,4},{9,5},{10,6},{11,7},{24,20},{25,21},{26,22},{27,23}} | collective-permute-start | bytes 1572872 | tf_op jit(solution)/shard_map/ppermute | solution.py:293
  111.0 25.6 %collective-permute-start.5 = (bf16[512,512]{1,0:T(8,128)(2,1)S(1)}, bf16[512,512]{1,0:T(8,128)(2,1)}, u32[]{:S(2)}, u32[]{:S(2)}) collective-permute-start(bf16[512,512]{1,0:T(8,128)(2,1)S(1)} %project.9.k1), channel_id=1, source_target_pairs={{0,4},{8,12},{1,5},{9,13},{2,6},{10,14},{3,7},{11,15},{16,20},{24,... | collective-permute-start | bytes 1572872 | tf_op jit(solution)/shard_map/ppermute | solution.py:296
  112.4 10.8 %copy-start.18 = (bf16[512,512]{1,0:T(8,128)(2,1)}, bf16[512,512]{1,0:T(8,128)(2,1)S(1)}, u32[]{:S(2)}) copy-start(bf16[512,512]{1,0:T(8,128)(2,1)S(1)} %collective-permute-done.7.k0) | copy-start | bytes 1572868
  123.2 28.0 %collective-permute-start.11 = (bf16[576,512]{1,0:T(8,128)(2,1)}, bf16[576,512]{1,0:T(8,128)(2,1)}, u32[]{:S(2)}, u32[]{:S(2)}) collective-permute-start(bf16[576,512]{1,0:T(8,128)(2,1)} %get-tuple-element.49), channel_id=1, source_target_pairs={{4,12},{5,13},{6,14},{7,15},{20,28},{21,29},{22,30},{23,31}} | collective-permute-start | bytes 1769480 | tf_op jit(solution)/shard_map/ppermute | solution.py:320
  125.3 0.8 copy-start.15
  126.1 25.1 %collective-permute-start.12 = (bf16[576,512]{1,0:T(8,128)(2,1)}, bf16[576,512]{1,0:T(8,128)(2,1)}, u32[]{:S(2)}, u32[]{:S(2)}) collective-permute-start(bf16[576,512]{1,0:T(8,128)(2,1)} %get-tuple-element.50), channel_id=1, source_target_pairs={{4,8},{5,9},{6,10},{7,11},{20,24},{21,25},{22,26},{23,27}} | collective-permute-start | bytes 1769480 | tf_op jit(solution)/shard_map/ppermute | solution.py:320
  136.6 1.0 copy-start.16
  149.1 0.8 copy-start.12
  149.9 34.3 %collective-permute-start.14 = (bf16[576,512]{1,0:T(8,128)(2,1)}, bf16[576,512]{1,0:T(8,128)(2,1)S(1)}, u32[]{:S(2)}, u32[]{:S(2)}) collective-permute-start(bf16[576,512]{1,0:T(8,128)(2,1)} %get-tuple-element.55), channel_id=1, source_target_pairs={{4,8},{5,9},{6,10},{7,11},{20,24},{21,25},{22,26},{23,27}} | collective-permute-start | bytes 1769480 | tf_op jit(solution)/shard_map/ppermute | solution.py:320
  152.4 31.8 %collective-permute-start.13 = (bf16[576,512]{1,0:T(8,128)(2,1)}, bf16[576,512]{1,0:T(8,128)(2,1)S(1)}, u32[]{:S(2)}, u32[]{:S(2)}) collective-permute-start(bf16[576,512]{1,0:T(8,128)(2,1)} %copy-done.12), channel_id=1, source_target_pairs={{4,12},{5,13},{6,14},{7,15},{20,28},{21,29},{22,30},{23,31}} | collective-permute-start | bytes 1769480 | tf_op jit(solution)/shard_map/ppermute | solution.py:320
  154.0 18.5 %copy-start.9 = (bf16[512,512]{1,0:T(8,128)(2,1)S(1)}, bf16[512,512]{1,0:T(8,128)(2,1)}, u32[]{:S(2)}) copy-start(bf16[512,512]{1,0:T(8,128)(2,1)} %copy-done.8) | copy-start | bytes 1572868
  154.0 18.5 %copy-start.14 = (bf16[512,512]{1,0:T(8,128)(2,1)S(1)}, bf16[512,512]{1,0:T(8,128)(2,1)}, u32[]{:S(2)}) copy-start(bf16[512,512]{1,0:T(8,128)(2,1)} %copy-done.13) | copy-start | bytes 1572868
  154.0 18.5 %copy-start.19 = (bf16[512,512]{1,0:T(8,128)(2,1)S(1)}, bf16[512,512]{1,0:T(8,128)(2,1)}, u32[]{:S(2)}) copy-start(bf16[512,512]{1,0:T(8,128)(2,1)} %copy-done.18) | copy-start | bytes 1572868
  168.8 3.7 %copy-start.2 = (bf16[2,2304,1024]{2,1,0:T(8,128)(2,1)}, bf16[2,2304,1024]{2,1,0:T(8,128)(2,1)S(1)}, u32[]{:S(2)}) copy-start(bf16[2,2304,1024]{2,1,0:T(8,128)(2,1)S(1)} %neighbour_kv.1.k_ref.v_ref) | copy-start | bytes 28311556
  172.5 5.8 %copy-start.5 = (bf16[512,512]{1,0:T(8,128)(2,1)S(1)}, bf16[512,512]{1,0:T(8,128)(2,1)}, u32[]{:S(2)}) copy-start(bf16[512,512]{1,0:T(8,128)(2,1)} %copy-done.4) | copy-start | bytes 1572868
  172.5 5.8 %copy-start.7 = (bf16[512,512]{1,0:T(8,128)(2,1)S(1)}, bf16[512,512]{1,0:T(8,128)(2,1)}, u32[]{:S(2)}) copy-start(bf16[512,512]{1,0:T(8,128)(2,1)} %copy-done.6) | copy-start | bytes 1572868
  172.5 5.8 %copy-start.17 = (bf16[512,512]{1,0:T(8,128)(2,1)S(1)}, bf16[512,512]{1,0:T(8,128)(2,1)}, u32[]{:S(2)}) copy-start(bf16[512,512]{1,0:T(8,128)(2,1)} %copy-done.15) | copy-start | bytes 1572868
  187.9 6.2 %collective-permute-start.16 = (bf16[512,1024]{1,0:T(8,128)(2,1)S(1)}, bf16[512,1024]{1,0:T(8,128)(2,1)}, u32[]{:S(2)}, u32[]{:S(2)}) collective-permute-start(bf16[512,1024]{1,0:T(8,128)(2,1)S(1)} %project_block.8), channel_id=1, source_target_pairs={{0,1},{1,0},{2,3},{3,2},{4,5},{5,4},{6,7},{7,6},{8,9},{9,8},{10,11... | collective-permute-start | bytes 3145736 | tf_op jit(solution)/shard_map/ppermute | solution.py:36
  193.5 6.4 %collective-permute-start.15 = (bf16[512,1024]{1,0:T(8,128)(2,1)S(1)}, bf16[512,1024]{1,0:T(8,128)(2,1)S(1)}, u32[]{:S(2)}, u32[]{:S(2)}) collective-permute-start(bf16[512,1024]{1,0:T(8,128)(2,1)S(1)} %project_block.10), channel_id=1, source_target_pairs={{0,1},{1,0},{2,3},{3,2},{4,5},{5,4},{6,7},{7,6},{8,9},{9,8},{10,11... | collective-permute-start | bytes 3145736 | tf_op jit(solution)/shard_map/ppermute | solution.py:36
  195.5 25.2 %collective-permute-start.17 = (bf16[512,1024]{1,0:T(8,128)(2,1)S(1)}, bf16[512,1024]{1,0:T(8,128)(2,1)S(1)}, u32[]{:S(2)}, u32[]{:S(2)}) collective-permute-start(bf16[512,1024]{1,0:T(8,128)(2,1)S(1)} %add_convert_fusion.4), channel_id=1, source_target_pairs={{0,2},{1,3},{2,0},{3,1},{4,6},{5,7},{6,4},{7,5},{8,10},{9,11},{10,... | collective-permute-start | bytes 3145736 | tf_op jit(solution)/shard_map/ppermute | solution.py:36
  199.8 48.8 %copy-start.11 = (f32[4096]{0:T(1024)S(1)}, f32[4096]{0:T(1024)}, u32[]{:S(2)}) copy-start(f32[4096]{0:T(1024)} %param.15) | copy-start | bytes 49156
  221.6 24.3 %collective-permute-start.19 = (bf16[512,1024]{1,0:T(8,128)(2,1)S(1)}, bf16[512,1024]{1,0:T(8,128)(2,1)S(1)}, u32[]{:S(2)}, u32[]{:S(2)}) collective-permute-start(bf16[512,1024]{1,0:T(8,128)(2,1)S(1)} %add_convert_fusion.3.refs_0_), channel_id=1, source_target_pairs={{0,2},{1,3},{2,0},{3,1},{4,6},{5,7},{6,4},{7,5},{8,10},{9,11},{10,... | collective-permute-start | bytes 3145736 | tf_op jit(solution)/shard_map/ppermute | solution.py:36
  223.2 22.8 %collective-permute-start.18 = (bf16[512,1024]{1,0:T(8,128)(2,1)S(1)}, bf16[512,1024]{1,0:T(8,128)(2,1)S(1)}, u32[]{:S(2)}, u32[]{:S(2)}) collective-permute-start(bf16[512,1024]{1,0:T(8,128)(2,1)S(1)} %add_convert_fusion.3.refs_0_), channel_id=1, source_target_pairs={{0,1},{1,0},{2,3},{3,2},{4,5},{5,4},{6,7},{7,6},{8,9},{9,8},{10,11... | collective-permute-start | bytes 3145736 | tf_op jit(solution)/shard_map/ppermute | solution.py:36
  245.9 2.7 collective-permute-start.20
  248.6 10.1 %slice-start = ((s8[9437184]{0:T(1024)(128)(4,1)}), s8[4194304]{0:T(1024)(128)(4,1)S(1)}, s32[]{:S(2)}) async-start(s8[9437184]{0:T(1024)(128)(4,1)} %bitcast.31), calls=%async_computation.2 | async-start | bytes 8388608
  248.6 10.1 %slice-start.1 = ((s8[9437184]{0:T(1024)(128)(4,1)}), s8[4194304]{0:T(1024)(128)(4,1)S(1)}, s32[]{:S(2)}) async-start(s8[9437184]{0:T(1024)(128)(4,1)} %bitcast.31), calls=%async_computation.3 | async-start | bytes 8388608
  251.4 7.3 %slice-start.2 = ((s8[9437184]{0:T(1024)(128)(4,1)}), s8[1048576]{0:T(1024)(128)(4,1)S(1)}, s32[]{:S(2)}) async-start(s8[9437184]{0:T(1024)(128)(4,1)} %bitcast.31), calls=%async_computation.4 | async-start | bytes 2097152
  268.9 6.1 %collective-permute-start.22 = (bf16[512,1024]{1,0:T(8,128)(2,1)S(1)}, bf16[512,1024]{1,0:T(8,128)(2,1)S(1)}, u32[]{:S(2)}, u32[]{:S(2)}) collective-permute-start(bf16[512,1024]{1,0:T(8,128)(2,1)S(1)} %project_block.12), channel_id=1, source_target_pairs={{0,1},{1,0},{2,3},{3,2},{4,5},{5,4},{6,7},{7,6},{8,9},{9,8},{10,11... | collective-permute-start | bytes 3145736 | tf_op jit(solution)/shard_map/ppermute | solution.py:36
  274.6 5.1 %collective-permute-start.21 = (bf16[512,1024]{1,0:T(8,128)(2,1)S(1)}, bf16[512,1024]{1,0:T(8,128)(2,1)S(1)}, u32[]{:S(2)}, u32[]{:S(2)}) collective-permute-start(bf16[512,1024]{1,0:T(8,128)(2,1)S(1)} %project_block.14), channel_id=1, source_target_pairs={{0,1},{1,0},{2,3},{3,2},{4,5},{5,4},{6,7},{7,6},{8,9},{9,8},{10,11... | collective-permute-start | bytes 3145736 | tf_op jit(solution)/shard_map/ppermute | solution.py:36
  275.5 25.3 %collective-permute-start.23 = (bf16[512,1024]{1,0:T(8,128)(2,1)S(1)}, bf16[512,1024]{1,0:T(8,128)(2,1)S(1)}, u32[]{:S(2)}, u32[]{:S(2)}) collective-permute-start(bf16[512,1024]{1,0:T(8,128)(2,1)S(1)} %add_convert_fusion.1), channel_id=1, source_target_pairs={{0,2},{1,3},{2,0},{3,1},{4,6},{5,7},{6,4},{7,5},{8,10},{9,11},{10,... | collective-permute-start | bytes 3145736 | tf_op jit(solution)/shard_map/ppermute | solution.py:36
Sparse Core Ops, SparseCore 0:
  73.0 35.1 all-gather.1
